TPU v7x, 256 devices: a whole 4x4x8 slice. The times are simulated.
256 devices in a mesh: row: 16 (over z, x_hi), rep: 16 (over x_lo, y, core).
Axes of the slice: x: 4 (x_hi: 2, x_lo: 2; x = x_hi * 2 + x_lo), y: 4, z: 8, core: 2. Of those that a mesh axis runs over, the one named last changes fastest.
Arguments:
- grad_out: bfloat16 [65536, 512], P(('row', 'rep')), may hold values from -6 to 6
- relu_mask: int32 [65536, 512], P(('row', 'rep')), may hold values 0 or 1
- aggregated: bfloat16 [65536, 512], P(('row', 'rep')), may hold values from -0.059814453 to 0.059814453
- weight: bfloat16 [512, 512], replicated, may hold values from -0.25 to 0.25
- tile_values: bfloat16 [16, 16, 4, 24, 128, 128], P('row', 'rep'), may hold values from 0 to 0.099609375
- tile_src: int32 [16, 16, 4, 24], P('row', 'rep'), may hold values from 0 to 1, as said below
- tile_dst: int32 [16, 16, 4, 24], P('row', 'rep'), may hold values from 0 to 31
- tile_count: int32 [16, 16, 4], P('row', 'rep'), may hold values from 3 to 24, as said below
Outputs:
- input_grad: bfloat16 [65536, 512], P(('row', 'rep'))
- weight_grad: float32 [512, 512], replicated
Inputs may be any that keep to these rules, and one draw needn't show every extreme that they name: `tile_src`: in each list no pair of source and destination block repeats, slots past the count included. `tile_count`: some list is full in every draw.
All inputs are finite; a program needn't handle non-finite values. No bound on the sum of `relu_mask` on one device may be relied on, other than what follows from the above.
Results may differ from a plain program's by a relative error of at most 0.018.
Values may be sent and summed in bfloat16 or wider, within the bound.
No kernel may reach another device: no remote copies, remote signals or barrier semaphores. Data moves between devices by JAX's collectives and lax.ppermute only.
A program may use at most 128 MiB of HBM per device.

v0:
```python
import jax
import jax.numpy as jnp
from jax import lax
from jax.sharding import PartitionSpec as P


def from_root(block, axis, owner):
    block = jnp.where(lax.axis_index(axis) == owner, block, jnp.zeros_like(block))
    return lax.psum(block, axis)


def padded_tiles(partial_value, source, tile_vals, sources, targets, live_count):
    slots = sources.shape[0]
    gathered = jnp.take(source, sources, axis=0)
    products = jnp.einsum("tab,taf->tbf", tile_vals, gathered, preferred_element_type=jnp.float32)
    alive_mask = (jnp.arange(slots, dtype=jnp.int32) < live_count).astype(jnp.float32)
    return partial_value.at[targets].add(products * alive_mask[:, None, None])


def local(grad_out, relu_mask, aggregated, weight, tile_values, tile_src, tile_dst, tile_count):
    masked = jnp.where(relu_mask != 0, grad_out, jnp.zeros_like(grad_out))
    node_grad = lax.dot_general(
        masked, weight, (((1,), (1,)), ((), ())), preferred_element_type=jnp.float32
    ).astype(jnp.bfloat16)
    local_wgrad = lax.dot_general(
        aggregated, masked, (((0,), (0,)), ((), ())), preferred_element_type=jnp.float32
    )
    weight_grad = lax.psum(local_wgrad, ("row", "rep"))
    sections = tile_src.shape[2]
    block_rows = tile_values.shape[-1]
    features = grad_out.shape[1]
    own_blocks = grad_out.shape[0] // block_rows
    groups = lax.axis_size("row")
    slab_blocks = groups * own_blocks
    blocks = node_grad.reshape(own_blocks, block_rows, features)
    partial_value = jnp.zeros((slab_blocks, block_rows, features), jnp.float32)
    for section_index in range(sections):
        source = from_root(blocks, "rep", section_index)
        tile_vals = tile_values[0, 0, section_index]
        sources = tile_src[0, 0, section_index]
        targets = tile_dst[0, 0, section_index]
        live_count = tile_count[0, 0, section_index]
        partial_value = padded_tiles(partial_value, source, tile_vals, sources, targets, live_count)
    sent = partial_value.astype(jnp.bfloat16)
    own_sum = lax.psum_scatter(sent, "row", scatter_dimension=0, tiled=True).astype(jnp.float32)
    input_grad = own_sum.reshape(own_blocks * block_rows, features).astype(jnp.bfloat16)
    return (input_grad, weight_grad)


def solution(mesh):
    in_specs = (
        P(("row", "rep"), None),
        P(("row", "rep"), None),
        P(("row", "rep"), None),
        P(),
        P("row", "rep", None, None, None, None),
        P("row", "rep", None, None),
        P("row", "rep", None, None),
        P("row", "rep", None),
    )
    out_specs = (P(("row", "rep"), None), P())
    return jax.shard_map(local, mesh=mesh, in_specs=in_specs, out_specs=out_specs, check_vma=False)
```

profile of v0, /device:TPU:2, one launch (start us, length us, event | category | flops | bytes accessed | tf_op | source)
XLA Modules:
  0.0 624.6 jit_solution(15098972801080002196)
XLA Ops:
  7.2 0.0 copy-start
  7.2 0.0 copy-start.9
  7.2 0.0 copy-start.8
  7.2 0.0 copy-start.10
  7.2 0.0 all-reduce.6.cloned.1.call-start
  7.3 0.9 copy-done
  8.2 2.5 broadcast_select_fusion
  10.7 0.0 all-reduce.6.cloned.1.call-update
  10.7 0.0 all-reduce.4.cloned.1.call-start
  10.8 0.0 copy-done.9
  10.8 0.0 copy-done.8
  10.8 0.0 copy-done.10
  10.8 1.3 convolution_bitcast_fusion
  12.1 0.0 all-reduce.4.cloned.1.call-update
  12.1 0.0 reduce-scatter.2.cloned.1.call-start
  12.2 0.0 copy-done.12
  12.2 0.0 copy-done.11
  12.2 0.7 fusion.40
  12.9 0.6 compare_convert_fusion.3
  13.5 0.0 copy-done.13
  13.5 0.6 compare_convert_fusion.2
  14.2 0.7 compare_convert_fusion.1
  14.9 0.6 compare_convert_fusion
  15.5 123.4 %all-reduce.6.cloned.1.call-done = (bf16[2,128,512]{2,1,0:T(8,128)(2,1)}, bf16[2,128,512]{2,1,0:T(8,128)(2,1)}, bf16[2,128,512]{2,1,0:T(8,128)(2,1)}, bf16[2,128,512]{2,1,0:T(8,128)(2,1)}) async-done(((bf16[2,128,512]{2,1,0:T(8,128)(2,1)}, bf16[2,128,512]{2,1,0:T(8,128)(2,1)}, bf16[2,128,512]{2,1,0:T(8,128)(2,1)}, bf16[2,128,512]{2,1,0:T(8,128)(2,1)}), (bf16[2,128,512]{2,1,0:T(8,128)(2,1)}, ...) | async-done | bytes 1048592 | tf_op jit(solution)/shard_map/psum | solution.py:9
  138.9 3.6 gather_fusion
  142.5 2.5 gather_fusion.1
  145.0 2.5 gather_fusion.2
  147.4 6.3 %multiply_bitcast_fusion.3 = f32[24,128,512]{1,2,0:T(8,128)} fusion(f32[24]{0:T(128)S(1)} %compare_convert_fusion.3, bf16[24,128,512]{2,1,0:T(8,128)(2,1)} %gather_fusion, pred[24]{0:T(512)(128)(4,1)S(1)} %get-tuple-element.25, bf16[1,1,4,24,128,128]{5,4,3,2,1,0:T(8,128)(2,1)} %param.14), kind=kOutput, calls=%fused_computation.11 | convolution fusion | flops 405798912 | bytes 10223736 | tf_op jit(solution)/shard_map/tab,taf->tbf/dot_general | solution.py:15
  153.7 0.0 copy-done.6
  153.7 4.0 multiply_bitcast_fusion.2
  157.7 4.0 multiply_bitcast_fusion.1
  161.7 6.6 %copy.16 = f32[24,128,512]{2,1,0:T(8,128)} copy(f32[24,128,512]{1,2,0:T(8,128)} %multiply_bitcast_fusion.3) | data formatting | bytes 12582912 | tf_op jit(solution)/shard_map/mul | solution.py:17
  168.3 6.6 %copy.18 = f32[24,128,512]{2,1,0:T(8,128)} copy(f32[24,128,512]{1,2,0:T(8,128)} %multiply_bitcast_fusion.2) | data formatting | bytes 12582912 | tf_op jit(solution)/shard_map/mul | solution.py:17
  174.9 6.7 %copy.20 = f32[24,128,512]{2,1,0:T(8,128)} copy(f32[24,128,512]{1,2,0:T(8,128)} %multiply_bitcast_fusion.1) | data formatting | bytes 12582912 | tf_op jit(solution)/shard_map/mul | solution.py:17
  181.6 0.0 copy-done.2
  181.6 2.6 gather_fusion.3
  184.2 6.1 multiply_bitcast_fusion
  190.3 6.5 %copy.22 = f32[24,128,512]{2,1,0:T(8,128)} copy(f32[24,128,512]{1,2,0:T(8,128)} %multiply_bitcast_fusion) | data formatting | bytes 12582912 | tf_op jit(solution)/shard_map/mul | solution.py:17
  196.9 4.3 broadcast_in_dim.13
  201.2 14.1 %scatter_fusion = f32[32,128,512]{2,1,0:T(8,128)} fusion(f32[32,128,512]{2,1,0:T(8,128)} %broadcast_in_dim.13, s32[24]{0:T(128)S(1)} %get-tuple-element.31, f32[24,128,512]{2,1,0:T(8,128)} %copy.16), kind=kCustom, calls=%fused_computation.4 | custom fusion | flops 1572864 | bytes 18874464 | tf_op jit(solution)/shard_map/scatter-add | solution.py:17
  215.2 14.1 %scatter_fusion.1 = f32[32,128,512]{2,1,0:T(8,128)} fusion(f32[32,128,512]{2,1,0:T(8,128)} %scatter_fusion, s32[24]{0:T(128)S(1)} %get-tuple-element.30, f32[24,128,512]{2,1,0:T(8,128)} %copy.18), kind=kCustom, calls=%fused_computation.5 | custom fusion | flops 1572864 | bytes 18874464 | tf_op jit(solution)/shard_map/scatter-add | solution.py:17
  229.3 14.2 %scatter_fusion.2 = f32[32,128,512]{2,1,0:T(8,128)} fusion(f32[32,128,512]{2,1,0:T(8,128)} %scatter_fusion.1, s32[24]{0:T(128)S(1)} %get-tuple-element.32, f32[24,128,512]{2,1,0:T(8,128)} %copy.20), kind=kCustom, calls=%fused_computation.6 | custom fusion | flops 1572864 | bytes 18874464 | tf_op jit(solution)/shard_map/scatter-add | solution.py:17
  243.5 14.0 %scatter_fusion.3 = f32[32,128,512]{2,1,0:T(8,128)} fusion(f32[32,128,512]{2,1,0:T(8,128)} %scatter_fusion.2, s32[24]{0:T(128)S(1)} %get-tuple-element.29, f32[24,128,512]{2,1,0:T(8,128)} %copy.22), kind=kCustom, calls=%fused_computation.7 | custom fusion | flops 1572864 | bytes 18874464 | tf_op jit(solution)/shard_map/scatter-add | solution.py:17
  257.5 6.0 convert_element_type.44
  263.5 0.0 reduce-scatter.2.cloned.1.call-update
  263.5 139.9 %all-reduce.4.cloned.1.call-done = f32[512,512]{0,1:T(8,128)} async-done(((f32[512,512]{0,1:T(8,128)}), f32[512,512]{0,1:T(8,128)}) %all-reduce.4.cloned.1.call-update) | async-done | bytes 1048592 | tf_op jit(solution)/shard_map/psum | solution.py:28
  403.4 2.5 copy.23
  405.9 212.1 %reduce-scatter.2.cloned.1.call-done = bf16[2,128,512]{2,1,0:T(8,128)(2,1)} async-done(((bf16[32,128,512]{2,1,0:T(8,128)(2,1)}), bf16[2,128,512]{2,1,0:T(8,128)(2,1)}) %reduce-scatter.2.cloned.1.call-update) | async-done | bytes 262160 | tf_op jit(solution)/shard_map/reduce_scatter | solution.py:45
  (19 shorter events, 0.1 us)
Async XLA Ops:
  7.2 1.1 copy-start
  7.2 3.6 copy-start.9
  7.2 3.6 copy-start.8
  7.2 3.6 copy-start.10
  7.2 131.7 %all-reduce.6.cloned.1.call-start = ((), (), s32[]{:S(2)}) async-start(), calls=%async_computation.3 | async-start | bytes 2097152 | tf_op jit(solution)/shard_map/psum | solution.py:9
  8.2 4.0 copy-start.12
  8.2 4.0 copy-start.11
  8.2 5.3 copy-start.13
  10.7 392.6 %all-reduce.4.cloned.1.call-start = ((), (), s32[]{:S(2)}) async-start(), calls=%async_computation.2 | async-start | bytes 2097152 | tf_op jit(solution)/shard_map/psum | solution.py:28
  12.1 605.9 %reduce-scatter.2.cloned.1.call-start = ((), (), s32[]{:S(2)}) async-start(), calls=%async_computation.1 | async-start | bytes 4456448 | tf_op jit(solution)/shard_map/reduce_scatter | solution.py:45
  138.9 3.6 copy-start.4
  142.5 2.5 copy-start.3
  147.4 6.3 %copy-start.6 = (bf16[24,128,512]{2,1,0:T(8,128)(2,1)S(1)}, bf16[24,128,512]{2,1,0:T(8,128)(2,1)}, u32[]{:S(2)}) copy-start(bf16[24,128,512]{2,1,0:T(8,128)(2,1)} %gather_fusion.1) | copy-start | bytes 9437188
  147.4 6.3 %copy-start.7 = (bf16[1,1,4,24,128,128]{5,4,3,2,1,0:T(8,128)(2,1)S(1)}, bf16[1,1,4,24,128,128]{5,4,3,2,1,0:T(8,128)(2,1)}, u32[]{:S(2)}) copy-start(bf16[1,1,4,24,128,128]{5,4,3,2,1,0:T(8,128)(2,1)} %param.14) | copy-start | bytes 9437188
  153.7 4.0 copy-start.5
  174.9 6.7 %copy-start.2 = (bf16[2,128,512]{2,1,0:T(8,128)(2,1)S(1)}, bf16[2,128,512]{2,1,0:T(8,128)(2,1)}, u32[]{:S(2)}) copy-start(bf16[2,128,512]{2,1,0:T(8,128)(2,1)} %get-tuple-element.10) | copy-start | bytes 786436
  263.5 354.6 %copy-start.1 = (bf16[512,512]{1,0:T(8,128)(2,1)S(1)}, bf16[512,512]{1,0:T(8,128)(2,1)}, u32[]{:S(2)}) copy-start(bf16[512,512]{1,0:T(8,128)(2,1)} %param.13) | copy-start | bytes 1572868
Sparse Core Ops, SparseCore 0:
  11.5 127.3 all-reduce.5
  145.8 257.5 all-reduce.3
  408.0 210.0 reduce-scatter.1
where the time goes:
time: 626 us; the launch traced here: 625 us
  waiting for transfers between devices  475 us (76%)
  other arithmetic  64.8 us (10%)
  local copies, waits for them, and re-layouts  46.1 us (7%)
  matrix products  24.2 us (4%)
  between operations  13.9 us (2%)
    reduce_scatter x1, waiting for transfers between devices, local(): lax.psum_scatter(sent, 'row', scatter_dimension=0, tiled=True)  212 us
    psum x1, waiting for transfers between devices, local(): weight_grad = lax.psum(local_wgrad, ('row', 'rep'))  140 us
    psum x1, waiting for transfers between devices, from_root(): return lax.psum(block, axis)  123 us
    scatter-add x4, other arithmetic, padded_tiles(): return partial_value.at[targets].add(products * alive_mask[:, None, None])  56.3 us
    mul x4, local copies, waits for them, and re-layouts, padded_tiles(): return partial_value.at[targets].add(products * alive_mask[:, None, None])  26.4 us
    dot_general x4, matrix products, padded_tiles(): jnp.einsum('tab,taf->tbf', tile_vals, gathered, preferred_element_type=jn...  20.4 us
  transfers between devices with their start and end apart: 3, of which 3 were waited for; matrix products, arithmetic and copies ran while one was open for 21% of the time, Pallas kernels for 0%

commit v1 on v0

v1 whole, which is shorter than its diff:
```python
import jax
import jax.numpy as jnp
from jax import lax
from jax.experimental import pallas as pl
from jax.experimental.pallas import tpu as pltpu
from jax.sharding import PartitionSpec as P

AXES = ("row", "rep")
X, Y, Z, C = 4, 4, 8, 2


def index_of(x, y, z, c):
    return (z * 2 + x // 2) * 16 + (x % 2) * 8 + y * 2 + c


def pairs(move):
    out = []
    for z in range(Z):
        for x in range(X):
            for y in range(Y):
                for c in range(C):
                    to = move(x, y, z, c)
                    if to is not None:
                        out.append((index_of(x, y, z, c), index_of(to[0] % X, to[1] % Y, to[2] % Z, to[3] % C)))
    return out


def send(value, move):
    return lax.ppermute(value, AXES, pairs(move))


def add(*terms):
    total = terms[0].astype(jnp.float32)
    for term in terms[1:]:
        total = total + term.astype(jnp.float32)
    return total


def narrow(value):
    return value.astype(jnp.bfloat16)


def flood(block, x_lo, y):
    def across(x, y, z, c):
        return (x + 1, y, z, c) if x % 2 == 0 and y < 2 else None

    def outward(x, y, z, c):
        return (x, 3 - y, z, c) if x % 2 == 0 and y < 2 else None

    def swap(x, y, z, c):
        return (x, 1 - y, z, c) if x % 2 == 0 and y < 2 else None

    by_x = send(block, across)
    by_y = send(block, outward)
    swapped = send(block, swap)
    first = jnp.where(x_lo == 0, jnp.where(y < 2, block, by_y), by_x)

    def swap_rest(x, y, z, c):
        if x % 2 == 0 and y >= 2:
            return (x, 5 - y, z, c)
        if x % 2 == 1 and y < 2:
            return (x, 1 - y, z, c)
        return None

    def across_rest(x, y, z, c):
        return (x + 1, y, z, c) if x % 2 == 0 and y >= 2 else None

    def far(x, y, z, c):
        return (x, y + 2, z, c) if x % 2 == 1 and y < 2 else None

    second = send(first, swap_rest)
    by_x2 = send(first, across_rest)
    by_y2 = send(first, far)
    last = jnp.logical_and(x_lo == 1, y >= 2)
    first = jnp.where(last, by_x2, first)
    second = jnp.where(last, by_y2, jnp.where(jnp.logical_and(x_lo == 0, y < 2), swapped, second))
    flip = jnp.logical_or(y == 1, y == 2)
    even = jnp.where(flip, second, first)
    odd = jnp.where(flip, first, second)
    return even, odd


def tiles_kernel(src_ref, dst_ref, count_ref, place_ref, tiles_ref, a_ref, b_ref, c_ref, d_ref, *rest):
    outs, (acc, held) = rest[:16], rest[16:]
    z, xh, core = place_ref[0], place_ref[1], place_ref[2]
    acc[...] = jnp.zeros_like(acc)
    for i, ref in enumerate((a_ref, b_ref, c_ref, d_ref)):
        held[2 * i] = ref[:128, :]
        held[2 * i + 1] = ref[128:, :]
    for section in range(4):
        slot = jnp.where(core == section % 2, section // 2, 2 + section // 2)

        def step(t, carry):
            d = dst_ref[section, t]
            s = src_ref[section, t]
            rel = lax.rem(d // 4 - z + 8, 8)
            half = lax.rem(d // 2 + xh, 2)
            at = rel * 4 + half * 2 + lax.rem(d, 2)
            product = lax.dot_general(
                tiles_ref[section * 24 + t],
                held[slot * 2 + s],
                (((0,), (0,)), ((), ())),
                preferred_element_type=jnp.float32,
            )
            acc[at] += product
            return carry

        lax.fori_loop(0, count_ref[section], step, 0)
    for i in range(16):
        for j in range(2):
            outs[i][pl.ds(j * 128, 128), :] = acc[2 * i + j].astype(jnp.bfloat16)


def tile_partials(src, dst, count, place, tiles, sources):
    smem = pl.BlockSpec(memory_space=pltpu.SMEM)
    vmem = pl.BlockSpec(memory_space=pltpu.VMEM)
    return pl.pallas_call(
        tiles_kernel,
        out_shape=[jax.ShapeDtypeStruct((256, 512), jnp.bfloat16)] * 16,
        in_specs=[smem] * 4 + [vmem] * 5,
        out_specs=[vmem] * 16,
        scratch_shapes=[pltpu.VMEM((32, 128, 512), jnp.float32), pltpu.VMEM((8, 128, 512), jnp.bfloat16)],
        compiler_params=pltpu.CompilerParams(vmem_limit_bytes=48 * 1024 * 1024),
        name="tile_partials",
    )(src, dst, count, place, tiles, *sources)


def up(x, y, z, c):
    return (x, y, z + 1, c)


def down(x, y, z, c):
    return (x, y, z - 1, c)


def chain(first, terms, move):
    moving = first
    for term in terms:
        moving = narrow(add(send(moving, move), term))
    return send(moving, move)


def spread(value, size, me, hop):
    rows = value.shape[0] // size
    own = lax.dynamic_slice_in_dim(value, me * rows, rows, 0)
    parts = [own]
    for k in range(1, size):
        to = lax.rem(me + k, size)
        piece = narrow(lax.dynamic_slice_in_dim(value, to * rows, rows, 0))
        parts.append(send(piece, hop(k)))
    return add(*parts)


def collect(value, size, me, hop):
    rows = value.shape[0]
    out = jnp.zeros((size, rows, value.shape[1]), value.dtype)
    out = lax.dynamic_update_slice_in_dim(out, value[None], me, 0)
    for k in range(1, size):
        got = send(value, hop(k))
        out = lax.dynamic_update_slice_in_dim(out, got[None], lax.rem(me - k + size, size), 0)
    return out.reshape(size * rows, value.shape[1])


HOPS = {
    "c": lambda k: lambda x, y, z, c: (x, y, z, c + k),
    "y": lambda k: lambda x, y, z, c: (x, y + k, z, c),
    "x": lambda k: lambda x, y, z, c: (x + k, y, z, c),
    "z": lambda k: lambda x, y, z, c: (x, y, z + k, c),
}


def local(grad_out, relu_mask, aggregated, weight, tile_values, tile_src, tile_dst, tile_count):
    row, rep = lax.axis_index("row"), lax.axis_index("rep")
    z, x_hi = row // 2, row % 2
    x_lo, y, core = rep // 8, (rep // 2) % 4, rep % 2
    masked = jnp.where(relu_mask != 0, grad_out, jnp.zeros_like(grad_out))
    node_grad = lax.dot_general(
        masked, weight, (((1,), (1,)), ((), ())), preferred_element_type=jnp.float32
    ).astype(jnp.bfloat16)
    even, odd = flood(node_grad, x_lo, y)
    other = HOPS["c"](1)
    sources = (even, odd, send(even, other), send(odd, other))
    place = jnp.stack([z, x_hi, core]).astype(jnp.int32)
    tiles = tile_values.reshape(tile_values.shape[2] * tile_values.shape[3], 128, 128)
    parts = tile_partials(tile_src[0, 0], tile_dst[0, 0], tile_count[0, 0], place, tiles, sources)
    mine = [parts[2 * k] for k in range(8)]
    theirs = [parts[2 * k + 1] for k in range(8)]
    theirs_up = chain(theirs[4], [theirs[3], theirs[2], theirs[1]], up)
    theirs_down = chain(theirs[5], [theirs[6], theirs[7]], down)
    crossing = narrow(add(theirs[0], theirs_up, theirs_down))
    crossed = send(crossing, HOPS["x"](2))
    mine_down = chain(mine[4], [mine[5], mine[6], mine[7]], down)
    mine_up = chain(mine[3], [mine[2], mine[1]], up)
    input_grad = narrow(add(mine[0], mine_up, mine_down, crossed))

    local_wgrad = lax.dot_general(
        aggregated, masked, (((0,), (0,)), ((), ())), preferred_element_type=jnp.float32
    )
    x = x_hi * 2 + x_lo
    total = spread(local_wgrad, C, core, HOPS["c"])
    total = spread(total, Y, y, HOPS["y"])
    total = spread(total, X, x, HOPS["x"])
    total = spread(total, Z, z, HOPS["z"])
    total = narrow(total)
    total = collect(total, Z, z, HOPS["z"])
    total = collect(total, X, x, HOPS["x"])
    total = collect(total, Y, y, HOPS["y"])
    total = collect(total, C, core, HOPS["c"])
    return (input_grad, total.astype(jnp.float32))


def solution(mesh):
    in_specs = (
        P(("row", "rep"), None),
        P(("row", "rep"), None),
        P(("row", "rep"), None),
        P(),
        P("row", "rep", None, None, None, None),
        P("row", "rep", None, None),
        P("row", "rep", None, None),
        P("row", "rep", None),
    )
    out_specs = (P(("row", "rep"), None), P())
    return jax.shard_map(local, mesh=mesh, in_specs=in_specs, out_specs=out_specs, check_vma=False)
```

time: 626 us -> 193 us (0.31)
  waiting for transfers between devices: 475 us -> 74.8 us
  starting transfers between devices: 0.12 us -> 82.7 us
  other arithmetic: 64.8 us -> 3.2 us
  local copies, waits for them, and re-layouts: 46.1 us -> 0.44 us
  Pallas kernels: 0 us -> 24.6 us
  matrix products: 24.2 us -> 1.97 us
  between operations: 13.9 us -> 1.53 us
    psum x2 -> x0, waiting for transfers between devices: 263 us -> none  [the longest x1 140 us: local(): weight_grad = lax.psum(local_wgrad, ('row', 'rep'))]
    reduce_scatter x1 -> x0, waiting for transfers between devices: 212 us -> none  [local(): lax.psum_scatter(sent, 'row', scatter_dimension=0, tiled=True)]
    ppermute x0 -> x51, starting transfers between devices: none -> 82.7 us  [send(): return lax.ppermute(value, AXES, pairs(move))]
    ppermute x0 -> x51, waiting for transfers between devices: none -> 74.8 us  [send(): return lax.ppermute(value, AXES, pairs(move))]
    scatter-add x4 -> x0, other arithmetic: 56.3 us -> none  [padded_tiles(): return partial_value.at[targets].add(products * alive_mask[:, None, None])]
    mul x4 -> x0, local copies, waits for them, and re-layouts: 26.4 us -> none  [padded_tiles(): return partial_value.at[targets].add(products * alive_mask[:, None, None])]
    pallas_call x0 -> x1, Pallas kernels: none -> 24.6 us  [tile_partials(): pl.pallas_call(tiles_kernel, out_shape=[jax.ShapeDtypeStruct((256, 512),...]
    dot_general x4 -> x0, matrix products: 20.4 us -> none  [padded_tiles(): jnp.einsum('tab,taf->tbf', tile_vals, gathered, preferred_element_type=jn...]
  transfers between devices with their start and end apart: 3 -> 51, of which waited for: 3 -> 26; matrix products, arithmetic and copies ran while one was open for 21% -> 2% of each run, Pallas kernels for 0% -> 13%
where the time goes in v1:
time: 193 us; the launch traced here: 189 us
  starting transfers between devices  82.7 us (43%)
  waiting for transfers between devices  74.8 us (39%)
  Pallas kernels  24.6 us (13%)
  other arithmetic  3.2 us (2%)
  matrix products  1.97 us (1%)
    ppermute x51, starting transfers between devices, send(): return lax.ppermute(value, AXES, pairs(move))  82.7 us
    ppermute x51, waiting for transfers between devices, send(): return lax.ppermute(value, AXES, pairs(move))  74.8 us
    pallas_call x1, Pallas kernels, tile_partials(): pl.pallas_call(tiles_kernel, out_shape=[jax.ShapeDtypeStruct((256, 512),...  24.6 us
  transfers between devices with their start and end apart: 51, of which 26 were waited for; matrix products, arithmetic and copies ran while one was open for 2% of the time, Pallas kernels for 13%

profile of v1, /device:TPU:2, one launch (start us, length us, event | category | flops | bytes accessed | tf_op | source)
XLA Modules:
  0.0 189.3 jit_solution(7257702341438476315)
XLA Ops:
  0.7 1.6 fusion.14
  4.1 3.1 %collective-permute-start.26 = (bf16[64,512]{1,0:T(8,128)(2,1)S(1)}, bf16[64,512]{1,0:T(8,128)(2,1)S(1)}, u32[]{:S(2)}, u32[]{:S(2)}) collective-permute-start(bf16[64,512]{1,0:T(8,128)(2,1)S(1)} %get-tuple-element.39), channel_id=1, source_target_pairs={{0,6},{1,7},{2,0},{3,1},{4,2},{5,3},{6,4},{7,5},{8,14},{9,15},{10,... | collective-permute-start | bytes 196616 | tf_op jit(solution)/shard_map/ppermute | solution.py:29
  8.8 1.5 collective-permute-done.26
  10.4 3.0 %collective-permute-done.25 = bf16[64,512]{1,0:T(8,128)(2,1)S(1)} collective-permute-done((bf16[64,512]{1,0:T(8,128)(2,1)S(1)}, bf16[64,512]{1,0:T(8,128)(2,1)S(1)}, u32[]{:S(2)}, u32[]{:S(2)}) %collective-permute-start.25) | collective-permute-done | bytes 65568 | tf_op jit(solution)/shard_map/ppermute | solution.py:29
  14.6 2.4 %collective-permute-start.28 = (bf16[16,512]{1,0:T(8,128)(2,1)S(1)}, bf16[16,512]{1,0:T(8,128)(2,1)S(1)}, u32[]{:S(2)}, u32[]{:S(2)}) collective-permute-start(bf16[16,512]{1,0:T(8,128)(2,1)S(1)} %get-tuple-element.43), channel_id=1, source_target_pairs={{0,16},{1,17},{2,18},{3,19},{4,20},{5,21},{6,22},{7,23},{8,24},{9,... | collective-permute-start | bytes 49160 | tf_op jit(solution)/shard_map/ppermute | solution.py:29
  17.1 1.8 collective-permute-start.27
  21.6 5.9 %collective-permute-start.36 = (bf16[2,512]{1,0:T(2,128)(2,1)S(1)}, bf16[2,512]{1,0:T(2,128)(2,1)S(1)}, u32[]{:S(2)}, u32[]{:S(2)}) collective-permute-start(bf16[2,512]{1,0:T(2,128)(2,1)S(1)} %get-tuple-element.45), channel_id=1, source_target_pairs={{0,224},{1,225},{2,226},{3,227},{4,228},{5,229},{6,230},{7,231},{8... | collective-permute-start | bytes 6152 | tf_op jit(solution)/shard_map/ppermute | solution.py:29
  27.5 1.5 collective-permute-start.35
  29.4 5.0 %collective-permute-start.33 = (bf16[2,512]{1,0:T(2,128)(2,1)S(1)}, bf16[2,512]{1,0:T(2,128)(2,1)S(1)}, u32[]{:S(2)}, u32[]{:S(2)}) collective-permute-start(bf16[2,512]{1,0:T(2,128)(2,1)S(1)} %get-tuple-element.48), channel_id=1, source_target_pairs={{0,128},{1,129},{2,130},{3,131},{4,132},{5,133},{6,134},{7,135},{8... | collective-permute-start | bytes 6152 | tf_op jit(solution)/shard_map/ppermute | solution.py:29
  37.0 1.8 collective-permute-start.30
  38.9 2.2 %collective-permute-done.32 = bf16[2,512]{1,0:T(2,128)(2,1)S(1)} collective-permute-done((bf16[2,512]{1,0:T(2,128)(2,1)S(1)}, bf16[2,512]{1,0:T(2,128)(2,1)S(1)}, u32[]{:S(2)}, u32[]{:S(2)}) %collective-permute-start.32) | collective-permute-done | bytes 2080 | tf_op jit(solution)/shard_map/ppermute | solution.py:29
  43.9 3.0 %collective-permute-start.2 = (bf16[256,512]{1,0:T(8,128)(2,1)S(1)}, bf16[256,512]{1,0:T(8,128)(2,1)S(1)}, u32[]{:S(2)}, u32[]{:S(2)}) collective-permute-start(bf16[256,512]{1,0:T(8,128)(2,1)S(1)} %select_select_fusion.1), channel_id=1, source_target_pairs={{8,12},{9,13},{10,14},{11,15},{24,28},{25,29},{26,30},{27,31},{40,... | collective-permute-start | bytes 786440 | tf_op jit(solution)/shard_map/ppermute | solution.py:29
  46.9 2.3 %collective-permute-start.4 = (bf16[256,512]{1,0:T(8,128)(2,1)S(1)}, bf16[256,512]{1,0:T(8,128)(2,1)S(1)}, u32[]{:S(2)}, u32[]{:S(2)}) collective-permute-start(bf16[256,512]{1,0:T(8,128)(2,1)S(1)} %select_select_fusion.1), channel_id=1, source_target_pairs={{4,6},{5,7},{6,4},{7,5},{8,10},{9,11},{10,8},{11,9},{20,22},{21,23... | collective-permute-start | bytes 786440 | tf_op jit(solution)/shard_map/ppermute | solution.py:29
  49.2 2.4 %collective-permute-start.38 = (bf16[2,512]{1,0:T(2,128)(2,1)S(1)}, bf16[2,512]{1,0:T(2,128)(2,1)S(1)}, u32[]{:S(2)}, u32[]{:S(2)}) collective-permute-start(bf16[2,512]{1,0:T(2,128)(2,1)S(1)} %get-tuple-element.35), channel_id=1, source_target_pairs={{0,64},{1,65},{2,66},{3,67},{4,68},{5,69},{6,70},{7,71},{8,72},{9,... | collective-permute-start | bytes 6152 | tf_op jit(solution)/shard_map/ppermute | solution.py:29
  51.6 3.3 %collective-permute-done.38 = bf16[2,512]{1,0:T(2,128)(2,1)S(1)} collective-permute-done((bf16[2,512]{1,0:T(2,128)(2,1)S(1)}, bf16[2,512]{1,0:T(2,128)(2,1)S(1)}, u32[]{:S(2)}, u32[]{:S(2)}) %collective-permute-start.38) | collective-permute-done | bytes 2080 | tf_op jit(solution)/shard_map/ppermute | solution.py:29
  55.0 3.3 %collective-permute-start.39 = (bf16[2,512]{1,0:T(2,128)(2,1)S(1)}, bf16[2,512]{1,0:T(2,128)(2,1)S(1)}, u32[]{:S(2)}, u32[]{:S(2)}) collective-permute-start(bf16[2,512]{1,0:T(2,128)(2,1)S(1)} %get-tuple-element.35), channel_id=1, source_target_pairs={{0,96},{1,97},{2,98},{3,99},{4,100},{5,101},{6,102},{7,103},{8,104... | collective-permute-start | bytes 6152 | tf_op jit(solution)/shard_map/ppermute | solution.py:29
  58.3 3.2 %collective-permute-done.39 = bf16[2,512]{1,0:T(2,128)(2,1)S(1)} collective-permute-done((bf16[2,512]{1,0:T(2,128)(2,1)S(1)}, bf16[2,512]{1,0:T(2,128)(2,1)S(1)}, u32[]{:S(2)}, u32[]{:S(2)}) %collective-permute-start.39) | collective-permute-done | bytes 2080 | tf_op jit(solution)/shard_map/ppermute | solution.py:29
  61.6 4.0 %collective-permute-start.40 = (bf16[2,512]{1,0:T(2,128)(2,1)S(1)}, bf16[2,512]{1,0:T(2,128)(2,1)S(1)}, u32[]{:S(2)}, u32[]{:S(2)}) collective-permute-start(bf16[2,512]{1,0:T(2,128)(2,1)S(1)} %get-tuple-element.35), channel_id=1, source_target_pairs={{0,128},{1,129},{2,130},{3,131},{4,132},{5,133},{6,134},{7,135},{8... | collective-permute-start | bytes 6152 | tf_op jit(solution)/shard_map/ppermute | solution.py:29
  65.6 3.5 %collective-permute-done.40 = bf16[2,512]{1,0:T(2,128)(2,1)S(1)} collective-permute-done((bf16[2,512]{1,0:T(2,128)(2,1)S(1)}, bf16[2,512]{1,0:T(2,128)(2,1)S(1)}, u32[]{:S(2)}, u32[]{:S(2)}) %collective-permute-start.40) | collective-permute-done | bytes 2080 | tf_op jit(solution)/shard_map/ppermute | solution.py:29
  69.1 3.1 %collective-permute-start.41 = (bf16[2,512]{1,0:T(2,128)(2,1)S(1)}, bf16[2,512]{1,0:T(2,128)(2,1)S(1)}, u32[]{:S(2)}, u32[]{:S(2)}) collective-permute-start(bf16[2,512]{1,0:T(2,128)(2,1)S(1)} %get-tuple-element.35), channel_id=1, source_target_pairs={{0,160},{1,161},{2,162},{3,163},{4,164},{5,165},{6,166},{7,167},{8... | collective-permute-start | bytes 6152 | tf_op jit(solution)/shard_map/ppermute | solution.py:29
  72.2 2.3 %collective-permute-done.41 = bf16[2,512]{1,0:T(2,128)(2,1)S(1)} collective-permute-done((bf16[2,512]{1,0:T(2,128)(2,1)S(1)}, bf16[2,512]{1,0:T(2,128)(2,1)S(1)}, u32[]{:S(2)}, u32[]{:S(2)}) %collective-permute-start.41) | collective-permute-done | bytes 2080 | tf_op jit(solution)/shard_map/ppermute | solution.py:29
  74.4 2.2 %collective-permute-start.42 = (bf16[2,512]{1,0:T(2,128)(2,1)S(1)}, bf16[2,512]{1,0:T(2,128)(2,1)S(1)}, u32[]{:S(2)}, u32[]{:S(2)}) collective-permute-start(bf16[2,512]{1,0:T(2,128)(2,1)S(1)} %get-tuple-element.35), channel_id=1, source_target_pairs={{0,192},{1,193},{2,194},{3,195},{4,196},{5,197},{6,198},{7,199},{8... | collective-permute-start | bytes 6152 | tf_op jit(solution)/shard_map/ppermute | solution.py:29
  76.7 2.3 %collective-permute-done.42 = bf16[2,512]{1,0:T(2,128)(2,1)S(1)} collective-permute-done((bf16[2,512]{1,0:T(2,128)(2,1)S(1)}, bf16[2,512]{1,0:T(2,128)(2,1)S(1)}, u32[]{:S(2)}, u32[]{:S(2)}) %collective-permute-start.42) | collective-permute-done | bytes 2080 | tf_op jit(solution)/shard_map/ppermute | solution.py:29
  78.9 2.3 %collective-permute-start.43 = (bf16[2,512]{1,0:T(2,128)(2,1)S(1)}, bf16[2,512]{1,0:T(2,128)(2,1)S(1)}, u32[]{:S(2)}, u32[]{:S(2)}) collective-permute-start(bf16[2,512]{1,0:T(2,128)(2,1)S(1)} %get-tuple-element.35), channel_id=1, source_target_pairs={{0,224},{1,225},{2,226},{3,227},{4,228},{5,229},{6,230},{7,231},{8... | collective-permute-start | bytes 6152 | tf_op jit(solution)/shard_map/ppermute | solution.py:29
  81.2 1.7 collective-permute-done.43
  83.0 1.8 collective-permute-start.44
  84.8 2.0 %collective-permute-done.44 = bf16[16,512]{1,0:T(8,128)(2,1)S(1)} collective-permute-done((bf16[16,512]{1,0:T(8,128)(2,1)S(1)}, bf16[16,512]{1,0:T(8,128)(2,1)S(1)}, u32[]{:S(2)}, u32[]{:S(2)}) %collective-permute-start.44) | collective-permute-done | bytes 16416 | tf_op jit(solution)/shard_map/ppermute | solution.py:29
  86.8 1.6 collective-permute-start.45
  88.4 3.7 %collective-permute-done.45 = bf16[16,512]{1,0:T(8,128)(2,1)S(1)} collective-permute-done((bf16[16,512]{1,0:T(8,128)(2,1)S(1)}, bf16[16,512]{1,0:T(8,128)(2,1)S(1)}, u32[]{:S(2)}, u32[]{:S(2)}) %collective-permute-start.45) | collective-permute-done | bytes 16416 | tf_op jit(solution)/shard_map/ppermute | solution.py:29
  92.0 3.0 %collective-permute-start.46 = (bf16[16,512]{1,0:T(8,128)(2,1)S(1)}, bf16[16,512]{1,0:T(8,128)(2,1)S(1)}, u32[]{:S(2)}, u32[]{:S(2)}) collective-permute-start(bf16[16,512]{1,0:T(8,128)(2,1)S(1)} %reshape.20), channel_id=1, source_target_pairs={{0,24},{1,25},{2,26},{3,27},{4,28},{5,29},{6,30},{7,31},{8,0},{9,1... | collective-permute-start | bytes 49160 | tf_op jit(solution)/shard_map/ppermute | solution.py:29
  96.5 2.0 %collective-permute-start.47 = (bf16[64,512]{1,0:T(8,128)(2,1)S(1)}, bf16[64,512]{1,0:T(8,128)(2,1)S(1)}, u32[]{:S(2)}, u32[]{:S(2)}) collective-permute-start(bf16[64,512]{1,0:T(8,128)(2,1)S(1)} %bitcast.60), channel_id=1, source_target_pairs={{0,2},{1,3},{2,4},{3,5},{4,6},{5,7},{6,0},{7,1},{8,10},{9,11},{10,... | collective-permute-start | bytes 196616 | tf_op jit(solution)/shard_map/ppermute | solution.py:29
  98.5 3.4 %collective-permute-done.47 = bf16[64,512]{1,0:T(8,128)(2,1)S(1)} collective-permute-done((bf16[64,512]{1,0:T(8,128)(2,1)S(1)}, bf16[64,512]{1,0:T(8,128)(2,1)S(1)}, u32[]{:S(2)}, u32[]{:S(2)}) %collective-permute-start.47) | collective-permute-done | bytes 65568 | tf_op jit(solution)/shard_map/ppermute | solution.py:29
  102.8 4.9 %collective-permute-done.48 = bf16[64,512]{1,0:T(8,128)(2,1)S(1)} collective-permute-done((bf16[64,512]{1,0:T(8,128)(2,1)S(1)}, bf16[64,512]{1,0:T(8,128)(2,1)S(1)}, u32[]{:S(2)}, u32[]{:S(2)}) %collective-permute-start.48) | collective-permute-done | bytes 65568 | tf_op jit(solution)/shard_map/ppermute | solution.py:29
  108.6 3.4 %collective-permute-done.49 = bf16[64,512]{1,0:T(8,128)(2,1)S(1)} collective-permute-done((bf16[64,512]{1,0:T(8,128)(2,1)S(1)}, bf16[64,512]{1,0:T(8,128)(2,1)S(1)}, u32[]{:S(2)}, u32[]{:S(2)}) %collective-permute-start.49) | collective-permute-done | bytes 65568 | tf_op jit(solution)/shard_map/ppermute | solution.py:29
  112.2 24.6 %tile_partials.1 = (bf16[256,512]{1,0:T(8,128)(2,1)S(1)}, bf16[256,512]{1,0:T(8,128)(2,1)S(1)}, bf16[256,512]{1,0:T(8,128)(2,1)S(1)}, bf16[256,512]{1,0:T(8,128)...) custom-call(s32[4,24]{1,0:T(4,128)S(1)} %bitcast.54, ...), custom_call_target="tpu_custom_call" | custom-call | tf_op jit(solution)/shard_map/tile_partials/pallas_call | solution.py:117
  137.0 2.1 %collective-permute-start.15 = (bf16[256,512]{1,0:T(8,128)(2,1)S(1)}, bf16[256,512]{1,0:T(8,128)(2,1)S(1)}, u32[]{:S(2)}, u32[]{:S(2)}) collective-permute-start(bf16[256,512]{1,0:T(8,128)(2,1)S(1)} %get-tuple-element.27), channel_id=1, source_target_pairs={{0,32},{1,33},{2,34},{3,35},{4,36},{5,37},{6,38},{7,39},{8,40},{9,... | collective-permute-start | bytes 786440 | tf_op jit(solution)/shard_map/ppermute | solution.py:29
  141.2 4.8 %collective-permute-done.19 = bf16[256,512]{1,0:T(8,128)(2,1)S(1)} collective-permute-done((bf16[256,512]{1,0:T(8,128)(2,1)S(1)}, bf16[256,512]{1,0:T(8,128)(2,1)S(1)}, u32[]{:S(2)}, u32[]{:S(2)}) %collective-permute-start.19) | collective-permute-done | bytes 262176 | tf_op jit(solution)/shard_map/ppermute | solution.py:29
  148.5 2.8 %collective-permute-done.11 = bf16[256,512]{1,0:T(8,128)(2,1)S(1)} collective-permute-done((bf16[256,512]{1,0:T(8,128)(2,1)S(1)}, bf16[256,512]{1,0:T(8,128)(2,1)S(1)}, u32[]{:S(2)}, u32[]{:S(2)}) %collective-permute-start.11) | collective-permute-done | bytes 262176 | tf_op jit(solution)/shard_map/ppermute | solution.py:29
  151.4 1.7 collective-permute-start.12
  153.6 5.1 %collective-permute-done.16 = bf16[256,512]{1,0:T(8,128)(2,1)S(1)} collective-permute-done((bf16[256,512]{1,0:T(8,128)(2,1)S(1)}, bf16[256,512]{1,0:T(8,128)(2,1)S(1)}, u32[]{:S(2)}, u32[]{:S(2)}) %collective-permute-start.16) | collective-permute-done | bytes 262176 | tf_op jit(solution)/shard_map/ppermute | solution.py:29
  159.2 3.0 %collective-permute-start.21 = (bf16[256,512]{1,0:T(8,128)(2,1)S(1)}, bf16[256,512]{1,0:T(8,128)(2,1)S(1)}, u32[]{:S(2)}, u32[]{:S(2)}) collective-permute-start(bf16[256,512]{1,0:T(8,128)(2,1)S(1)} %add_convert_fusion.2), channel_id=1, source_target_pairs={{0,224},{1,225},{2,226},{3,227},{4,228},{5,229},{6,230},{7,231},{8... | collective-permute-start | bytes 786440 | tf_op jit(solution)/shard_map/ppermute | solution.py:29
  162.3 1.9 %collective-permute-start.13 = (bf16[256,512]{1,0:T(8,128)(2,1)S(1)}, bf16[256,512]{1,0:T(8,128)(2,1)S(1)}, u32[]{:S(2)}, u32[]{:S(2)}) collective-permute-start(bf16[256,512]{1,0:T(8,128)(2,1)S(1)} %add_convert_fusion.8), channel_id=1, source_target_pairs={{0,224},{1,225},{2,226},{3,227},{4,228},{5,229},{6,230},{7,231},{8... | collective-permute-start | bytes 786440 | tf_op jit(solution)/shard_map/ppermute | solution.py:29
  164.3 5.3 %collective-permute-done.17 = bf16[256,512]{1,0:T(8,128)(2,1)S(1)} collective-permute-done((bf16[256,512]{1,0:T(8,128)(2,1)S(1)}, bf16[256,512]{1,0:T(8,128)(2,1)S(1)}, u32[]{:S(2)}, u32[]{:S(2)}) %collective-permute-start.17) | collective-permute-done | bytes 262176 | tf_op jit(solution)/shard_map/ppermute | solution.py:29
  170.0 2.8 %collective-permute-done.13 = bf16[256,512]{1,0:T(8,128)(2,1)S(1)} collective-permute-done((bf16[256,512]{1,0:T(8,128)(2,1)S(1)}, bf16[256,512]{1,0:T(8,128)(2,1)S(1)}, u32[]{:S(2)}, u32[]{:S(2)}) %collective-permute-start.13) | collective-permute-done | bytes 262176 | tf_op jit(solution)/shard_map/ppermute | solution.py:29
  172.8 3.8 %collective-permute-start.14 = (bf16[256,512]{1,0:T(8,128)(2,1)S(1)}, bf16[256,512]{1,0:T(8,128)(2,1)S(1)}, u32[]{:S(2)}, u32[]{:S(2)}) collective-permute-start(bf16[256,512]{1,0:T(8,128)(2,1)S(1)} %add_convert_fusion.7), channel_id=1, source_target_pairs={{0,224},{1,225},{2,226},{3,227},{4,228},{5,229},{6,230},{7,231},{8... | collective-permute-start | bytes 786440 | tf_op jit(solution)/shard_map/ppermute | solution.py:29
  176.6 3.6 %collective-permute-done.18 = bf16[256,512]{1,0:T(8,128)(2,1)S(1)} collective-permute-done((bf16[256,512]{1,0:T(8,128)(2,1)S(1)}, bf16[256,512]{1,0:T(8,128)(2,1)S(1)}, u32[]{:S(2)}, u32[]{:S(2)}) %collective-permute-start.18) | collective-permute-done | bytes 262176 | tf_op jit(solution)/shard_map/ppermute | solution.py:29
  182.0 2.6 %collective-permute-done.10 = bf16[256,512]{1,0:T(8,128)(2,1)S(1)} collective-permute-done((bf16[256,512]{1,0:T(8,128)(2,1)S(1)}, bf16[256,512]{1,0:T(8,128)(2,1)S(1)}, u32[]{:S(2)}, u32[]{:S(2)}) %collective-permute-start.10) | collective-permute-done | bytes 262176 | tf_op jit(solution)/shard_map/ppermute | solution.py:29
  184.6 3.7 %collective-permute-done.22 = bf16[256,512]{1,0:T(8,128)(2,1)S(1)} collective-permute-done((bf16[256,512]{1,0:T(8,128)(2,1)S(1)}, bf16[256,512]{1,0:T(8,128)(2,1)S(1)}, u32[]{:S(2)}, u32[]{:S(2)}) %collective-permute-start.22) | collective-permute-done | bytes 262176 | tf_op jit(solution)/shard_map/ppermute | solution.py:29
  (117 shorter events, 25.2 us)
Async XLA Ops:
  4.1 6.2 %collective-permute-start.26 = (bf16[64,512]{1,0:T(8,128)(2,1)S(1)}, bf16[64,512]{1,0:T(8,128)(2,1)S(1)}, u32[]{:S(2)}, u32[]{:S(2)}) collective-permute-start(bf16[64,512]{1,0:T(8,128)(2,1)S(1)} %get-tuple-element.39), channel_id=1, source_target_pairs={{0,6},{1,7},{2,0},{3,1},{4,2},{5,3},{6,4},{7,5},{8,14},{9,15},{10,... | collective-permute-start | bytes 196616 | tf_op jit(solution)/shard_map/ppermute | solution.py:29
  7.2 6.1 %collective-permute-start.25 = (bf16[64,512]{1,0:T(8,128)(2,1)S(1)}, bf16[64,512]{1,0:T(8,128)(2,1)S(1)}, u32[]{:S(2)}, u32[]{:S(2)}) collective-permute-start(bf16[64,512]{1,0:T(8,128)(2,1)S(1)} %get-tuple-element.40), channel_id=1, source_target_pairs={{0,4},{1,5},{2,6},{3,7},{4,0},{5,1},{6,2},{7,3},{8,12},{9,13},{10,... | collective-permute-start | bytes 196616 | tf_op jit(solution)/shard_map/ppermute | solution.py:29
  7.8 6.1 %collective-permute-start.24 = (bf16[64,512]{1,0:T(8,128)(2,1)S(1)}, bf16[64,512]{1,0:T(8,128)(2,1)S(1)}, u32[]{:S(2)}, u32[]{:S(2)}) collective-permute-start(bf16[64,512]{1,0:T(8,128)(2,1)S(1)} %get-tuple-element.38), channel_id=1, source_target_pairs={{0,2},{1,3},{2,4},{3,5},{4,6},{5,7},{6,0},{7,1},{8,10},{9,11},{10,... | collective-permute-start | bytes 196616 | tf_op jit(solution)/shard_map/ppermute | solution.py:29
  14.0 7.5 %collective-permute-start.29 = (bf16[16,512]{1,0:T(8,128)(2,1)S(1)}, bf16[16,512]{1,0:T(8,128)(2,1)S(1)}, u32[]{:S(2)}, u32[]{:S(2)}) collective-permute-start(bf16[16,512]{1,0:T(8,128)(2,1)S(1)} %get-tuple-element.42), channel_id=1, source_target_pairs={{0,24},{1,25},{2,26},{3,27},{4,28},{5,29},{6,30},{7,31},{8,0},{9,1... | collective-permute-start | bytes 49160 | tf_op jit(solution)/shard_map/ppermute | solution.py:29
  14.6 6.9 %collective-permute-start.28 = (bf16[16,512]{1,0:T(8,128)(2,1)S(1)}, bf16[16,512]{1,0:T(8,128)(2,1)S(1)}, u32[]{:S(2)}, u32[]{:S(2)}) collective-permute-start(bf16[16,512]{1,0:T(8,128)(2,1)S(1)} %get-tuple-element.43), channel_id=1, source_target_pairs={{0,16},{1,17},{2,18},{3,19},{4,20},{5,21},{6,22},{7,23},{8,24},{9,... | collective-permute-start | bytes 49160 | tf_op jit(solution)/shard_map/ppermute | solution.py:29
  17.1 4.5 %collective-permute-start.27 = (bf16[16,512]{1,0:T(8,128)(2,1)S(1)}, bf16[16,512]{1,0:T(8,128)(2,1)S(1)}, u32[]{:S(2)}, u32[]{:S(2)}) collective-permute-start(bf16[16,512]{1,0:T(8,128)(2,1)S(1)} %get-tuple-element.41), channel_id=1, source_target_pairs={{0,8},{1,9},{2,10},{3,11},{4,12},{5,13},{6,14},{7,15},{8,16},{9,17... | collective-permute-start | bytes 49160 | tf_op jit(solution)/shard_map/ppermute | solution.py:29
  19.3 23.9 %collective-permute-start.1 = (bf16[256,512]{1,0:T(8,128)(2,1)S(1)}, bf16[256,512]{1,0:T(8,128)(2,1)S(1)}, u32[]{:S(2)}, u32[]{:S(2)}) collective-permute-start(bf16[256,512]{1,0:T(8,128)(2,1)S(1)} %convolution_convert_fusion), channel_id=1, source_target_pairs={{0,8},{1,9},{2,10},{3,11},{16,24},{17,25},{18,26},{19,27},{32,40},... | collective-permute-start | bytes 786440 | tf_op jit(solution)/shard_map/ppermute | solution.py:29
  20.7 22.5 %collective-permute-start = (bf16[256,512]{1,0:T(8,128)(2,1)S(1)}, bf16[256,512]{1,0:T(8,128)(2,1)S(1)}, u32[]{:S(2)}, u32[]{:S(2)}) collective-permute-start(bf16[256,512]{1,0:T(8,128)(2,1)S(1)} %convolution_convert_fusion), channel_id=1, source_target_pairs={{0,6},{1,7},{2,4},{3,5},{16,22},{17,23},{18,20},{19,21},{32,38},{3... | collective-permute-start | bytes 786440 | tf_op jit(solution)/shard_map/ppermute | solution.py:29
  21.6 7.8 %collective-permute-start.36 = (bf16[2,512]{1,0:T(2,128)(2,1)S(1)}, bf16[2,512]{1,0:T(2,128)(2,1)S(1)}, u32[]{:S(2)}, u32[]{:S(2)}) collective-permute-start(bf16[2,512]{1,0:T(2,128)(2,1)S(1)} %get-tuple-element.45), channel_id=1, source_target_pairs={{0,224},{1,225},{2,226},{3,227},{4,228},{5,229},{6,230},{7,231},{8... | collective-permute-start | bytes 6152 | tf_op jit(solution)/shard_map/ppermute | solution.py:29
  27.5 7.0 %collective-permute-start.35 = (bf16[2,512]{1,0:T(2,128)(2,1)S(1)}, bf16[2,512]{1,0:T(2,128)(2,1)S(1)}, u32[]{:S(2)}, u32[]{:S(2)}) collective-permute-start(bf16[2,512]{1,0:T(2,128)(2,1)S(1)} %get-tuple-element.46), channel_id=1, source_target_pairs={{0,192},{1,193},{2,194},{3,195},{4,196},{5,197},{6,198},{7,199},{8... | collective-permute-start | bytes 6152 | tf_op jit(solution)/shard_map/ppermute | solution.py:29
  29.0 6.6 %collective-permute-start.34 = (bf16[2,512]{1,0:T(2,128)(2,1)S(1)}, bf16[2,512]{1,0:T(2,128)(2,1)S(1)}, u32[]{:S(2)}, u32[]{:S(2)}) collective-permute-start(bf16[2,512]{1,0:T(2,128)(2,1)S(1)} %get-tuple-element.47), channel_id=1, source_target_pairs={{0,160},{1,161},{2,162},{3,163},{4,164},{5,165},{6,166},{7,167},{8... | collective-permute-start | bytes 6152 | tf_op jit(solution)/shard_map/ppermute | solution.py:29
  29.4 7.6 %collective-permute-start.33 = (bf16[2,512]{1,0:T(2,128)(2,1)S(1)}, bf16[2,512]{1,0:T(2,128)(2,1)S(1)}, u32[]{:S(2)}, u32[]{:S(2)}) collective-permute-start(bf16[2,512]{1,0:T(2,128)(2,1)S(1)} %get-tuple-element.48), channel_id=1, source_target_pairs={{0,128},{1,129},{2,130},{3,131},{4,132},{5,133},{6,134},{7,135},{8... | collective-permute-start | bytes 6152 | tf_op jit(solution)/shard_map/ppermute | solution.py:29
  34.5 6.6 %collective-permute-start.32 = (bf16[2,512]{1,0:T(2,128)(2,1)S(1)}, bf16[2,512]{1,0:T(2,128)(2,1)S(1)}, u32[]{:S(2)}, u32[]{:S(2)}) collective-permute-start(bf16[2,512]{1,0:T(2,128)(2,1)S(1)} %get-tuple-element.49), channel_id=1, source_target_pairs={{0,96},{1,97},{2,98},{3,99},{4,100},{5,101},{6,102},{7,103},{8,104... | collective-permute-start | bytes 6152 | tf_op jit(solution)/shard_map/ppermute | solution.py:29
  35.6 6.2 %collective-permute-start.31 = (bf16[2,512]{1,0:T(2,128)(2,1)S(1)}, bf16[2,512]{1,0:T(2,128)(2,1)S(1)}, u32[]{:S(2)}, u32[]{:S(2)}) collective-permute-start(bf16[2,512]{1,0:T(2,128)(2,1)S(1)} %get-tuple-element.50), channel_id=1, source_target_pairs={{0,64},{1,65},{2,66},{3,67},{4,68},{5,69},{6,70},{7,71},{8,72},{9,... | collective-permute-start | bytes 6152 | tf_op jit(solution)/shard_map/ppermute | solution.py:29
  37.0 4.8 %collective-permute-start.30 = (bf16[2,512]{1,0:T(2,128)(2,1)S(1)}, bf16[2,512]{1,0:T(2,128)(2,1)S(1)}, u32[]{:S(2)}, u32[]{:S(2)}) collective-permute-start(bf16[2,512]{1,0:T(2,128)(2,1)S(1)} %get-tuple-element.44), channel_id=1, source_target_pairs={{0,32},{1,33},{2,34},{3,35},{4,36},{5,37},{6,38},{7,39},{8,40},{9,... | collective-permute-start | bytes 6152 | tf_op jit(solution)/shard_map/ppermute | solution.py:29
  41.1 66.7 %collective-permute-start.3 = (bf16[256,512]{1,0:T(8,128)(2,1)S(1)}, bf16[256,512]{1,0:T(8,128)(2,1)S(1)}, u32[]{:S(2)}, u32[]{:S(2)}) collective-permute-start(bf16[256,512]{1,0:T(8,128)(2,1)S(1)} %convolution_convert_fusion), channel_id=1, source_target_pairs={{0,2},{1,3},{2,0},{3,1},{16,18},{17,19},{18,16},{19,17},{32,34},{3... | collective-permute-start | bytes 786440 | tf_op jit(solution)/shard_map/ppermute | solution.py:29
  41.9 7.3 %collective-permute-start.37 = (bf16[2,512]{1,0:T(2,128)(2,1)S(1)}, bf16[2,512]{1,0:T(2,128)(2,1)S(1)}, u32[]{:S(2)}, u32[]{:S(2)}) collective-permute-start(bf16[2,512]{1,0:T(2,128)(2,1)S(1)} %get-tuple-element.35), channel_id=1, source_target_pairs={{0,32},{1,33},{2,34},{3,35},{4,36},{5,37},{6,38},{7,39},{8,40},{9,... | collective-permute-start | bytes 6152 | tf_op jit(solution)/shard_map/ppermute | solution.py:29
  43.2 64.5 %collective-permute-start.5 = (bf16[256,512]{1,0:T(8,128)(2,1)S(1)}, bf16[256,512]{1,0:T(8,128)(2,1)S(1)}, u32[]{:S(2)}, u32[]{:S(2)}) collective-permute-start(bf16[256,512]{1,0:T(8,128)(2,1)S(1)} %select_select_fusion.1), channel_id=1, source_target_pairs={{4,12},{5,13},{6,14},{7,15},{20,28},{21,29},{22,30},{23,31},{36,44... | collective-permute-start | bytes 786440 | tf_op jit(solution)/shard_map/ppermute | solution.py:29
  43.9 63.8 %collective-permute-start.2 = (bf16[256,512]{1,0:T(8,128)(2,1)S(1)}, bf16[256,512]{1,0:T(8,128)(2,1)S(1)}, u32[]{:S(2)}, u32[]{:S(2)}) collective-permute-start(bf16[256,512]{1,0:T(8,128)(2,1)S(1)} %select_select_fusion.1), channel_id=1, source_target_pairs={{8,12},{9,13},{10,14},{11,15},{24,28},{25,29},{26,30},{27,31},{40,... | collective-permute-start | bytes 786440 | tf_op jit(solution)/shard_map/ppermute | solution.py:29
  46.9 60.9 %collective-permute-start.4 = (bf16[256,512]{1,0:T(8,128)(2,1)S(1)}, bf16[256,512]{1,0:T(8,128)(2,1)S(1)}, u32[]{:S(2)}, u32[]{:S(2)}) collective-permute-start(bf16[256,512]{1,0:T(8,128)(2,1)S(1)} %select_select_fusion.1), channel_id=1, source_target_pairs={{4,6},{5,7},{6,4},{7,5},{8,10},{9,11},{10,8},{11,9},{20,22},{21,23... | collective-permute-start | bytes 786440 | tf_op jit(solution)/shard_map/ppermute | solution.py:29
  49.2 5.8 %collective-permute-start.38 = (bf16[2,512]{1,0:T(2,128)(2,1)S(1)}, bf16[2,512]{1,0:T(2,128)(2,1)S(1)}, u32[]{:S(2)}, u32[]{:S(2)}) collective-permute-start(bf16[2,512]{1,0:T(2,128)(2,1)S(1)} %get-tuple-element.35), channel_id=1, source_target_pairs={{0,64},{1,65},{2,66},{3,67},{4,68},{5,69},{6,70},{7,71},{8,72},{9,... | collective-permute-start | bytes 6152 | tf_op jit(solution)/shard_map/ppermute | solution.py:29
  55.0 6.6 %collective-permute-start.39 = (bf16[2,512]{1,0:T(2,128)(2,1)S(1)}, bf16[2,512]{1,0:T(2,128)(2,1)S(1)}, u32[]{:S(2)}, u32[]{:S(2)}) collective-permute-start(bf16[2,512]{1,0:T(2,128)(2,1)S(1)} %get-tuple-element.35), channel_id=1, source_target_pairs={{0,96},{1,97},{2,98},{3,99},{4,100},{5,101},{6,102},{7,103},{8,104... | collective-permute-start | bytes 6152 | tf_op jit(solution)/shard_map/ppermute | solution.py:29
  61.6 7.5 %collective-permute-start.40 = (bf16[2,512]{1,0:T(2,128)(2,1)S(1)}, bf16[2,512]{1,0:T(2,128)(2,1)S(1)}, u32[]{:S(2)}, u32[]{:S(2)}) collective-permute-start(bf16[2,512]{1,0:T(2,128)(2,1)S(1)} %get-tuple-element.35), channel_id=1, source_target_pairs={{0,128},{1,129},{2,130},{3,131},{4,132},{5,133},{6,134},{7,135},{8... | collective-permute-start | bytes 6152 | tf_op jit(solution)/shard_map/ppermute | solution.py:29
  69.1 5.4 %collective-permute-start.41 = (bf16[2,512]{1,0:T(2,128)(2,1)S(1)}, bf16[2,512]{1,0:T(2,128)(2,1)S(1)}, u32[]{:S(2)}, u32[]{:S(2)}) collective-permute-start(bf16[2,512]{1,0:T(2,128)(2,1)S(1)} %get-tuple-element.35), channel_id=1, source_target_pairs={{0,160},{1,161},{2,162},{3,163},{4,164},{5,165},{6,166},{7,167},{8... | collective-permute-start | bytes 6152 | tf_op jit(solution)/shard_map/ppermute | solution.py:29
  74.4 4.5 %collective-permute-start.42 = (bf16[2,512]{1,0:T(2,128)(2,1)S(1)}, bf16[2,512]{1,0:T(2,128)(2,1)S(1)}, u32[]{:S(2)}, u32[]{:S(2)}) collective-permute-start(bf16[2,512]{1,0:T(2,128)(2,1)S(1)} %get-tuple-element.35), channel_id=1, source_target_pairs={{0,192},{1,193},{2,194},{3,195},{4,196},{5,197},{6,198},{7,199},{8... | collective-permute-start | bytes 6152 | tf_op jit(solution)/shard_map/ppermute | solution.py:29
  86.8 5.2 %collective-permute-start.45 = (bf16[16,512]{1,0:T(8,128)(2,1)S(1)}, bf16[16,512]{1,0:T(8,128)(2,1)S(1)}, u32[]{:S(2)}, u32[]{:S(2)}) collective-permute-start(bf16[16,512]{1,0:T(8,128)(2,1)S(1)} %reshape.20), channel_id=1, source_target_pairs={{0,16},{1,17},{2,18},{3,19},{4,20},{5,21},{6,22},{7,23},{8,24},{9,... | collective-permute-start | bytes 49160 | tf_op jit(solution)/shard_map/ppermute | solution.py:29
  92.0 4.5 %collective-permute-start.46 = (bf16[16,512]{1,0:T(8,128)(2,1)S(1)}, bf16[16,512]{1,0:T(8,128)(2,1)S(1)}, u32[]{:S(2)}, u32[]{:S(2)}) collective-permute-start(bf16[16,512]{1,0:T(8,128)(2,1)S(1)} %reshape.20), channel_id=1, source_target_pairs={{0,24},{1,25},{2,26},{3,27},{4,28},{5,29},{6,30},{7,31},{8,0},{9,1... | collective-permute-start | bytes 49160 | tf_op jit(solution)/shard_map/ppermute | solution.py:29
  96.5 5.5 %collective-permute-start.47 = (bf16[64,512]{1,0:T(8,128)(2,1)S(1)}, bf16[64,512]{1,0:T(8,128)(2,1)S(1)}, u32[]{:S(2)}, u32[]{:S(2)}) collective-permute-start(bf16[64,512]{1,0:T(8,128)(2,1)S(1)} %bitcast.60), channel_id=1, source_target_pairs={{0,2},{1,3},{2,4},{3,5},{4,6},{5,7},{6,0},{7,1},{8,10},{9,11},{10,... | collective-permute-start | bytes 196616 | tf_op jit(solution)/shard_map/ppermute | solution.py:29
  102.0 5.8 %collective-permute-start.48 = (bf16[64,512]{1,0:T(8,128)(2,1)S(1)}, bf16[64,512]{1,0:T(8,128)(2,1)S(1)}, u32[]{:S(2)}, u32[]{:S(2)}) collective-permute-start(bf16[64,512]{1,0:T(8,128)(2,1)S(1)} %bitcast.62), channel_id=1, source_target_pairs={{0,4},{1,5},{2,6},{3,7},{4,0},{5,1},{6,2},{7,3},{8,12},{9,13},{10,... | collective-permute-start | bytes 196616 | tf_op jit(solution)/shard_map/ppermute | solution.py:29
  107.7 4.3 %collective-permute-start.49 = (bf16[64,512]{1,0:T(8,128)(2,1)S(1)}, bf16[64,512]{1,0:T(8,128)(2,1)S(1)}, u32[]{:S(2)}, u32[]{:S(2)}) collective-permute-start(bf16[64,512]{1,0:T(8,128)(2,1)S(1)} %bitcast.63), channel_id=1, source_target_pairs={{0,6},{1,7},{2,0},{3,1},{4,2},{5,3},{6,4},{7,5},{8,14},{9,15},{10,... | collective-permute-start | bytes 196616 | tf_op jit(solution)/shard_map/ppermute | solution.py:29
  108.0 4.2 %collective-permute-start.6 = (bf16[256,512]{1,0:T(8,128)(2,1)S(1)}, bf16[256,512]{1,0:T(8,128)(2,1)S(1)}, u32[]{:S(2)}, u32[]{:S(2)}) collective-permute-start(bf16[256,512]{1,0:T(8,128)(2,1)S(1)} %broadcast_select_fusion.2.a_ref), channel_id=1, source_target_pairs={{0,1},{1,0},{2,3},{3,2},{4,5},{5,4},{6,7},{7,6},{8,9},{9,8},{10,11... | collective-permute-start | bytes 786440 | tf_op jit(solution)/shard_map/ppermute | solution.py:29
  108.1 4.1 %collective-permute-start.7 = (bf16[256,512]{1,0:T(8,128)(2,1)S(1)}, bf16[256,512]{1,0:T(8,128)(2,1)S(1)}, u32[]{:S(2)}, u32[]{:S(2)}) collective-permute-start(bf16[256,512]{1,0:T(8,128)(2,1)S(1)} %get-tuple-element.36.b_ref), channel_id=1, source_target_pairs={{0,1},{1,0},{2,3},{3,2},{4,5},{5,4},{6,7},{7,6},{8,9},{9,8},{10,11... | collective-permute-start | bytes 786440 | tf_op jit(solution)/shard_map/ppermute | solution.py:29
  112.0 27.1 %collective-permute-start.50 = (bf16[256,512]{1,0:T(8,128)(2,1)S(1)}, bf16[256,512]{1,0:T(8,128)(2,1)S(1)}, u32[]{:S(2)}, u32[]{:S(2)}) collective-permute-start(bf16[256,512]{1,0:T(8,128)(2,1)S(1)} %bitcast.58), channel_id=1, source_target_pairs={{0,1},{1,0},{2,3},{3,2},{4,5},{5,4},{6,7},{7,6},{8,9},{9,8},{10,11... | collective-permute-start | bytes 786440 | tf_op jit(solution)/shard_map/ppermute | solution.py:29
  136.9 9.2 %collective-permute-start.19 = (bf16[256,512]{1,0:T(8,128)(2,1)S(1)}, bf16[256,512]{1,0:T(8,128)(2,1)S(1)}, u32[]{:S(2)}, u32[]{:S(2)}) collective-permute-start(bf16[256,512]{1,0:T(8,128)(2,1)S(1)} %get-tuple-element.31), channel_id=1, source_target_pairs={{0,224},{1,225},{2,226},{3,227},{4,228},{5,229},{6,230},{7,231},{8... | collective-permute-start | bytes 786440 | tf_op jit(solution)/shard_map/ppermute | solution.py:29
  137.0 10.5 %collective-permute-start.15 = (bf16[256,512]{1,0:T(8,128)(2,1)S(1)}, bf16[256,512]{1,0:T(8,128)(2,1)S(1)}, u32[]{:S(2)}, u32[]{:S(2)}) collective-permute-start(bf16[256,512]{1,0:T(8,128)(2,1)S(1)} %get-tuple-element.27), channel_id=1, source_target_pairs={{0,32},{1,33},{2,34},{3,35},{4,36},{5,37},{6,38},{7,39},{8,40},{9,... | collective-permute-start | bytes 786440 | tf_op jit(solution)/shard_map/ppermute | solution.py:29
  139.1 12.2 %collective-permute-start.11 = (bf16[256,512]{1,0:T(8,128)(2,1)S(1)}, bf16[256,512]{1,0:T(8,128)(2,1)S(1)}, u32[]{:S(2)}, u32[]{:S(2)}) collective-permute-start(bf16[256,512]{1,0:T(8,128)(2,1)S(1)} %get-tuple-element.22), channel_id=1, source_target_pairs={{0,224},{1,225},{2,226},{3,227},{4,228},{5,229},{6,230},{7,231},{8... | collective-permute-start | bytes 786440 | tf_op jit(solution)/shard_map/ppermute | solution.py:29
  140.5 12.7 %collective-permute-start.8 = (bf16[256,512]{1,0:T(8,128)(2,1)S(1)}, bf16[256,512]{1,0:T(8,128)(2,1)S(1)}, u32[]{:S(2)}, u32[]{:S(2)}) collective-permute-start(bf16[256,512]{1,0:T(8,128)(2,1)S(1)} %get-tuple-element.19), channel_id=1, source_target_pairs={{0,32},{1,33},{2,34},{3,35},{4,36},{5,37},{6,38},{7,39},{8,40},{9,... | collective-permute-start | bytes 786440 | tf_op jit(solution)/shard_map/ppermute | solution.py:29
  146.2 13.0 %collective-permute-start.20 = (bf16[256,512]{1,0:T(8,128)(2,1)S(1)}, bf16[256,512]{1,0:T(8,128)(2,1)S(1)}, u32[]{:S(2)}, u32[]{:S(2)}) collective-permute-start(bf16[256,512]{1,0:T(8,128)(2,1)S(1)} %add_convert_fusion.3), channel_id=1, source_target_pairs={{0,224},{1,225},{2,226},{3,227},{4,228},{5,229},{6,230},{7,231},{8... | collective-permute-start | bytes 786440 | tf_op jit(solution)/shard_map/ppermute | solution.py:29
  147.6 11.2 %collective-permute-start.16 = (bf16[256,512]{1,0:T(8,128)(2,1)S(1)}, bf16[256,512]{1,0:T(8,128)(2,1)S(1)}, u32[]{:S(2)}, u32[]{:S(2)}) collective-permute-start(bf16[256,512]{1,0:T(8,128)(2,1)S(1)} %add_convert_fusion.6), channel_id=1, source_target_pairs={{0,32},{1,33},{2,34},{3,35},{4,36},{5,37},{6,38},{7,39},{8,40},{9,... | collective-permute-start | bytes 786440 | tf_op jit(solution)/shard_map/ppermute | solution.py:29
  151.4 10.9 %collective-permute-start.12 = (bf16[256,512]{1,0:T(8,128)(2,1)S(1)}, bf16[256,512]{1,0:T(8,128)(2,1)S(1)}, u32[]{:S(2)}, u32[]{:S(2)}) collective-permute-start(bf16[256,512]{1,0:T(8,128)(2,1)S(1)} %add_convert_fusion.9), channel_id=1, source_target_pairs={{0,224},{1,225},{2,226},{3,227},{4,228},{5,229},{6,230},{7,231},{8... | collective-permute-start | bytes 786440 | tf_op jit(solution)/shard_map/ppermute | solution.py:29
  153.2 16.6 %collective-permute-start.9 = (bf16[256,512]{1,0:T(8,128)(2,1)S(1)}, bf16[256,512]{1,0:T(8,128)(2,1)S(1)}, u32[]{:S(2)}, u32[]{:S(2)}) collective-permute-start(bf16[256,512]{1,0:T(8,128)(2,1)S(1)} %add_convert_fusion.11), channel_id=1, source_target_pairs={{0,32},{1,33},{2,34},{3,35},{4,36},{5,37},{6,38},{7,39},{8,40},{9,... | collective-permute-start | bytes 786440 | tf_op jit(solution)/shard_map/ppermute | solution.py:29
  158.8 10.8 %collective-permute-start.17 = (bf16[256,512]{1,0:T(8,128)(2,1)S(1)}, bf16[256,512]{1,0:T(8,128)(2,1)S(1)}, u32[]{:S(2)}, u32[]{:S(2)}) collective-permute-start(bf16[256,512]{1,0:T(8,128)(2,1)S(1)} %add_convert_fusion.5), channel_id=1, source_target_pairs={{0,32},{1,33},{2,34},{3,35},{4,36},{5,37},{6,38},{7,39},{8,40},{9,... | collective-permute-start | bytes 786440 | tf_op jit(solution)/shard_map/ppermute | solution.py:29
  159.2 17.4 %collective-permute-start.21 = (bf16[256,512]{1,0:T(8,128)(2,1)S(1)}, bf16[256,512]{1,0:T(8,128)(2,1)S(1)}, u32[]{:S(2)}, u32[]{:S(2)}) collective-permute-start(bf16[256,512]{1,0:T(8,128)(2,1)S(1)} %add_convert_fusion.2), channel_id=1, source_target_pairs={{0,224},{1,225},{2,226},{3,227},{4,228},{5,229},{6,230},{7,231},{8... | collective-permute-start | bytes 786440 | tf_op jit(solution)/shard_map/ppermute | solution.py:29
  162.3 10.4 %collective-permute-start.13 = (bf16[256,512]{1,0:T(8,128)(2,1)S(1)}, bf16[256,512]{1,0:T(8,128)(2,1)S(1)}, u32[]{:S(2)}, u32[]{:S(2)}) collective-permute-start(bf16[256,512]{1,0:T(8,128)(2,1)S(1)} %add_convert_fusion.8), channel_id=1, source_target_pairs={{0,224},{1,225},{2,226},{3,227},{4,228},{5,229},{6,230},{7,231},{8... | collective-permute-start | bytes 786440 | tf_op jit(solution)/shard_map/ppermute | solution.py:29
  169.7 10.5 %collective-permute-start.18 = (bf16[256,512]{1,0:T(8,128)(2,1)S(1)}, bf16[256,512]{1,0:T(8,128)(2,1)S(1)}, u32[]{:S(2)}, u32[]{:S(2)}) collective-permute-start(bf16[256,512]{1,0:T(8,128)(2,1)S(1)} %add_convert_fusion.4), channel_id=1, source_target_pairs={{0,32},{1,33},{2,34},{3,35},{4,36},{5,37},{6,38},{7,39},{8,40},{9,... | collective-permute-start | bytes 786440 | tf_op jit(solution)/shard_map/ppermute | solution.py:29
  169.9 14.7 %collective-permute-start.10 = (bf16[256,512]{1,0:T(8,128)(2,1)S(1)}, bf16[256,512]{1,0:T(8,128)(2,1)S(1)}, u32[]{:S(2)}, u32[]{:S(2)}) collective-permute-start(bf16[256,512]{1,0:T(8,128)(2,1)S(1)} %add_convert_fusion.10), channel_id=1, source_target_pairs={{0,32},{1,33},{2,34},{3,35},{4,36},{5,37},{6,38},{7,39},{8,40},{9,... | collective-permute-start | bytes 786440 | tf_op jit(solution)/shard_map/ppermute | solution.py:29
  172.8 11.8 %collective-permute-start.14 = (bf16[256,512]{1,0:T(8,128)(2,1)S(1)}, bf16[256,512]{1,0:T(8,128)(2,1)S(1)}, u32[]{:S(2)}, u32[]{:S(2)}) collective-permute-start(bf16[256,512]{1,0:T(8,128)(2,1)S(1)} %add_convert_fusion.7), channel_id=1, source_target_pairs={{0,224},{1,225},{2,226},{3,227},{4,228},{5,229},{6,230},{7,231},{8... | collective-permute-start | bytes 786440 | tf_op jit(solution)/shard_map/ppermute | solution.py:29
  180.3 8.0 %collective-permute-start.22 = (bf16[256,512]{1,0:T(8,128)(2,1)S(1)}, bf16[256,512]{1,0:T(8,128)(2,1)S(1)}, u32[]{:S(2)}, u32[]{:S(2)}) collective-permute-start(bf16[256,512]{1,0:T(8,128)(2,1)S(1)} %add_convert_fusion.1), channel_id=1, source_target_pairs={{0,16},{1,17},{2,18},{3,19},{4,20},{5,21},{6,22},{7,23},{8,24},{9,... | collective-permute-start | bytes 786440 | tf_op jit(solution)/shard_map/ppermute | solution.py:29
  (9 other events, 343.0 us)

commit v2 on v0

v2 whole, which is shorter than its diff:
```python
import functools

import jax
import jax.numpy as jnp
from jax import lax
from jax.experimental import pallas as pl
from jax.experimental.pallas import tpu as pltpu
from jax.sharding import PartitionSpec as P

AXES = ("row", "rep")
X, Y, Z, C = 4, 4, 8, 2


def index_of(x, y, z, c):
    return (z * 2 + x // 2) * 16 + (x % 2) * 8 + y * 2 + c


def pairs(move):
    out = []
    for z in range(Z):
        for x in range(X):
            for y in range(Y):
                for c in range(C):
                    to = move(x, y, z, c)
                    if to is not None:
                        out.append((index_of(x, y, z, c), index_of(to[0] % X, to[1] % Y, to[2] % Z, to[3] % C)))
    return out


def send(value, move):
    return lax.ppermute(value, AXES, pairs(move))


def add(*terms):
    total = terms[0].astype(jnp.float32)
    for term in terms[1:]:
        total = total + term.astype(jnp.float32)
    return total


def narrow(value):
    return value.astype(jnp.bfloat16)


def flood(block, x_lo, y):
    def across(x, y, z, c):
        return (x + 1, y, z, c) if x % 2 == 0 and y < 2 else None

    def outward(x, y, z, c):
        return (x, 3 - y, z, c) if x % 2 == 0 and y < 2 else None

    def swap(x, y, z, c):
        return (x, 1 - y, z, c) if x % 2 == 0 and y < 2 else None

    by_x = send(block, across)
    by_y = send(block, outward)
    swapped = send(block, swap)

    def swap_rest(x, y, z, c):
        return (x, 5 - y, z, c) if x % 2 == 0 and y >= 2 else None

    def across_all(x, y, z, c):
        return (x + 1, y, z, c) if x % 2 == 0 else None

    def distant(x, y, z, c):
        return (x, y + 2, z, c) if x % 2 == 1 and y < 2 else None

    by_far = send(by_x, distant)
    by_swap = send(by_y, swap_rest)
    by_x2 = send(jnp.where(y < 2, swapped, by_y), across_all)
    first = jnp.where(x_lo == 0, jnp.where(y < 2, block, by_y), jnp.where(y < 2, by_x, by_x2))
    second = jnp.where(x_lo == 0, jnp.where(y < 2, swapped, by_swap), jnp.where(y < 2, by_x2, by_far))
    flip = jnp.logical_or(y == 1, y == 2)
    even = jnp.where(flip, second, first)
    odd = jnp.where(flip, first, second)
    return even, odd


FIRST = [(4, 1), (3, 1), (5, 1)]
SECOND = [(4, 0), (2, 1), (6, 1), (3, 0), (5, 0), (1, 1), (7, 1), (2, 0), (6, 0), (0, 1), (1, 0), (7, 0), (0, 0)]
SLOTS = 96


def plan_kernel(src_ref, dst_ref, count_ref, place_ref, order_ref, list_ref, filled_ref):
    z, xh, core = place_ref[0], place_ref[1], place_ref[2]
    for i in range(32):
        filled_ref[i] = 0
    for section in range(4):
        slot = jnp.where(core == section % 2, section // 2, 2 + section // 2)

        def step(t, carry):
            d = dst_ref[section, t]
            s = src_ref[section, t]
            rel = lax.rem(d // 4 - z + 8, 8)
            half = lax.rem(d // 2 + xh, 2)
            at = order_ref[rel * 2 + half] * 2 + lax.rem(d, 2)
            n = filled_ref[at]
            list_ref[at, n] = (section * 24 + t) * 8 + slot * 2 + s
            filled_ref[at] = n + 1
            return carry

        lax.fori_loop(0, count_ref[section], step, 0)


def plan(src, dst, count, place):
    order = [0] * 16
    for i, (rel, half) in enumerate(FIRST + SECOND):
        order[rel * 2 + half] = i
    smem = pl.BlockSpec(memory_space=pltpu.SMEM)
    return pl.pallas_call(
        plan_kernel,
        out_shape=[
            jax.ShapeDtypeStruct((32, 8), jnp.int32),
            jax.ShapeDtypeStruct((32,), jnp.int32),
        ],
        in_specs=[smem] * 5,
        out_specs=[smem, smem],
        name="plan",
    )(src, dst, count, place, jnp.array(order, jnp.int32))


def rows_kernel(base, groups, list_ref, filled_ref, tiles_ref, sources_ref, *rest):
    outs, acc = rest[:groups], rest[groups]

    def pair(at, p, n):
        one = list_ref[at, 2 * p]
        paired = 2 * p + 1 < n
        two = jnp.where(paired, list_ref[at, 2 * p + 1], 0)
        second = tiles_ref[two // 8]
        left = jnp.concatenate([tiles_ref[one // 8], jnp.where(paired, second, jnp.zeros_like(second))], axis=0)
        right = jnp.concatenate([sources_ref[lax.rem(one, 8)], sources_ref[lax.rem(two, 8)]], axis=0)
        return lax.dot_general(left, right, (((0,), (0,)), ((), ())), preferred_element_type=jnp.float32)

    for g in range(groups):
        def block(j, carry):
            at = base + 2 * g + j
            n = filled_ref[at]
            out = outs[g].at[pl.ds(pl.multiple_of(j * 128, 128), 128), :]

            @pl.when(n == 0)
            def _():
                out[...] = jnp.zeros((128, 512), jnp.bfloat16)

            @pl.when(n > 0)
            def _():
                acc[...] = pair(at, 0, n)

                def more(p, c):
                    acc[...] += pair(at, p, n)
                    return c

                lax.fori_loop(1, (n + 1) // 2, more, 0)
                out[...] = acc[...].astype(jnp.bfloat16)

            return carry

        lax.fori_loop(0, 2, block, 0)


def rows(base, groups, lists, filled, tiles, sources, name):
    smem = pl.BlockSpec(memory_space=pltpu.SMEM)
    vmem = pl.BlockSpec(memory_space=pltpu.VMEM)
    return pl.pallas_call(
        functools.partial(rows_kernel, base, groups),
        out_shape=[jax.ShapeDtypeStruct((256, 512), jnp.bfloat16)] * groups,
        in_specs=[smem, smem, vmem, vmem],
        out_specs=[vmem] * groups,
        scratch_shapes=[pltpu.VMEM((128, 512), jnp.float32)],
        compiler_params=pltpu.CompilerParams(vmem_limit_bytes=16 * 1024 * 1024),
        cost_estimate=pl.CostEstimate(flops=groups * 400_000_000, bytes_accessed=groups * 1_000_000, transcendentals=0),
        name=name,
    )(lists, filled, tiles, sources)


def stage_kernel(sums, n_in, *refs):
    ins, outs = refs[:n_in], refs[n_in:]
    for out, terms in zip(outs, sums):
        total = None
        for at, start in terms:
            term = ins[at][pl.ds(start, out.shape[0]), :].astype(jnp.float32)
            total = term if total is None else total + term
        out[...] = total.astype(out.dtype)


def stage(name, *sums):
    arrays, plans, shapes = [], [], []
    for terms in sums:
        plan_of, rows_of = [], None
        for term in terms:
            value, start, count = term if isinstance(term, tuple) else (term, 0, term.shape[0])
            place = next((i for i, known in enumerate(arrays) if known is value), None)
            if place is None:
                place = len(arrays)
                arrays.append(value)
            plan_of.append((place, start))
            rows_of = count
        plans.append(tuple(plan_of))
        shapes.append(jax.ShapeDtypeStruct((rows_of, 512), jnp.bfloat16))
    vmem = pl.BlockSpec(memory_space=pltpu.VMEM)
    return pl.pallas_call(
        functools.partial(stage_kernel, tuple(plans), len(arrays)),
        out_shape=shapes,
        in_specs=[vmem] * len(arrays),
        out_specs=[vmem] * len(shapes),
        compiler_params=pltpu.CompilerParams(vmem_limit_bytes=16 * 1024 * 1024),
        name=name,
    )(*arrays)


def top(value):
    return (value, 0, 128)


def low(value):
    return (value, 128, 128)


def up(x, y, z, c):
    return (x, y, z + 1, c)


def down(x, y, z, c):
    return (x, y, z - 1, c)


def halves(value, bit):
    rows = value.shape[0] // 2
    kept = lax.dynamic_slice_in_dim(value, bit * rows, rows, 0)
    return kept, narrow(lax.dynamic_slice_in_dim(value, (1 - bit) * rows, rows, 0))


def joined(bit, value, got):
    return jnp.concatenate([jnp.where(bit == 0, value, got), jnp.where(bit == 0, got, value)])


def flipped(axis, step):
    def move(x, y, z, c):
        at = {"x": x, "y": y, "z": z, "c": c}
        at[axis] ^= step
        return at["x"], at["y"], at["z"], at["c"]

    return move


def local(grad_out, relu_mask, aggregated, weight, tile_values, tile_src, tile_dst, tile_count):
    row, rep = lax.axis_index("row"), lax.axis_index("rep")
    z, x_hi = row // 2, row % 2
    x_lo, y, core = rep // 8, (rep // 2) % 4, rep % 2
    place = jnp.stack([z, x_hi, core]).astype(jnp.int32)
    masked = jnp.where(relu_mask != 0, grad_out, jnp.zeros_like(grad_out))
    node_grad = lax.dot_general(
        masked, weight, (((1,), (1,)), ((), ())), preferred_element_type=jnp.float32
    ).astype(jnp.bfloat16)
    tiles = tile_values.reshape(SLOTS, 128, 128)
    lists, filled = plan(tile_src[0, 0], tile_dst[0, 0], tile_count[0, 0], place)
    aggregated, _ = lax.optimization_barrier((aggregated, node_grad))
    w = lax.dot_general(aggregated, masked, (((0,), (0,)), ((), ())), preferred_element_type=jnp.float32)

    even, odd = flood(node_grad, x_lo, y)
    kept, given = halves(w, core)
    w = add(kept, send(given, flipped("c", 1)))
    kept, given = halves(w, y % 2)
    w = add(kept, send(given, flipped("y", 1)))
    kept, given = halves(w, y // 2)
    even2, odd2 = send(even, flipped("c", 1)), send(odd, flipped("c", 1))
    even, odd, even2, odd2, given = stage("s0", [even], [odd], [even2], [odd2], [given])
    sources = jnp.concatenate([even, odd, even2, odd2]).reshape(8, 128, 512)
    w_got = send(given, flipped("y", 2))
    part = {}
    part.update(zip(FIRST, rows(0, len(FIRST), lists, filled, tiles, sources, "rows_first")))
    cross = flipped("x", 2)
    crossed = send(part[4, 1], cross)
    o_up, o_down = send(part[3, 1], up), send(part[5, 1], down)
    late = rows(2 * len(FIRST), len(SECOND), lists, filled, tiles, sources, "rows_second")
    part.update(zip(SECOND, late))

    a_up, b_down, w = stage(
        "s1", [top(part[4, 0]), top(crossed)], [low(part[4, 0]), low(crossed)], [narrow(add(kept, w_got))]
    )
    a_up, b_down, w_got = send(a_up, up), send(b_down, down), send(w, flipped("z", 1))
    o_up, o_down, w = stage("s2", [part[2, 1], o_up], [part[6, 1], o_down], [w, w_got])
    o_up, o_down, w_got = send(o_up, up), send(o_down, down), send(w, flipped("z", 2))
    a_up, b_up, a_down, b_down, w = stage(
        "s3",
        [top(part[3, 0]), a_up],
        [low(part[3, 0])],
        [top(part[5, 0])],
        [low(part[5, 0]), b_down],
        [w, w_got],
    )
    m_up, m_down = send(jnp.concatenate([a_up, b_up]), up), send(jnp.concatenate([a_down, b_down]), down)
    w_got = send(w, flipped("z", 4))
    o_up, o_down, w = stage("s4", [part[1, 1], o_up], [part[7, 1], o_down], [w, w_got])
    o_up, o_down, w_got = send(o_up, up), send(o_down, down), send(w, flipped("x", 1))
    m_up, m_down, w = stage("s5", [part[2, 0], m_up], [part[6, 0], m_down], [w, w_got])
    m_up, m_down, w_got = send(m_up, up), send(m_down, down), send(w, flipped("x", 2))
    crossing, w = stage("s6", [part[0, 1], o_up, o_down], [w, w_got])
    crossed, w_got = send(crossing, cross), send(w, flipped("y", 2))
    w = joined(y // 2, w, w_got)
    m_up, m_down, w = stage("s7", [part[1, 0], m_up], [part[7, 0], m_down], [w])
    m_up, m_down, w_got = send(m_up, up), send(m_down, down), send(w, flipped("y", 1))
    w = joined(y % 2, w, w_got)
    w = joined(core, w, send(w, flipped("c", 1)))
    (input_grad,) = stage("s8", [part[0, 0], m_up, m_down, crossed])
    return (input_grad, w.astype(jnp.float32))


def solution(mesh):
    in_specs = (
        P(("row", "rep"), None),
        P(("row", "rep"), None),
        P(("row", "rep"), None),
        P(),
        P("row", "rep", None, None, None, None),
        P("row", "rep", None, None),
        P("row", "rep", None, None),
        P("row", "rep", None),
    )
    out_specs = (P(("row", "rep"), None), P())
    return jax.shard_map(local, mesh=mesh, in_specs=in_specs, out_specs=out_specs, check_vma=False)
```

time: 626 us -> 111 us (0.18)
  the two profiles are of different devices: /device:TPU:2 before, /device:TPU:70 now
where the time goes in v2:
time: 111 us; the launch traced here: 109 us
  starting transfers between devices  47.9 us (43%)
  waiting for transfers between devices  42.2 us (38%)
  Pallas kernels  11.5 us (10%)
  matrix products  3.01 us (3%)
  other arithmetic  2.22 us (2%)
  local copies, waits for them, and re-layouts  1.14 us (1%)
    ppermute x35, starting transfers between devices, send(): return lax.ppermute(value, AXES, pairs(move))  47.9 us
    ppermute x35, waiting for transfers between devices, send(): return lax.ppermute(value, AXES, pairs(move))  42.2 us
    pallas_call x2, Pallas kernels, rows(): pl.pallas_call(functools.partial(rows_kernel, base, groups), out_shape=[j...  7.39 us
    pallas_call x1, Pallas kernels, plan(): pl.pallas_call(plan_kernel, out_shape=[jax.ShapeDtypeStruct((32, 8), jnp....  2.39 us
  transfers between devices with their start and end apart: 35, of which 20 were waited for; matrix products, arithmetic and copies ran while one was open for 2% of the time, Pallas kernels for 10%

profile of v2, /device:TPU:70, one launch (start us, length us, event | category | flops | bytes accessed | tf_op | source)
XLA Modules:
  0.0 108.9 jit_solution(12303261487132762722)
XLA Ops:
  0.6 1.0 copy-done
  1.7 1.5 %convolution_convert_fusion = bf16[256,512]{1,0:T(8,128)(2,1)S(1)} fusion(bf16[512,512]{1,0:T(8,128)(2,1)S(1)} %copy-done, bf16[256,512]{1,0:T(8,128)(2,1)} %param.9, s32[256,512]{1,0:T(8,128)} %param.10), kind=kOutput, calls=%fused_computation | convolution fusion | flops 134610944 | bytes 1572864 | tf_op jit(solution)/shard_map/dot_general | solution.py:251
  3.1 1.3 %collective-permute-start.4 = (bf16[256,512]{1,0:T(8,128)(2,1)S(1)}, bf16[256,512]{1,0:T(8,128)(2,1)S(1)}, u32[]{:S(2)}, u32[]{:S(2)}) collective-permute-start(bf16[256,512]{1,0:T(8,128)(2,1)S(1)} %convolution_convert_fusion), channel_id=1, source_target_pairs={{0,8},{1,9},{2,10},{3,11},{16,24},{17,25},{18,26},{19,27},{32,40},... | collective-permute-start | bytes 786440 | tf_op jit(solution)/shard_map/ppermute | solution.py:31
  4.4 0.7 collective-permute-start.1
  5.1 0.7 collective-permute-start
  5.8 1.5 %fusion = f32[512,512]{1,0:T(8,128)S(1)} fusion(bf16[256,512]{1,0:T(8,128)(2,1)} %param.11, bf16[256,512]{1,0:T(8,128)(2,1)} %param.9, s32[256,512]{1,0:T(8,128)} %param.10), kind=kOutput, calls=%fused_computation.26 | convolution fusion | flops 134479872 | bytes 2097152 | tf_op jit(solution)/shard_map/dot_general | solution.py:257
  8.1 2.4 %plan.1 = (s32[32,8]{1,0:T(8,128)}, s32[32]{0:T(128)}) custom-call(s32[4,24]{1,0:T(4,128)} %bitcast.14, s32[4,24]{1,0:T(4,128)} %bitcast.15, s32[4]{0:T(128)} %bitcast.16, s32[3]{0:T(128)} %pad_add_fusion.place_ref, s32[16]{0:T(128)} %constant.92.clone.order_ref), custom_call_target="tpu_custom_call" | custom-call | tf_op jit(solution)/shard_map/plan/pallas_call | solution.py:110
  10.6 1.3 %collective-permute-start.3 = (bf16[256,512]{1,0:T(8,128)(2,1)S(1)}, bf16[256,512]{1,0:T(8,128)(2,1)S(1)}, u32[]{:S(2)}, u32[]{:S(2)}) collective-permute-start(bf16[256,512]{1,0:T(8,128)(2,1)S(1)} %broadcast_select_fusion.2), channel_id=1, source_target_pairs={{0,8},{1,9},{2,10},{3,11},{4,12},{5,13},{6,14},{7,15},{16,24},{17,... | collective-permute-start | bytes 786440 | tf_op jit(solution)/shard_map/ppermute | solution.py:31
  11.9 0.7 collective-permute-start.2
  13.1 4.5 %collective-permute-start.5 = (bf16[256,512]{1,0:T(8,128)(2,1)S(1)}, bf16[256,512]{1,0:T(8,128)(2,1)S(1)}, u32[]{:S(2)}, u32[]{:S(2)}) collective-permute-start(bf16[256,512]{1,0:T(8,128)(2,1)S(1)} %collective-permute-done.4), channel_id=1, source_target_pairs={{8,12},{9,13},{10,14},{11,15},{24,28},{25,29},{26,30},{27,31},{40,... | collective-permute-start | bytes 786440 | tf_op jit(solution)/shard_map/ppermute | solution.py:31
  18.0 6.3 %collective-permute-done.5 = bf16[256,512]{1,0:T(8,128)(2,1)S(1)} collective-permute-done((bf16[256,512]{1,0:T(8,128)(2,1)S(1)}, bf16[256,512]{1,0:T(8,128)(2,1)S(1)}, u32[]{:S(2)}, u32[]{:S(2)}) %collective-permute-start.5) | collective-permute-done | bytes 262176 | tf_op jit(solution)/shard_map/ppermute | solution.py:31
  24.2 1.5 %collective-permute-done.3 = bf16[256,512]{1,0:T(8,128)(2,1)S(1)} collective-permute-done((bf16[256,512]{1,0:T(8,128)(2,1)S(1)}, bf16[256,512]{1,0:T(8,128)(2,1)S(1)}, u32[]{:S(2)}, u32[]{:S(2)}) %collective-permute-start.3) | collective-permute-done | bytes 262176 | tf_op jit(solution)/shard_map/ppermute | solution.py:31
  26.5 0.7 collective-permute-done.9
  27.9 2.6 %collective-permute-start.11 = (bf16[64,512]{1,0:T(8,128)(2,1)S(1)}, bf16[64,512]{1,0:T(8,128)(2,1)S(1)}, u32[]{:S(2)}, u32[]{:S(2)}) collective-permute-start(bf16[64,512]{1,0:T(8,128)(2,1)S(1)} %get-tuple-element.61), channel_id=1, source_target_pairs={{0,4},{1,5},{2,6},{3,7},{4,0},{5,1},{6,2},{7,3},{8,12},{9,13},{10,... | collective-permute-start | bytes 196616 | tf_op jit(solution)/shard_map/ppermute | solution.py:31
  30.6 2.1 %rows_first.1 = (bf16[256,512]{1,0:T(8,128)(2,1)S(1)}, bf16[256,512]{1,0:T(8,128)(2,1)S(1)}, bf16[256,512]{1,0:T(8,128)(2,1)S(1)}) custom-call(s32[32,8]{1,0:T(8,128)S(1)} %copy-done.2, s32[32]{0:T(128)S(1)} %copy-done.3, bf16[96,128,128]{2,1,0:T(8,128)(2,1)S(1)} %bitcast.12, bf16[8,128,512]{2,1,0:T(8,128)(2,1)S(1)} %bitcast.10), custom_call_target="tpu_custom_call" | custom-call | flops 1200000000 | bytes 3000000 | tf_op jit(solution)/shard_map/rows_first/pallas_call | solution.py:163
  33.3 5.3 %rows_second.1 = (bf16[256,512]{1,0:T(8,128)(2,1)S(1)}, bf16[256,512]{1,0:T(8,128)(2,1)S(1)}, bf16[256,512]{1,0:T(8,128)(2,1)S(1)}, bf16[256,512]{1,0:T(8,128)(2...) custom-call(s32[32,8]{1,0:T(8,128)S(1)} %copy-done.2, ...), custom_call_target="tpu_custom_call" | custom-call | flops 5200000000 | bytes 13000000 | tf_op jit(solution)/shard_map/rows_second/pallas_call | solution.py:163
  38.6 5.0 %collective-permute-start.14 = (bf16[256,512]{1,0:T(8,128)(2,1)S(1)}, bf16[256,512]{1,0:T(8,128)(2,1)S(1)}, u32[]{:S(2)}, u32[]{:S(2)}) collective-permute-start(bf16[256,512]{1,0:T(8,128)(2,1)S(1)} %get-tuple-element.66), channel_id=1, source_target_pairs={{0,32},{1,33},{2,34},{3,35},{4,36},{5,37},{6,38},{7,39},{8,40},{9,... | collective-permute-start | bytes 786440 | tf_op jit(solution)/shard_map/ppermute | solution.py:31
  43.7 2.1 %collective-permute-start.16 = (bf16[64,512]{1,0:T(8,128)(2,1)S(1)}, bf16[64,512]{1,0:T(8,128)(2,1)S(1)}, u32[]{:S(2)}, u32[]{:S(2)}) collective-permute-start(bf16[64,512]{1,0:T(8,128)(2,1)S(1)} %get-tuple-element.69.refs_4_), channel_id=1, source_target_pairs={{0,32},{1,33},{2,34},{3,35},{4,36},{5,37},{6,38},{7,39},{8,40},{9,... | collective-permute-start | bytes 196616 | tf_op jit(solution)/shard_map/ppermute | solution.py:31
  45.9 2.0 %collective-permute-start.13 = (bf16[128,512]{1,0:T(8,128)(2,1)S(1)}, bf16[128,512]{1,0:T(8,128)(2,1)S(1)}, u32[]{:S(2)}, u32[]{:S(2)}) collective-permute-start(bf16[128,512]{1,0:T(8,128)(2,1)S(1)} %get-tuple-element.64), channel_id=1, source_target_pairs={{0,224},{1,225},{2,226},{3,227},{4,228},{5,229},{6,230},{7,231},{8... | collective-permute-start | bytes 393224 | tf_op jit(solution)/shard_map/ppermute | solution.py:31
  47.9 2.0 %collective-permute-done.14.refs_1_ = bf16[256,512]{1,0:T(8,128)(2,1)S(1)} collective-permute-done((bf16[256,512]{1,0:T(8,128)(2,1)S(1)}, bf16[256,512]{1,0:T(8,128)(2,1)S(1)}, u32[]{:S(2)}, u32[]{:S(2)}) %collective-permute-start.14) | collective-permute-done | bytes 262176 | tf_op jit(solution)/shard_map/ppermute | solution.py:31
  49.9 2.5 %collective-permute-done.15.refs_3_ = bf16[256,512]{1,0:T(8,128)(2,1)S(1)} collective-permute-done((bf16[256,512]{1,0:T(8,128)(2,1)S(1)}, bf16[256,512]{1,0:T(8,128)(2,1)S(1)}, u32[]{:S(2)}, u32[]{:S(2)}) %collective-permute-start.15) | collective-permute-done | bytes 262176 | tf_op jit(solution)/shard_map/ppermute | solution.py:31
  52.4 0.7 collective-permute-done.16.refs_5_
  53.3 1.1 %collective-permute-start.20 = (bf16[256,512]{1,0:T(8,128)(2,1)S(1)}, bf16[256,512]{1,0:T(8,128)(2,1)S(1)}, u32[]{:S(2)}, u32[]{:S(2)}) collective-permute-start(bf16[256,512]{1,0:T(8,128)(2,1)S(1)} %get-tuple-element.77), channel_id=1, source_target_pairs={{0,32},{1,33},{2,34},{3,35},{4,36},{5,37},{6,38},{7,39},{8,40},{9,... | collective-permute-start | bytes 786440 | tf_op jit(solution)/shard_map/ppermute | solution.py:31
  54.5 1.4 %collective-permute-start.21 = (bf16[256,512]{1,0:T(8,128)(2,1)S(1)}, bf16[256,512]{1,0:T(8,128)(2,1)S(1)}, u32[]{:S(2)}, u32[]{:S(2)}) collective-permute-start(bf16[256,512]{1,0:T(8,128)(2,1)S(1)} %get-tuple-element.79), channel_id=1, source_target_pairs={{0,224},{1,225},{2,226},{3,227},{4,228},{5,229},{6,230},{7,231},{8... | collective-permute-start | bytes 786440 | tf_op jit(solution)/shard_map/ppermute | solution.py:31
  55.8 3.4 %collective-permute-done.17.refs_5_ = bf16[64,512]{1,0:T(8,128)(2,1)S(1)} collective-permute-done((bf16[64,512]{1,0:T(8,128)(2,1)S(1)}, bf16[64,512]{1,0:T(8,128)(2,1)S(1)}, u32[]{:S(2)}, u32[]{:S(2)}) %collective-permute-start.17) | collective-permute-done | bytes 65568 | tf_op jit(solution)/shard_map/ppermute | solution.py:31
  59.3 4.2 %collective-permute-start.22 = (bf16[64,512]{1,0:T(8,128)(2,1)S(1)}, bf16[64,512]{1,0:T(8,128)(2,1)S(1)}, u32[]{:S(2)}, u32[]{:S(2)}) collective-permute-start(bf16[64,512]{1,0:T(8,128)(2,1)S(1)} %get-tuple-element.80.refs_4_), channel_id=1, source_target_pairs={{0,128},{1,129},{2,130},{3,131},{4,132},{5,133},{6,134},{7,135},{8... | collective-permute-start | bytes 196616 | tf_op jit(solution)/shard_map/ppermute | solution.py:31
  63.5 0.9 collective-permute-start.19
  64.5 1.2 %collective-permute-start.18 = (bf16[256,512]{1,0:T(8,128)(2,1)S(1)}, bf16[256,512]{1,0:T(8,128)(2,1)S(1)}, u32[]{:S(2)}, u32[]{:S(2)}) collective-permute-start(bf16[256,512]{1,0:T(8,128)(2,1)S(1)} %pad_maximum_fusion.1), channel_id=1, source_target_pairs={{0,32},{1,33},{2,34},{3,35},{4,36},{5,37},{6,38},{7,39},{8,40},{9,... | collective-permute-start | bytes 786440 | tf_op jit(solution)/shard_map/ppermute | solution.py:31
  65.7 4.6 %collective-permute-done.22.refs_5_ = bf16[64,512]{1,0:T(8,128)(2,1)S(1)} collective-permute-done((bf16[64,512]{1,0:T(8,128)(2,1)S(1)}, bf16[64,512]{1,0:T(8,128)(2,1)S(1)}, u32[]{:S(2)}, u32[]{:S(2)}) %collective-permute-start.22) | collective-permute-done | bytes 65568 | tf_op jit(solution)/shard_map/ppermute | solution.py:31
  70.5 1.3 %collective-permute-start.26 = (bf16[256,512]{1,0:T(8,128)(2,1)S(1)}, bf16[256,512]{1,0:T(8,128)(2,1)S(1)}, u32[]{:S(2)}, u32[]{:S(2)}) collective-permute-start(bf16[256,512]{1,0:T(8,128)(2,1)S(1)} %get-tuple-element.86), channel_id=1, source_target_pairs={{0,32},{1,33},{2,34},{3,35},{4,36},{5,37},{6,38},{7,39},{8,40},{9,... | collective-permute-start | bytes 786440 | tf_op jit(solution)/shard_map/ppermute | solution.py:31
  71.8 1.0 collective-permute-start.27
  72.8 1.8 %collective-permute-start.23 = (bf16[64,512]{1,0:T(8,128)(2,1)S(1)}, bf16[64,512]{1,0:T(8,128)(2,1)S(1)}, u32[]{:S(2)}, u32[]{:S(2)}) collective-permute-start(bf16[64,512]{1,0:T(8,128)(2,1)S(1)} %get-tuple-element.81.refs_4_), channel_id=1, source_target_pairs={{0,8},{1,9},{2,10},{3,11},{4,12},{5,13},{6,14},{7,15},{8,0},{9,1},... | collective-permute-start | bytes 196616 | tf_op jit(solution)/shard_map/ppermute | solution.py:31
  74.6 1.3 %collective-permute-done.18.refs_1_ = bf16[256,512]{1,0:T(8,128)(2,1)S(1)} collective-permute-done((bf16[256,512]{1,0:T(8,128)(2,1)S(1)}, bf16[256,512]{1,0:T(8,128)(2,1)S(1)}, u32[]{:S(2)}, u32[]{:S(2)}) %collective-permute-start.18) | collective-permute-done | bytes 262176 | tf_op jit(solution)/shard_map/ppermute | solution.py:31
  75.8 1.4 %collective-permute-done.23.refs_5_ = bf16[64,512]{1,0:T(8,128)(2,1)S(1)} collective-permute-done((bf16[64,512]{1,0:T(8,128)(2,1)S(1)}, bf16[64,512]{1,0:T(8,128)(2,1)S(1)}, u32[]{:S(2)}, u32[]{:S(2)}) %collective-permute-start.23) | collective-permute-done | bytes 65568 | tf_op jit(solution)/shard_map/ppermute | solution.py:31
  77.4 2.6 %collective-permute-start.28 = (bf16[64,512]{1,0:T(8,128)(2,1)S(1)}, bf16[64,512]{1,0:T(8,128)(2,1)S(1)}, u32[]{:S(2)}, u32[]{:S(2)}) collective-permute-start(bf16[64,512]{1,0:T(8,128)(2,1)S(1)} %get-tuple-element.88.refs_3_), channel_id=1, source_target_pairs={{0,16},{1,17},{2,18},{3,19},{4,20},{5,21},{6,22},{7,23},{8,24},{9,... | collective-permute-start | bytes 196616 | tf_op jit(solution)/shard_map/ppermute | solution.py:31
  80.0 3.2 %collective-permute-done.28.refs_4_ = bf16[64,512]{1,0:T(8,128)(2,1)S(1)} collective-permute-done((bf16[64,512]{1,0:T(8,128)(2,1)S(1)}, bf16[64,512]{1,0:T(8,128)(2,1)S(1)}, u32[]{:S(2)}, u32[]{:S(2)}) %collective-permute-start.28) | collective-permute-done | bytes 65568 | tf_op jit(solution)/shard_map/ppermute | solution.py:31
  83.4 1.2 %collective-permute-start.29 = (bf16[64,512]{1,0:T(8,128)(2,1)S(1)}, bf16[64,512]{1,0:T(8,128)(2,1)S(1)}, u32[]{:S(2)}, u32[]{:S(2)}) collective-permute-start(bf16[64,512]{1,0:T(8,128)(2,1)S(1)} %get-tuple-element.89), channel_id=1, source_target_pairs={{0,4},{1,5},{2,6},{3,7},{4,0},{5,1},{6,2},{7,3},{8,12},{9,13},{10,... | collective-permute-start | bytes 196616 | tf_op jit(solution)/shard_map/ppermute | solution.py:31
  84.6 2.0 %collective-permute-start.24 = (bf16[256,512]{1,0:T(8,128)(2,1)S(1)}, bf16[256,512]{1,0:T(8,128)(2,1)S(1)}, u32[]{:S(2)}, u32[]{:S(2)}) collective-permute-start(bf16[256,512]{1,0:T(8,128)(2,1)S(1)} %get-tuple-element.82), channel_id=1, source_target_pairs={{0,32},{1,33},{2,34},{3,35},{4,36},{5,37},{6,38},{7,39},{8,40},{9,... | collective-permute-start | bytes 786440 | tf_op jit(solution)/shard_map/ppermute | solution.py:31
  86.6 2.6 %collective-permute-done.29 = bf16[64,512]{1,0:T(8,128)(2,1)S(1)} collective-permute-done((bf16[64,512]{1,0:T(8,128)(2,1)S(1)}, bf16[64,512]{1,0:T(8,128)(2,1)S(1)}, u32[]{:S(2)}, u32[]{:S(2)}) %collective-permute-start.29) | collective-permute-done | bytes 65568 | tf_op jit(solution)/shard_map/ppermute | solution.py:31
  89.3 1.7 %collective-permute-done.24.refs_1_ = bf16[256,512]{1,0:T(8,128)(2,1)S(1)} collective-permute-done((bf16[256,512]{1,0:T(8,128)(2,1)S(1)}, bf16[256,512]{1,0:T(8,128)(2,1)S(1)}, u32[]{:S(2)}, u32[]{:S(2)}) %collective-permute-start.24) | collective-permute-done | bytes 262176 | tf_op jit(solution)/shard_map/ppermute | solution.py:31
  91.0 2.9 %collective-permute-done.25.refs_3_ = bf16[256,512]{1,0:T(8,128)(2,1)S(1)} collective-permute-done((bf16[256,512]{1,0:T(8,128)(2,1)S(1)}, bf16[256,512]{1,0:T(8,128)(2,1)S(1)}, u32[]{:S(2)}, u32[]{:S(2)}) %collective-permute-start.25) | collective-permute-done | bytes 262176 | tf_op jit(solution)/shard_map/ppermute | solution.py:31
  94.1 2.1 %collective-permute-start.32 = (bf16[256,512]{1,0:T(8,128)(2,1)S(1)}, bf16[256,512]{1,0:T(8,128)(2,1)S(1)}, u32[]{:S(2)}, u32[]{:S(2)}) collective-permute-start(bf16[256,512]{1,0:T(8,128)(2,1)S(1)} %get-tuple-element.92), channel_id=1, source_target_pairs={{0,16},{1,17},{2,18},{3,19},{4,20},{5,21},{6,22},{7,23},{8,24},{9,... | collective-permute-start | bytes 786440 | tf_op jit(solution)/shard_map/ppermute | solution.py:31
  96.2 4.3 %collective-permute-start.30 = (bf16[256,512]{1,0:T(8,128)(2,1)S(1)}, bf16[256,512]{1,0:T(8,128)(2,1)S(1)}, u32[]{:S(2)}, u32[]{:S(2)}) collective-permute-start(bf16[256,512]{1,0:T(8,128)(2,1)S(1)} %get-tuple-element.90), channel_id=1, source_target_pairs={{0,32},{1,33},{2,34},{3,35},{4,36},{5,37},{6,38},{7,39},{8,40},{9,... | collective-permute-start | bytes 786440 | tf_op jit(solution)/shard_map/ppermute | solution.py:31
  100.7 1.4 %collective-permute-done.32.refs_3_ = bf16[256,512]{1,0:T(8,128)(2,1)S(1)} collective-permute-done((bf16[256,512]{1,0:T(8,128)(2,1)S(1)}, bf16[256,512]{1,0:T(8,128)(2,1)S(1)}, u32[]{:S(2)}, u32[]{:S(2)}) %collective-permute-start.32) | collective-permute-done | bytes 262176 | tf_op jit(solution)/shard_map/ppermute | solution.py:31
  102.1 2.3 %collective-permute-done.30.refs_1_ = bf16[256,512]{1,0:T(8,128)(2,1)S(1)} collective-permute-done((bf16[256,512]{1,0:T(8,128)(2,1)S(1)}, bf16[256,512]{1,0:T(8,128)(2,1)S(1)}, u32[]{:S(2)}, u32[]{:S(2)}) %collective-permute-start.30) | collective-permute-done | bytes 262176 | tf_op jit(solution)/shard_map/ppermute | solution.py:31
  104.4 2.5 %collective-permute-done.31.refs_2_ = bf16[256,512]{1,0:T(8,128)(2,1)S(1)} collective-permute-done((bf16[256,512]{1,0:T(8,128)(2,1)S(1)}, bf16[256,512]{1,0:T(8,128)(2,1)S(1)}, u32[]{:S(2)}, u32[]{:S(2)}) %collective-permute-start.31) | collective-permute-done | bytes 262176 | tf_op jit(solution)/shard_map/ppermute | solution.py:31
  106.9 0.8 s8_.1
  107.8 1.1 %maximum_convert_fusion = f32[512,512]{1,0:T(8,128)} fusion(bf16[256,512]{1,0:T(8,128)(2,1)S(1)} %get-tuple-element.98, bf16[256,512]{1,0:T(8,128)(2,1)S(1)} %get-tuple-element.97), kind=kLoop, calls=%fused_computation.2 | loop fusion | flops 1048576 | bytes 1572864 | tf_op jit(solution)/shard_map/convert_element_type | solution.py:305
  (63 shorter events, 5.0 us)
Async XLA Ops:
  0.6 1.0 copy-start
  3.1 9.9 %collective-permute-start.4 = (bf16[256,512]{1,0:T(8,128)(2,1)S(1)}, bf16[256,512]{1,0:T(8,128)(2,1)S(1)}, u32[]{:S(2)}, u32[]{:S(2)}) collective-permute-start(bf16[256,512]{1,0:T(8,128)(2,1)S(1)} %convolution_convert_fusion), channel_id=1, source_target_pairs={{0,8},{1,9},{2,10},{3,11},{16,24},{17,25},{18,26},{19,27},{32,40},... | collective-permute-start | bytes 786440 | tf_op jit(solution)/shard_map/ppermute | solution.py:31
  4.4 6.1 %collective-permute-start.1 = (bf16[256,512]{1,0:T(8,128)(2,1)S(1)}, bf16[256,512]{1,0:T(8,128)(2,1)S(1)}, u32[]{:S(2)}, u32[]{:S(2)}) collective-permute-start(bf16[256,512]{1,0:T(8,128)(2,1)S(1)} %convolution_convert_fusion), channel_id=1, source_target_pairs={{0,6},{1,7},{2,4},{3,5},{16,22},{17,23},{18,20},{19,21},{32,38},{3... | collective-permute-start | bytes 786440 | tf_op jit(solution)/shard_map/ppermute | solution.py:31
  5.1 5.4 %collective-permute-start = (bf16[256,512]{1,0:T(8,128)(2,1)S(1)}, bf16[256,512]{1,0:T(8,128)(2,1)S(1)}, u32[]{:S(2)}, u32[]{:S(2)}) collective-permute-start(bf16[256,512]{1,0:T(8,128)(2,1)S(1)} %convolution_convert_fusion), channel_id=1, source_target_pairs={{0,2},{1,3},{2,0},{3,1},{16,18},{17,19},{18,16},{19,17},{32,34},{3... | collective-permute-start | bytes 786440 | tf_op jit(solution)/shard_map/ppermute | solution.py:31
  7.4 10.2 %collective-permute-start.8 = (bf16[256,512]{1,0:T(8,128)(2,1)S(1)}, bf16[256,512]{1,0:T(8,128)(2,1)S(1)}, u32[]{:S(2)}, u32[]{:S(2)}) collective-permute-start(bf16[256,512]{1,0:T(8,128)(2,1)S(1)} %dynamic-slice_convert_fusion), channel_id=1, source_target_pairs={{0,1},{1,0},{2,3},{3,2},{4,5},{5,4},{6,7},{7,6},{8,9},{9,8},{10,11... | collective-permute-start | bytes 786440 | tf_op jit(solution)/shard_map/ppermute | solution.py:31
  10.6 15.1 %collective-permute-start.3 = (bf16[256,512]{1,0:T(8,128)(2,1)S(1)}, bf16[256,512]{1,0:T(8,128)(2,1)S(1)}, u32[]{:S(2)}, u32[]{:S(2)}) collective-permute-start(bf16[256,512]{1,0:T(8,128)(2,1)S(1)} %broadcast_select_fusion.2), channel_id=1, source_target_pairs={{0,8},{1,9},{2,10},{3,11},{4,12},{5,13},{6,14},{7,15},{16,24},{17,... | collective-permute-start | bytes 786440 | tf_op jit(solution)/shard_map/ppermute | solution.py:31
  11.9 12.3 %collective-permute-start.2 = (bf16[256,512]{1,0:T(8,128)(2,1)S(1)}, bf16[256,512]{1,0:T(8,128)(2,1)S(1)}, u32[]{:S(2)}, u32[]{:S(2)}) collective-permute-start(bf16[256,512]{1,0:T(8,128)(2,1)S(1)} %collective-permute-done.1), channel_id=1, source_target_pairs={{4,6},{5,7},{6,4},{7,5},{20,22},{21,23},{22,20},{23,21},{36,38},{3... | collective-permute-start | bytes 786440 | tf_op jit(solution)/shard_map/ppermute | solution.py:31
  13.1 11.1 %collective-permute-start.5 = (bf16[256,512]{1,0:T(8,128)(2,1)S(1)}, bf16[256,512]{1,0:T(8,128)(2,1)S(1)}, u32[]{:S(2)}, u32[]{:S(2)}) collective-permute-start(bf16[256,512]{1,0:T(8,128)(2,1)S(1)} %collective-permute-done.4), channel_id=1, source_target_pairs={{8,12},{9,13},{10,14},{11,15},{24,28},{25,29},{26,30},{27,31},{40,... | collective-permute-start | bytes 786440 | tf_op jit(solution)/shard_map/ppermute | solution.py:31
  17.7 9.5 %collective-permute-start.9 = (bf16[128,512]{1,0:T(8,128)(2,1)S(1)}, bf16[128,512]{1,0:T(8,128)(2,1)S(1)}, u32[]{:S(2)}, u32[]{:S(2)}) collective-permute-start(bf16[128,512]{1,0:T(8,128)(2,1)S(1)} %dynamic-slice_convert_fusion.1), channel_id=1, source_target_pairs={{0,2},{1,3},{2,0},{3,1},{4,6},{5,7},{6,4},{7,5},{8,10},{9,11},{10,... | collective-permute-start | bytes 393224 | tf_op jit(solution)/shard_map/ppermute | solution.py:31
  25.8 4.8 %copy-start.1 = (bf16[1,1,4,24,128,128]{5,4,3,2,1,0:T(8,128)(2,1)S(1)}, bf16[1,1,4,24,128,128]{5,4,3,2,1,0:T(8,128)(2,1)}, u32[]{:S(2)}) copy-start(bf16[1,1,4,24,128,128]{5,4,3,2,1,0:T(8,128)(2,1)} %param.13) | copy-start | bytes 9437188
  25.8 4.8 %copy-start.2 = (s32[32,8]{1,0:T(8,128)S(1)}, s32[32,8]{1,0:T(8,128)}, u32[]{:S(2)}) copy-start(s32[32,8]{1,0:T(8,128)} %get-tuple-element.48.list_ref) | copy-start | bytes 3076
  25.8 4.8 %copy-start.3 = (s32[32]{0:T(128)S(1)}, s32[32]{0:T(128)}, u32[]{:S(2)}) copy-start(s32[32]{0:T(128)} %get-tuple-element.49.filled_ref) | copy-start | bytes 388
  25.9 1.6 %collective-permute-start.6 = (bf16[256,512]{1,0:T(8,128)(2,1)S(1)}, bf16[256,512]{1,0:T(8,128)(2,1)S(1)}, u32[]{:S(2)}, u32[]{:S(2)}) collective-permute-start(bf16[256,512]{1,0:T(8,128)(2,1)S(1)} %broadcast_select_fusion.4.refs_0_), channel_id=1, source_target_pairs={{0,1},{1,0},{2,3},{3,2},{4,5},{5,4},{6,7},{7,6},{8,9},{9,8},{10,11... | collective-permute-start | bytes 786440 | tf_op jit(solution)/shard_map/ppermute | solution.py:31
  26.0 1.9 %collective-permute-start.7 = (bf16[256,512]{1,0:T(8,128)(2,1)S(1)}, bf16[256,512]{1,0:T(8,128)(2,1)S(1)}, u32[]{:S(2)}, u32[]{:S(2)}) collective-permute-start(bf16[256,512]{1,0:T(8,128)(2,1)S(1)} %get-tuple-element.94.refs_1_), channel_id=1, source_target_pairs={{0,1},{1,0},{2,3},{3,2},{4,5},{5,4},{6,7},{7,6},{8,9},{9,8},{10,11... | collective-permute-start | bytes 786440 | tf_op jit(solution)/shard_map/ppermute | solution.py:31
  27.9 15.7 %collective-permute-start.11 = (bf16[64,512]{1,0:T(8,128)(2,1)S(1)}, bf16[64,512]{1,0:T(8,128)(2,1)S(1)}, u32[]{:S(2)}, u32[]{:S(2)}) collective-permute-start(bf16[64,512]{1,0:T(8,128)(2,1)S(1)} %get-tuple-element.61), channel_id=1, source_target_pairs={{0,4},{1,5},{2,6},{3,7},{4,0},{5,1},{6,2},{7,3},{8,12},{9,13},{10,... | collective-permute-start | bytes 196616 | tf_op jit(solution)/shard_map/ppermute | solution.py:31
  32.7 10.9 %collective-permute-start.10 = (bf16[256,512]{1,0:T(8,128)(2,1)S(1)}, bf16[256,512]{1,0:T(8,128)(2,1)S(1)}, u32[]{:S(2)}, u32[]{:S(2)}) collective-permute-start(bf16[256,512]{1,0:T(8,128)(2,1)S(1)} %get-tuple-element.60), channel_id=1, source_target_pairs={{0,16},{1,17},{2,18},{3,19},{4,20},{5,21},{6,22},{7,23},{8,24},{9,... | collective-permute-start | bytes 786440 | tf_op jit(solution)/shard_map/ppermute | solution.py:31
  38.6 11.3 %collective-permute-start.14 = (bf16[256,512]{1,0:T(8,128)(2,1)S(1)}, bf16[256,512]{1,0:T(8,128)(2,1)S(1)}, u32[]{:S(2)}, u32[]{:S(2)}) collective-permute-start(bf16[256,512]{1,0:T(8,128)(2,1)S(1)} %get-tuple-element.66), channel_id=1, source_target_pairs={{0,32},{1,33},{2,34},{3,35},{4,36},{5,37},{6,38},{7,39},{8,40},{9,... | collective-permute-start | bytes 786440 | tf_op jit(solution)/shard_map/ppermute | solution.py:31
  43.6 8.8 %collective-permute-start.15 = (bf16[256,512]{1,0:T(8,128)(2,1)S(1)}, bf16[256,512]{1,0:T(8,128)(2,1)S(1)}, u32[]{:S(2)}, u32[]{:S(2)}) collective-permute-start(bf16[256,512]{1,0:T(8,128)(2,1)S(1)} %get-tuple-element.68), channel_id=1, source_target_pairs={{0,224},{1,225},{2,226},{3,227},{4,228},{5,229},{6,230},{7,231},{8... | collective-permute-start | bytes 786440 | tf_op jit(solution)/shard_map/ppermute | solution.py:31
  43.7 9.4 %collective-permute-start.16 = (bf16[64,512]{1,0:T(8,128)(2,1)S(1)}, bf16[64,512]{1,0:T(8,128)(2,1)S(1)}, u32[]{:S(2)}, u32[]{:S(2)}) collective-permute-start(bf16[64,512]{1,0:T(8,128)(2,1)S(1)} %get-tuple-element.69.refs_4_), channel_id=1, source_target_pairs={{0,32},{1,33},{2,34},{3,35},{4,36},{5,37},{6,38},{7,39},{8,40},{9,... | collective-permute-start | bytes 196616 | tf_op jit(solution)/shard_map/ppermute | solution.py:31
  45.8 10.0 %collective-permute-start.12 = (bf16[128,512]{1,0:T(8,128)(2,1)S(1)}, bf16[128,512]{1,0:T(8,128)(2,1)S(1)}, u32[]{:S(2)}, u32[]{:S(2)}) collective-permute-start(bf16[128,512]{1,0:T(8,128)(2,1)S(1)} %get-tuple-element.62), channel_id=1, source_target_pairs={{0,32},{1,33},{2,34},{3,35},{4,36},{5,37},{6,38},{7,39},{8,40},{9,... | collective-permute-start | bytes 393224 | tf_op jit(solution)/shard_map/ppermute | solution.py:31
  45.9 9.9 %collective-permute-start.13 = (bf16[128,512]{1,0:T(8,128)(2,1)S(1)}, bf16[128,512]{1,0:T(8,128)(2,1)S(1)}, u32[]{:S(2)}, u32[]{:S(2)}) collective-permute-start(bf16[128,512]{1,0:T(8,128)(2,1)S(1)} %get-tuple-element.64), channel_id=1, source_target_pairs={{0,224},{1,225},{2,226},{3,227},{4,228},{5,229},{6,230},{7,231},{8... | collective-permute-start | bytes 393224 | tf_op jit(solution)/shard_map/ppermute | solution.py:31
  53.2 6.0 %collective-permute-start.17 = (bf16[64,512]{1,0:T(8,128)(2,1)S(1)}, bf16[64,512]{1,0:T(8,128)(2,1)S(1)}, u32[]{:S(2)}, u32[]{:S(2)}) collective-permute-start(bf16[64,512]{1,0:T(8,128)(2,1)S(1)} %get-tuple-element.70.refs_4_), channel_id=1, source_target_pairs={{0,64},{1,65},{2,66},{3,67},{4,68},{5,69},{6,70},{7,71},{8,72},{9,... | collective-permute-start | bytes 196616 | tf_op jit(solution)/shard_map/ppermute | solution.py:31
  53.3 17.0 %collective-permute-start.20 = (bf16[256,512]{1,0:T(8,128)(2,1)S(1)}, bf16[256,512]{1,0:T(8,128)(2,1)S(1)}, u32[]{:S(2)}, u32[]{:S(2)}) collective-permute-start(bf16[256,512]{1,0:T(8,128)(2,1)S(1)} %get-tuple-element.77), channel_id=1, source_target_pairs={{0,32},{1,33},{2,34},{3,35},{4,36},{5,37},{6,38},{7,39},{8,40},{9,... | collective-permute-start | bytes 786440 | tf_op jit(solution)/shard_map/ppermute | solution.py:31
  54.5 15.9 %collective-permute-start.21 = (bf16[256,512]{1,0:T(8,128)(2,1)S(1)}, bf16[256,512]{1,0:T(8,128)(2,1)S(1)}, u32[]{:S(2)}, u32[]{:S(2)}) collective-permute-start(bf16[256,512]{1,0:T(8,128)(2,1)S(1)} %get-tuple-element.79), channel_id=1, source_target_pairs={{0,224},{1,225},{2,226},{3,227},{4,228},{5,229},{6,230},{7,231},{8... | collective-permute-start | bytes 786440 | tf_op jit(solution)/shard_map/ppermute | solution.py:31
  59.3 11.0 %collective-permute-start.22 = (bf16[64,512]{1,0:T(8,128)(2,1)S(1)}, bf16[64,512]{1,0:T(8,128)(2,1)S(1)}, u32[]{:S(2)}, u32[]{:S(2)}) collective-permute-start(bf16[64,512]{1,0:T(8,128)(2,1)S(1)} %get-tuple-element.80.refs_4_), channel_id=1, source_target_pairs={{0,128},{1,129},{2,130},{3,131},{4,132},{5,133},{6,134},{7,135},{8... | collective-permute-start | bytes 196616 | tf_op jit(solution)/shard_map/ppermute | solution.py:31
  63.5 11.1 %collective-permute-start.19 = (bf16[256,512]{1,0:T(8,128)(2,1)S(1)}, bf16[256,512]{1,0:T(8,128)(2,1)S(1)}, u32[]{:S(2)}, u32[]{:S(2)}) collective-permute-start(bf16[256,512]{1,0:T(8,128)(2,1)S(1)} %pad_maximum_fusion.2), channel_id=1, source_target_pairs={{0,224},{1,225},{2,226},{3,227},{4,228},{5,229},{6,230},{7,231},{8... | collective-permute-start | bytes 786440 | tf_op jit(solution)/shard_map/ppermute | solution.py:31
  64.5 11.4 %collective-permute-start.18 = (bf16[256,512]{1,0:T(8,128)(2,1)S(1)}, bf16[256,512]{1,0:T(8,128)(2,1)S(1)}, u32[]{:S(2)}, u32[]{:S(2)}) collective-permute-start(bf16[256,512]{1,0:T(8,128)(2,1)S(1)} %pad_maximum_fusion.1), channel_id=1, source_target_pairs={{0,32},{1,33},{2,34},{3,35},{4,36},{5,37},{6,38},{7,39},{8,40},{9,... | collective-permute-start | bytes 786440 | tf_op jit(solution)/shard_map/ppermute | solution.py:31
  70.5 12.8 %collective-permute-start.26 = (bf16[256,512]{1,0:T(8,128)(2,1)S(1)}, bf16[256,512]{1,0:T(8,128)(2,1)S(1)}, u32[]{:S(2)}, u32[]{:S(2)}) collective-permute-start(bf16[256,512]{1,0:T(8,128)(2,1)S(1)} %get-tuple-element.86), channel_id=1, source_target_pairs={{0,32},{1,33},{2,34},{3,35},{4,36},{5,37},{6,38},{7,39},{8,40},{9,... | collective-permute-start | bytes 786440 | tf_op jit(solution)/shard_map/ppermute | solution.py:31
  71.8 11.5 %collective-permute-start.27 = (bf16[256,512]{1,0:T(8,128)(2,1)S(1)}, bf16[256,512]{1,0:T(8,128)(2,1)S(1)}, u32[]{:S(2)}, u32[]{:S(2)}) collective-permute-start(bf16[256,512]{1,0:T(8,128)(2,1)S(1)} %get-tuple-element.87), channel_id=1, source_target_pairs={{0,224},{1,225},{2,226},{3,227},{4,228},{5,229},{6,230},{7,231},{8... | collective-permute-start | bytes 786440 | tf_op jit(solution)/shard_map/ppermute | solution.py:31
  72.8 4.5 %collective-permute-start.23 = (bf16[64,512]{1,0:T(8,128)(2,1)S(1)}, bf16[64,512]{1,0:T(8,128)(2,1)S(1)}, u32[]{:S(2)}, u32[]{:S(2)}) collective-permute-start(bf16[64,512]{1,0:T(8,128)(2,1)S(1)} %get-tuple-element.81.refs_4_), channel_id=1, source_target_pairs={{0,8},{1,9},{2,10},{3,11},{4,12},{5,13},{6,14},{7,15},{8,0},{9,1},... | collective-permute-start | bytes 196616 | tf_op jit(solution)/shard_map/ppermute | solution.py:31
  77.4 5.9 %collective-permute-start.28 = (bf16[64,512]{1,0:T(8,128)(2,1)S(1)}, bf16[64,512]{1,0:T(8,128)(2,1)S(1)}, u32[]{:S(2)}, u32[]{:S(2)}) collective-permute-start(bf16[64,512]{1,0:T(8,128)(2,1)S(1)} %get-tuple-element.88.refs_3_), channel_id=1, source_target_pairs={{0,16},{1,17},{2,18},{3,19},{4,20},{5,21},{6,22},{7,23},{8,24},{9,... | collective-permute-start | bytes 196616 | tf_op jit(solution)/shard_map/ppermute | solution.py:31
  83.4 5.9 %collective-permute-start.29 = (bf16[64,512]{1,0:T(8,128)(2,1)S(1)}, bf16[64,512]{1,0:T(8,128)(2,1)S(1)}, u32[]{:S(2)}, u32[]{:S(2)}) collective-permute-start(bf16[64,512]{1,0:T(8,128)(2,1)S(1)} %get-tuple-element.89), channel_id=1, source_target_pairs={{0,4},{1,5},{2,6},{3,7},{4,0},{5,1},{6,2},{7,3},{8,12},{9,13},{10,... | collective-permute-start | bytes 196616 | tf_op jit(solution)/shard_map/ppermute | solution.py:31
  84.6 6.4 %collective-permute-start.24 = (bf16[256,512]{1,0:T(8,128)(2,1)S(1)}, bf16[256,512]{1,0:T(8,128)(2,1)S(1)}, u32[]{:S(2)}, u32[]{:S(2)}) collective-permute-start(bf16[256,512]{1,0:T(8,128)(2,1)S(1)} %get-tuple-element.82), channel_id=1, source_target_pairs={{0,32},{1,33},{2,34},{3,35},{4,36},{5,37},{6,38},{7,39},{8,40},{9,... | collective-permute-start | bytes 786440 | tf_op jit(solution)/shard_map/ppermute | solution.py:31
  86.6 7.3 %collective-permute-start.25 = (bf16[256,512]{1,0:T(8,128)(2,1)S(1)}, bf16[256,512]{1,0:T(8,128)(2,1)S(1)}, u32[]{:S(2)}, u32[]{:S(2)}) collective-permute-start(bf16[256,512]{1,0:T(8,128)(2,1)S(1)} %get-tuple-element.84), channel_id=1, source_target_pairs={{0,224},{1,225},{2,226},{3,227},{4,228},{5,229},{6,230},{7,231},{8... | collective-permute-start | bytes 786440 | tf_op jit(solution)/shard_map/ppermute | solution.py:31
  94.0 6.5 %collective-permute-start.33 = (bf16[128,512]{1,0:T(8,128)(2,1)S(1)}, bf16[128,512]{1,0:T(8,128)(2,1)S(1)}, u32[]{:S(2)}, u32[]{:S(2)}) collective-permute-start(bf16[128,512]{1,0:T(8,128)(2,1)S(1)} %get-tuple-element.93), channel_id=1, source_target_pairs={{0,2},{1,3},{2,0},{3,1},{4,6},{5,7},{6,4},{7,5},{8,10},{9,11},{10,... | collective-permute-start | bytes 393224 | tf_op jit(solution)/shard_map/ppermute | solution.py:31
  94.1 8.0 %collective-permute-start.32 = (bf16[256,512]{1,0:T(8,128)(2,1)S(1)}, bf16[256,512]{1,0:T(8,128)(2,1)S(1)}, u32[]{:S(2)}, u32[]{:S(2)}) collective-permute-start(bf16[256,512]{1,0:T(8,128)(2,1)S(1)} %get-tuple-element.92), channel_id=1, source_target_pairs={{0,16},{1,17},{2,18},{3,19},{4,20},{5,21},{6,22},{7,23},{8,24},{9,... | collective-permute-start | bytes 786440 | tf_op jit(solution)/shard_map/ppermute | solution.py:31
  96.2 8.2 %collective-permute-start.30 = (bf16[256,512]{1,0:T(8,128)(2,1)S(1)}, bf16[256,512]{1,0:T(8,128)(2,1)S(1)}, u32[]{:S(2)}, u32[]{:S(2)}) collective-permute-start(bf16[256,512]{1,0:T(8,128)(2,1)S(1)} %get-tuple-element.90), channel_id=1, source_target_pairs={{0,32},{1,33},{2,34},{3,35},{4,36},{5,37},{6,38},{7,39},{8,40},{9,... | collective-permute-start | bytes 786440 | tf_op jit(solution)/shard_map/ppermute | solution.py:31
  100.5 6.4 %collective-permute-start.31 = (bf16[256,512]{1,0:T(8,128)(2,1)S(1)}, bf16[256,512]{1,0:T(8,128)(2,1)S(1)}, u32[]{:S(2)}, u32[]{:S(2)}) collective-permute-start(bf16[256,512]{1,0:T(8,128)(2,1)S(1)} %get-tuple-element.91), channel_id=1, source_target_pairs={{0,224},{1,225},{2,226},{3,227},{4,228},{5,229},{6,230},{7,231},{8... | collective-permute-start | bytes 786440 | tf_op jit(solution)/shard_map/ppermute | solution.py:31
  100.6 7.1 %collective-permute-start.34 = (bf16[256,512]{1,0:T(8,128)(2,1)S(1)}, bf16[256,512]{1,0:T(8,128)(2,1)S(1)}, u32[]{:S(2)}, u32[]{:S(2)}) collective-permute-start(bf16[256,512]{1,0:T(8,128)(2,1)S(1)} %pad_maximum_fusion.3), channel_id=1, source_target_pairs={{0,1},{1,0},{2,3},{3,2},{4,5},{5,4},{6,7},{7,6},{8,9},{9,8},{10,11... | collective-permute-start | bytes 786440 | tf_op jit(solution)/shard_map/ppermute | solution.py:31

commit v3 on v0

v3 whole, which is shorter than its diff:
```python
import functools

import jax
import jax.numpy as jnp
from jax import lax
from jax.experimental import pallas as pl
from jax.experimental.pallas import tpu as pltpu
from jax.sharding import PartitionSpec as P

AXES = ("row", "rep")
X, Y, Z, C = 4, 4, 8, 2


def index_of(x, y, z, c):
    return (z * 2 + x // 2) * 16 + (x % 2) * 8 + y * 2 + c


def pairs(move):
    out = []
    for z in range(Z):
        for x in range(X):
            for y in range(Y):
                for c in range(C):
                    to = move(x, y, z, c)
                    if to is not None:
                        out.append((index_of(x, y, z, c), index_of(to[0] % X, to[1] % Y, to[2] % Z, to[3] % C)))
    return out


def send(value, move):
    return lax.ppermute(value, AXES, pairs(move))


def add(*terms):
    total = terms[0].astype(jnp.float32)
    for term in terms[1:]:
        total = total + term.astype(jnp.float32)
    return total


def narrow(value):
    return value.astype(jnp.bfloat16)


def across(x, y, z, c):
    return (x + 1, y, z, c) if x % 2 == 0 and y < 2 else None


def outward(x, y, z, c):
    return (x, 3 - y, z, c) if x % 2 == 0 and y < 2 else None


def swap(x, y, z, c):
    return (x, 1 - y, z, c) if x % 2 == 0 and y < 2 else None


def swap_rest(x, y, z, c):
    return (x, 5 - y, z, c) if x % 2 == 0 and y >= 2 else None


def across_all(x, y, z, c):
    return (x + 1, y, z, c) if x % 2 == 0 else None


def distant(x, y, z, c):
    return (x, y + 2, z, c) if x % 2 == 1 and y < 2 else None


FIRST = [(4, 1), (2, 1), (6, 1)]
SECOND = [(3, 1), (5, 1), (4, 0), (1, 1), (7, 1)]
THIRD = [(3, 0), (5, 0), (0, 1), (2, 0), (6, 0), (1, 0), (7, 0), (0, 0)]
SLOTS = 96


COUNT = 8
SPARE = 32


def plan_kernel(src_ref, dst_ref, count_ref, order_ref, given_ref, table_ref, passed_ref):
    row = lax.axis_index("row")
    z, xh, core = row // 2, lax.rem(row, 2), lax.rem(lax.axis_index("rep"), 2)
    for i in range(SPARE + 1):
        table_ref[i, COUNT] = 0
    for section in range(4):
        slot = jnp.where(core == section % 2, section // 2, 2 + section // 2)
        live = count_ref[section]

        def step(t, carry):
            d = dst_ref[section, t]
            rel = ((d >> 2) - z) & 7
            half = ((d >> 1) + xh) & 1
            at = jnp.where(t < live, order_ref[rel * 2 + half] * 2 + (d & 1), SPARE)
            n = table_ref[at, COUNT]
            table_ref[at, n & 7] = (section * 24 + t) * 8 + slot * 2 + src_ref[section, t]
            table_ref[at, COUNT] = n + 1
            return carry

        lax.fori_loop(0, 24, step, 0, unroll=True)
    passed_ref[...] = given_ref[...]


def plan(src, dst, count, given):
    order = [0] * 16
    for i, (rel, half) in enumerate(FIRST + SECOND + THIRD):
        order[rel * 2 + half] = i
    smem, vmem = pl.BlockSpec(memory_space=pltpu.SMEM), pl.BlockSpec(memory_space=pltpu.VMEM)
    return pl.pallas_call(
        plan_kernel,
        out_shape=[jax.ShapeDtypeStruct((SPARE + 1, 16), jnp.int32), jax.ShapeDtypeStruct(given.shape, given.dtype)],
        in_specs=[smem] * 4 + [vmem],
        out_specs=[smem, vmem],
        compiler_params=pltpu.CompilerParams(vmem_limit_bytes=10 * 1024 * 1024),
        name="plan",
    )(src, dst, count, jnp.array(order, jnp.int32), given)


def rows_kernel(base, sizes, table_ref, tiles_ref, sources_ref, *rest):
    outs, acc = rest[: len(sizes)], rest[len(sizes)]

    def pair(at, p, n):
        one = table_ref[at, 2 * p]
        paired = 2 * p + 1 < n
        two = jnp.where(paired, table_ref[at, 2 * p + 1], 0)
        second = tiles_ref[two // 8]
        left = jnp.concatenate([tiles_ref[one // 8], jnp.where(paired, second, jnp.zeros_like(second))], axis=0)
        right = jnp.concatenate([sources_ref[lax.rem(one, 8)], sources_ref[lax.rem(two, 8)]], axis=0)
        return lax.dot_general(left, right, (((0,), (0,)), ((), ())), preferred_element_type=jnp.float32)

    for g, size in enumerate(sizes):
        first = base + 2 * sum(sizes[:g])

        def block(j, carry):
            at = first + j
            n = table_ref[at, COUNT]
            out = outs[g].at[pl.ds(pl.multiple_of(j * 128, 128), 128), :]

            @pl.when(n == 0)
            def _():
                out[...] = jnp.zeros((128, 512), jnp.bfloat16)

            @pl.when(n > 0)
            def _():
                acc[...] = pair(at, 0, n)

                def more(p, c):
                    acc[...] += pair(at, p, n)
                    return c

                lax.fori_loop(1, (n + 1) // 2, more, 0)
                out[...] = acc[...].astype(jnp.bfloat16)

            return carry

        lax.fori_loop(0, 2 * size, block, 0)


def rows(base, sizes, table, tiles, sources, name):
    smem = pl.BlockSpec(memory_space=pltpu.SMEM)
    vmem = pl.BlockSpec(memory_space=pltpu.VMEM)
    return pl.pallas_call(
        functools.partial(rows_kernel, base, tuple(sizes)),
        out_shape=[jax.ShapeDtypeStruct((256 * size, 512), jnp.bfloat16) for size in sizes],
        in_specs=[smem, vmem, vmem],
        out_specs=[vmem] * len(sizes),
        scratch_shapes=[pltpu.VMEM((128, 512), jnp.float32)],
        compiler_params=pltpu.CompilerParams(vmem_limit_bytes=10 * 1024 * 1024),
        cost_estimate=pl.CostEstimate(flops=sum(sizes) * 400_000_000, bytes_accessed=1_000_000, transcendentals=0),
        name=name,
    )(table, tiles, sources)


def stage_kernel(plans, n_in, n_anchors, *refs):
    ins, outs = refs[:n_in], refs[n_in + n_anchors :]
    for out, segments in zip(outs, plans):
        at = 0
        for count, terms in segments:
            values = [ins[i][pl.ds(start, count), :].astype(jnp.float32) for i, start in terms]
            while len(values) > 1:
                values = [sum(values[i : i + 2]) for i in range(0, len(values), 2)]
            out[pl.ds(at, count), :] = values[0].astype(out.dtype)
            at += count


def stage(name, *outputs, anchors=()):
    arrays, plans, shapes = [], [], []
    for segments in outputs:
        planned = []
        for count, *terms in segments:
            numbered = []
            for term in terms:
                value, start = term if isinstance(term, tuple) else (term, 0)
                place = next((i for i, known in enumerate(arrays) if known is value), None)
                if place is None:
                    place = len(arrays)
                    arrays.append(value)
                numbered.append((place, start))
            planned.append((count, tuple(numbered)))
        plans.append(tuple(planned))
        shapes.append(jax.ShapeDtypeStruct((sum(count for count, _ in planned), 512), jnp.bfloat16))
    vmem, anywhere = pl.BlockSpec(memory_space=pltpu.VMEM), pl.BlockSpec(memory_space=pl.ANY)
    return pl.pallas_call(
        functools.partial(stage_kernel, tuple(plans), len(arrays), len(anchors)),
        out_shape=shapes,
        in_specs=[vmem] * len(arrays) + [anywhere if anchor.dtype == jnp.int32 else vmem for anchor in anchors],
        out_specs=[vmem] * len(shapes),
        compiler_params=pltpu.CompilerParams(vmem_limit_bytes=6 * 1024 * 1024),
        cost_estimate=pl.CostEstimate(flops=1000, bytes_accessed=1000, transcendentals=0),
        name=name,
    )(*arrays, *anchors)


def up(x, y, z, c):
    return (x, y, z + 1, c)


def down(x, y, z, c):
    return (x, y, z - 1, c)


def halves(value, bit):
    rows = value.shape[0] // 2
    kept = lax.dynamic_slice_in_dim(value, bit * rows, rows, 0)
    return kept, narrow(lax.dynamic_slice_in_dim(value, (1 - bit) * rows, rows, 0))


def joined(bit, value, got):
    return jnp.concatenate([jnp.where(bit == 0, value, got), jnp.where(bit == 0, got, value)])


def later(name, anchor, *terms):
    return stage(name, [(terms[0].shape[0], *terms)], anchors=(anchor,))[0]


def flipped(axis, step):
    def move(x, y, z, c):
        at = {"x": x, "y": y, "z": z, "c": c}
        at[axis] ^= step
        return at["x"], at["y"], at["z"], at["c"]

    return move


def local(grad_out, relu_mask, aggregated, weight, tile_values, tile_src, tile_dst, tile_count):
    rep = lax.axis_index("rep")
    x_lo, y, core = rep // 8, (rep // 2) % 4, rep % 2
    other, cross = flipped("c", 1), flipped("x", 2)
    tiles = tile_values.reshape(SLOTS, 128, 128)

    masked = jnp.where(relu_mask != 0, grad_out, jnp.zeros_like(grad_out))
    node_grad = lax.dot_general(
        masked, weight, (((1,), (1,)), ((), ())), preferred_element_type=jnp.float32
    ).astype(jnp.bfloat16)
    w = lax.dot_general(aggregated, masked, (((0,), (0,)), ((), ())), preferred_element_type=jnp.float32)
    kept, given = halves(w, core)
    by_x, by_y, swapped = send(node_grad, across), send(node_grad, outward), send(node_grad, swap)
    w = add(kept, send(given, other))
    kept, given = halves(w, y % 2)
    table, given = plan(tile_src[0, 0], tile_dst[0, 0], tile_count[0, 0], given)
    onward = jnp.where(y < 2, swapped, by_y)
    by_x2, by_far, by_swap = send(onward, across_all), send(by_x, distant), send(by_y, swap_rest)
    w = add(kept, send(given, flipped("y", 1)))
    first = jnp.where(x_lo == 0, jnp.where(y < 2, node_grad, by_y), jnp.where(y < 2, by_x, by_x2))
    second = jnp.where(x_lo == 0, jnp.where(y < 2, swapped, by_swap), jnp.where(y < 2, by_x2, by_far))
    flip = jnp.logical_or(y == 1, y == 2)
    even, odd = jnp.where(flip, second, first), jnp.where(flip, first, second)

    even2, odd2 = send(even, other), send(odd, other)
    w = narrow(w)
    w_got = send(w, flipped("z", 1))
    sources, w = stage(
        "s0", [(256, even), (256, odd), (256, even2), (256, odd2)], [(128, w, w_got)]
    )
    sources = sources.reshape(8, 128, 512)

    t4, t2, t6 = rows(0, [1, 1, 1], table, tiles, sources, "rows_first")
    x4, up_got, down_got = send(t4, cross), send(t2, up), send(t6, down)
    kept, given = halves(w, y // 2)
    w_got = send(given, flipped("y", 2))
    t35, m4, t1, t7 = rows(6, [2, 1, 1, 1], table, tiles, sources, "rows_second")
    to_up, to_down, t35, w = stage(
        "s1",
        [(256, t1, up_got), (128, m4, x4)],
        [(256, t7, down_got), (128, (m4, 128), (x4, 128))],
        [(512, t35)],
        [(64, kept, w_got)],
    )

    up_t, down_t, x35 = send(to_up, up), send(to_down, down), send(t35, cross)
    w = narrow(add(w, send(w, flipped("z", 2))))
    w_got = send(w, flipped("z", 4))
    m3, m5, t0, m2, m6, m1, m7, m0 = rows(16, [1] * 8, table, tiles, sources, "rows_third")
    to_up, to_down, w = stage(
        "s2",
        [(128, m3, x35, (up_t, 256)), (128, (m3, 128), (x35, 128))],
        [(128, m5, (x35, 256)), (128, (m5, 128), (x35, 384), (down_t, 256))],
        [(64, w, w_got)],
    )

    up_got, down_got = send(to_up, up), send(to_down, down)
    w_got = [send(w, flipped("x", step)) for step in (1, 2, 3)]
    to_up, to_down, w = stage("s3", [(256, m2, up_got)], [(256, m6, down_got)], [(64, w, *w_got)])

    up_got, down_got = send(to_up, up), send(to_down, down)
    w_got = [send(w, flipped("y", step)) for step in (1, 2, 3)]
    to_up, to_down, crossing = stage(
        "s4", [(256, m1, up_got)], [(256, m7, down_got)], [(256, t0, up_t, down_t)]
    )
    w = stage("v5", *[[(64, piece)] for piece in (w, *w_got)], anchors=(to_up,))
    w = joined(y % 2, joined(y // 2, w[0], w[2]), joined(y // 2, w[1], w[3]))

    up_got, down_got, crossed = send(to_up, up), send(to_down, down), send(crossing, cross)
    w_got = send(w, other)
    (input_grad,) = stage("s5", [(256, m0, up_got, down_got, crossed)])
    return (input_grad, joined(core, w, w_got).astype(jnp.float32))


def solution(mesh):
    in_specs = (
        P(("row", "rep"), None),
        P(("row", "rep"), None),
        P(("row", "rep"), None),
        P(),
        P("row", "rep", None, None, None, None),
        P("row", "rep", None, None),
        P("row", "rep", None, None),
        P("row", "rep", None),
    )
    out_specs = (P(("row", "rep"), None), P())
    return jax.shard_map(local, mesh=mesh, in_specs=in_specs, out_specs=out_specs, check_vma=False)
```

time: 626 us -> 108 us (0.17)
  waiting for transfers between devices: 475 us -> 33.9 us
  other arithmetic: 64.8 us -> 2.56 us
  starting transfers between devices: 0.12 us -> 50.3 us
  local copies, waits for them, and re-layouts: 46.1 us -> 2.99 us
  matrix products: 24.2 us -> 3 us
  Pallas kernels: 0 us -> 13.5 us
  between operations: 13.9 us -> 1.14 us
    psum x2 -> x0, waiting for transfers between devices: 263 us -> none  [the longest x1 140 us: local(): weight_grad = lax.psum(local_wgrad, ('row', 'rep'))]
    reduce_scatter x1 -> x0, waiting for transfers between devices: 212 us -> none  [local(): lax.psum_scatter(sent, 'row', scatter_dimension=0, tiled=True)]
    scatter-add x4 -> x0, other arithmetic: 56.3 us -> none  [padded_tiles(): return partial_value.at[targets].add(products * alive_mask[:, None, None])]
    ppermute x0 -> x34, starting transfers between devices: none -> 50.3 us  [send(): return lax.ppermute(value, AXES, pairs(move))]
    ppermute x0 -> x34, waiting for transfers between devices: none -> 33.9 us  [send(): return lax.ppermute(value, AXES, pairs(move))]
    mul x4 -> x0, local copies, waits for them, and re-layouts: 26.4 us -> none  [padded_tiles(): return partial_value.at[targets].add(products * alive_mask[:, None, None])]
    dot_general x4 -> x0, matrix products: 20.4 us -> none  [padded_tiles(): jnp.einsum('tab,taf->tbf', tile_vals, gathered, preferred_element_type=jn...]
    pallas_call x0 -> x11, Pallas kernels: none -> 13.5 us  [the longest x3 8.65 us: rows(): pl.pallas_call(functools.partial(rows_kernel, base, tuple(sizes)), out_sh...]
  transfers between devices with their start and end apart: 3 -> 34, of which waited for: 3 -> 16; matrix products, arithmetic and copies ran while one was open for 21% -> 4% of each run, Pallas kernels for 0% -> 9%
where the time goes in v3:
time: 108 us; the launch traced here: 107 us
  starting transfers between devices  50.3 us (47%)
  waiting for transfers between devices  33.9 us (31%)
  Pallas kernels  13.5 us (12%)
  matrix products  3 us (3%)
  local copies, waits for them, and re-layouts  2.99 us (3%)
  other arithmetic  2.56 us (2%)
  between operations  1.14 us (1%)
    ppermute x34, starting transfers between devices, send(): return lax.ppermute(value, AXES, pairs(move))  50.3 us
    ppermute x34, waiting for transfers between devices, send(): return lax.ppermute(value, AXES, pairs(move))  33.9 us
    pallas_call x3, Pallas kernels, rows(): pl.pallas_call(functools.partial(rows_kernel, base, tuple(sizes)), out_sh...  8.65 us
    unnamed x16, local copies, waits for them, and re-layouts  2.91 us
    pallas_call x7, Pallas kernels, stage(): pl.pallas_call(functools.partial(stage_kernel, tuple(plans), len(arrays),...  2.42 us
    pallas_call x1, Pallas kernels, plan(): pl.pallas_call(plan_kernel, out_shape=[jax.ShapeDtypeStruct((SPARE + 1, 1...  2.4 us
  transfers between devices with their start and end apart: 34, of which 16 were waited for; matrix products, arithmetic and copies ran while one was open for 4% of the time, Pallas kernels for 9%

profile of v3, /device:TPU:2, one launch (start us, length us, event | category | flops | bytes accessed | tf_op | source)
XLA Modules:
  0.0 107.3 jit_solution(13180573684151945567)
XLA Ops:
  0.7 1.0 copy-done
  1.7 1.5 %convolution_convert_fusion = bf16[256,512]{1,0:T(8,128)(2,1)S(1)} fusion(bf16[512,512]{1,0:T(8,128)(2,1)S(1)} %copy-done, bf16[256,512]{1,0:T(8,128)(2,1)} %param.9, s32[256,512]{1,0:T(8,128)} %param.10), kind=kOutput, calls=%fused_computation | convolution fusion | flops 134610944 | bytes 1572864 | tf_op jit(solution)/shard_map/dot_general | solution.py:250
  3.2 1.3 %collective-permute-start.5 = (bf16[256,512]{1,0:T(8,128)(2,1)S(1)}, bf16[256,512]{1,0:T(8,128)(2,1)}, u32[]{:S(2)}, u32[]{:S(2)}) collective-permute-start(bf16[256,512]{1,0:T(8,128)(2,1)S(1)} %convolution_convert_fusion), channel_id=1, source_target_pairs={{0,8},{1,9},{2,10},{3,11},{16,24},{17,25},{18,26},{19,27},{32,40},... | collective-permute-start | bytes 786440 | tf_op jit(solution)/shard_map/ppermute | solution.py:31
  4.5 0.7 collective-permute-start.2
  5.1 0.7 collective-permute-start.1
  5.8 1.5 %fusion.1 = f32[512,512]{0,1:T(8,128)S(1)} fusion(bf16[256,512]{1,0:T(8,128)(2,1)} %param.11, bf16[256,512]{1,0:T(8,128)(2,1)} %param.9, s32[256,512]{1,0:T(8,128)} %param.10), kind=kOutput, calls=%fused_computation.27 | convolution fusion | flops 134479872 | bytes 2097152 | tf_op jit(solution)/shard_map/dot_general | solution.py:253
  7.7 1.3 %collective-permute-start.4 = (bf16[256,512]{1,0:T(8,128)(2,1)S(1)}, bf16[256,512]{1,0:T(8,128)(2,1)S(1)}, u32[]{:S(2)}, u32[]{:S(2)}) collective-permute-start(bf16[256,512]{1,0:T(8,128)(2,1)S(1)} %broadcast_select_fusion.2), channel_id=1, source_target_pairs={{0,8},{1,9},{2,10},{3,11},{4,12},{5,13},{6,14},{7,15},{16,24},{17,... | collective-permute-start | bytes 786440 | tf_op jit(solution)/shard_map/ppermute | solution.py:31
  9.0 0.7 collective-permute-start.3
  9.7 3.5 %collective-permute-done.5 = bf16[256,512]{1,0:T(8,128)(2,1)} collective-permute-done((bf16[256,512]{1,0:T(8,128)(2,1)S(1)}, bf16[256,512]{1,0:T(8,128)(2,1)}, u32[]{:S(2)}, u32[]{:S(2)}) %collective-permute-start.5) | collective-permute-done | bytes 262176 | tf_op jit(solution)/shard_map/ppermute | solution.py:31
  13.2 1.7 %collective-permute-start.6 = (bf16[256,512]{1,0:T(8,128)(2,1)}, bf16[256,512]{1,0:T(8,128)(2,1)S(1)}, u32[]{:S(2)}, u32[]{:S(2)}) collective-permute-start(bf16[256,512]{1,0:T(8,128)(2,1)} %collective-permute-done.5), channel_id=1, source_target_pairs={{8,12},{9,13},{10,14},{11,15},{24,28},{25,29},{26,30},{27,31},{40,... | collective-permute-start | bytes 786440 | tf_op jit(solution)/shard_map/ppermute | solution.py:31
  15.1 2.4 %plan.1 = (s32[33,16]{1,0:T(8,128)S(1)}, bf16[128,512]{1,0:T(8,128)(2,1)S(1)}) custom-call(s32[4,24]{1,0:T(4,128)S(1)} %bitcast.11, s32[4,24]{1,0:T(4,128)S(1)} %bitcast.12, s32[4]{0:T(128)S(1)} %bitcast.13, s32[16]{0:T(128)S(1)} %copy-done.4, bf16[128,512]{1,0:T(8,128)(2,1)S(1)} %dynamic-slice_convert_fusion.1.given_ref), custom_call_target="tpu_custom_call" | custom-call | tf_op jit(solution)/shard_map/plan/pallas_call | solution.py:107
  17.5 1.3 %collective-permute-start.9 = (bf16[128,512]{1,0:T(8,128)(2,1)S(1)}, bf16[128,512]{1,0:T(8,128)(2,1)S(1)}, u32[]{:S(2)}, u32[]{:S(2)}) collective-permute-start(bf16[128,512]{1,0:T(8,128)(2,1)S(1)} %get-tuple-element.39), channel_id=1, source_target_pairs={{0,2},{1,3},{2,0},{3,1},{4,6},{5,7},{6,4},{7,5},{8,10},{9,11},{10,... | collective-permute-start | bytes 393224 | tf_op jit(solution)/shard_map/ppermute | solution.py:31
  18.7 3.1 %collective-permute-done.6 = bf16[256,512]{1,0:T(8,128)(2,1)S(1)} collective-permute-done((bf16[256,512]{1,0:T(8,128)(2,1)}, bf16[256,512]{1,0:T(8,128)(2,1)S(1)}, u32[]{:S(2)}, u32[]{:S(2)}) %collective-permute-start.6) | collective-permute-done | bytes 262176 | tf_op jit(solution)/shard_map/ppermute | solution.py:31
  21.8 4.3 %collective-permute-done.4 = bf16[256,512]{1,0:T(8,128)(2,1)S(1)} collective-permute-done((bf16[256,512]{1,0:T(8,128)(2,1)S(1)}, bf16[256,512]{1,0:T(8,128)(2,1)S(1)}, u32[]{:S(2)}, u32[]{:S(2)}) %collective-permute-start.4) | collective-permute-done | bytes 262176 | tf_op jit(solution)/shard_map/ppermute | solution.py:31
  26.1 1.1 %broadcast_select_fusion.3 = (bf16[256,512]{1,0:T(8,128)(2,1)S(1)}, bf16[256,512]{1,0:T(8,128)(2,1)S(1)}, bf16[256,512]{1,0:T(8,128)(2,1)S(1)}) fusion(pred[]{:T(512)S(6)} %or.3, bf16[256,512]{1,0:T(8,128)(2,1)} %collective-permute-done.5, bf16[256,512]{1,0:T(8,128)(2,1)S(1)} %collective-permute-done.4, bf16[256,512]{1,0:T(8,128)(2,1)S(1)} %convolution_convert_fusion, ...), kind=kLoop, calls=%fused_computation.14 | loop fusion | flops 917504 | bytes 2621443 | tf_op jit(solution)/shard_map/jit(_where)/select_n | solution.py:265
  27.8 2.0 %collective-permute-start.10 = (bf16[128,512]{1,0:T(8,128)(2,1)S(1)}, bf16[128,512]{1,0:T(8,128)(2,1)S(1)}, u32[]{:S(2)}, u32[]{:S(2)}) collective-permute-start(bf16[128,512]{1,0:T(8,128)(2,1)S(1)} %add_convert_fusion.refs_4_), channel_id=1, source_target_pairs={{0,32},{1,33},{2,34},{3,35},{4,36},{5,37},{6,38},{7,39},{8,40},{9,... | collective-permute-start | bytes 393224 | tf_op jit(solution)/shard_map/ppermute | solution.py:31
  29.8 3.8 %collective-permute-done.10.refs_5_ = bf16[128,512]{1,0:T(8,128)(2,1)S(1)} collective-permute-done((bf16[128,512]{1,0:T(8,128)(2,1)S(1)}, bf16[128,512]{1,0:T(8,128)(2,1)S(1)}, u32[]{:S(2)}, u32[]{:S(2)}) %collective-permute-start.10) | collective-permute-done | bytes 131104 | tf_op jit(solution)/shard_map/ppermute | solution.py:31
  33.7 1.9 %copy-done.5 = bf16[1,1,4,24,128,128]{5,4,3,2,1,0:T(8,128)(2,1)S(1)} copy-done((bf16[1,1,4,24,128,128]{5,4,3,2,1,0:T(8,128)(2,1)S(1)}, bf16[1,1,4,24,128,128]{5,4,3,2,1,0:T(8,128)(2,1)}, u32[]{:S(2)}) %copy-start.5) | copy-done | bytes 3145752
  35.6 1.5 %rows_first.1 = (bf16[256,512]{1,0:T(8,128)(2,1)S(1)}, bf16[256,512]{1,0:T(8,128)(2,1)S(1)}, bf16[256,512]{1,0:T(8,128)(2,1)S(1)}) custom-call(s32[33,16]{1,0:T(8,128)S(1)} %get-tuple-element.38.table_ref, bf16[96,128,128]{2,1,0:T(8,128)(2,1)S(1)} %bitcast.14, bf16[8,128,512]{2,1,0:T(8,128)(2,1)S(1)} %bitcast.17), custom_call_target="tpu_custom_call" | custom-call | flops 1200000000 | bytes 1000000 | tf_op jit(solution)/shard_map/rows_first/pallas_call | solution.py:160
  37.1 2.5 %collective-permute-start.11 = (bf16[256,512]{1,0:T(8,128)(2,1)S(1)}, bf16[256,512]{1,0:T(8,128)(2,1)S(1)}, u32[]{:S(2)}, u32[]{:S(2)}) collective-permute-start(bf16[256,512]{1,0:T(8,128)(2,1)S(1)} %get-tuple-element.46), channel_id=1, source_target_pairs={{0,32},{1,33},{2,34},{3,35},{4,36},{5,37},{6,38},{7,39},{8,40},{9,... | collective-permute-start | bytes 786440 | tf_op jit(solution)/shard_map/ppermute | solution.py:31
  39.6 1.7 %collective-permute-start.12 = (bf16[256,512]{1,0:T(8,128)(2,1)S(1)}, bf16[256,512]{1,0:T(8,128)(2,1)S(1)}, u32[]{:S(2)}, u32[]{:S(2)}) collective-permute-start(bf16[256,512]{1,0:T(8,128)(2,1)S(1)} %get-tuple-element.48), channel_id=1, source_target_pairs={{0,16},{1,17},{2,18},{3,19},{4,20},{5,21},{6,22},{7,23},{8,24},{9,... | collective-permute-start | bytes 786440 | tf_op jit(solution)/shard_map/ppermute | solution.py:31
  41.3 4.7 %collective-permute-start.13 = (bf16[256,512]{1,0:T(8,128)(2,1)S(1)}, bf16[256,512]{1,0:T(8,128)(2,1)S(1)}, u32[]{:S(2)}, u32[]{:S(2)}) collective-permute-start(bf16[256,512]{1,0:T(8,128)(2,1)S(1)} %get-tuple-element.50), channel_id=1, source_target_pairs={{0,224},{1,225},{2,226},{3,227},{4,228},{5,229},{6,230},{7,231},{8... | collective-permute-start | bytes 786440 | tf_op jit(solution)/shard_map/ppermute | solution.py:31
  46.1 2.7 %rows_second.1 = (bf16[512,512]{1,0:T(8,128)(2,1)S(1)}, bf16[256,512]{1,0:T(8,128)(2,1)S(1)}, bf16[256,512]{1,0:T(8,128)(2,1)S(1)}, bf16[256,512]{1,0:T(8,128)(2,1)S(1)}) custom-call(s32[33,16]{1,0:T(8,128)S(1)} %get-tuple-element.38.table_ref, bf16[96,128,128]{2,1,0:T(8,128)(2,1)S(1)} %bitcast.15, bf16[8,128,512]{2,1,0:T(8,128)(2,1)S(1)} %bitcast.18), custom_call_target="tpu_custom_call" | custom-call | flops 2000000000 | bytes 1000000 | tf_op jit(solution)/shard_map/rows_second/pallas_call | solution.py:160
  48.9 3.0 %collective-permute-done.14.refs_8_ = bf16[64,512]{1,0:T(8,128)(2,1)S(1)} collective-permute-done((bf16[64,512]{1,0:T(8,128)(2,1)S(1)}, bf16[64,512]{1,0:T(8,128)(2,1)S(1)}, u32[]{:S(2)}, u32[]{:S(2)}) %collective-permute-start.14) | collective-permute-done | bytes 65568 | tf_op jit(solution)/shard_map/ppermute | solution.py:31
  52.1 1.5 %collective-permute-start.18 = (bf16[64,512]{1,0:T(8,128)(2,1)S(1)}, bf16[64,512]{1,0:T(8,128)(2,1)S(1)}, u32[]{:S(2)}, u32[]{:S(2)}) collective-permute-start(bf16[64,512]{1,0:T(8,128)(2,1)S(1)} %get-tuple-element.57), channel_id=1, source_target_pairs={{0,64},{1,65},{2,66},{3,67},{4,68},{5,69},{6,70},{7,71},{8,72},{9,... | collective-permute-start | bytes 196616 | tf_op jit(solution)/shard_map/ppermute | solution.py:31
  53.7 3.0 %collective-permute-start.16 = (bf16[384,512]{1,0:T(8,128)(2,1)S(1)}, bf16[384,512]{1,0:T(8,128)(2,1)S(1)}, u32[]{:S(2)}, u32[]{:S(2)}) collective-permute-start(bf16[384,512]{1,0:T(8,128)(2,1)S(1)} %get-tuple-element.54), channel_id=1, source_target_pairs={{0,32},{1,33},{2,34},{3,35},{4,36},{5,37},{6,38},{7,39},{8,40},{9,... | collective-permute-start | bytes 1179656 | tf_op jit(solution)/shard_map/ppermute | solution.py:31
  56.9 1.3 %collective-permute-start.15 = (bf16[512,512]{1,0:T(8,128)(2,1)S(1)}, bf16[512,512]{1,0:T(8,128)(2,1)S(1)}, u32[]{:S(2)}, u32[]{:S(2)}) collective-permute-start(bf16[512,512]{1,0:T(8,128)(2,1)S(1)} %get-tuple-element.53), channel_id=1, source_target_pairs={{0,16},{1,17},{2,18},{3,19},{4,20},{5,21},{6,22},{7,23},{8,24},{9,... | collective-permute-start | bytes 1572872 | tf_op jit(solution)/shard_map/ppermute | solution.py:31
  58.6 5.1 %collective-permute-start.19 = (bf16[64,512]{1,0:T(8,128)(2,1)S(1)}, bf16[64,512]{1,0:T(8,128)(2,1)S(1)}, u32[]{:S(2)}, u32[]{:S(2)}) collective-permute-start(bf16[64,512]{1,0:T(8,128)(2,1)S(1)} %add_convert_fusion.1.refs_5_), channel_id=1, source_target_pairs={{0,128},{1,129},{2,130},{3,131},{4,132},{5,133},{6,134},{7,135},{8... | collective-permute-start | bytes 196616 | tf_op jit(solution)/shard_map/ppermute | solution.py:31
  63.7 4.5 %rows_third.1 = (bf16[256,512]{1,0:T(8,128)(2,1)S(1)}, bf16[256,512]{1,0:T(8,128)(2,1)S(1)}, bf16[256,512]{1,0:T(8,128)(2,1)S(1)}, bf16[256,512]{1,0:T(8,128)(2,...) custom-call(s32[33,16]{1,0:T(8,128)S(1)} %get-tuple-element.38.table, ...), custom_call_target="tpu_custom_call" | custom-call | flops 3200000000 | bytes 1000000 | tf_op jit(solution)/shard_map/rows_third/pallas_call | solution.py:160
  68.3 0.7 collective-permute-done.15.refs_1_
  69.2 1.8 %collective-permute-start.20 = (bf16[256,512]{1,0:T(8,128)(2,1)S(1)}, bf16[256,512]{1,0:T(8,128)(2,1)S(1)}, u32[]{:S(2)}, u32[]{:S(2)}) collective-permute-start(bf16[256,512]{1,0:T(8,128)(2,1)S(1)} %get-tuple-element.58), channel_id=1, source_target_pairs={{0,32},{1,33},{2,34},{3,35},{4,36},{5,37},{6,38},{7,39},{8,40},{9,... | collective-permute-start | bytes 786440 | tf_op jit(solution)/shard_map/ppermute | solution.py:31
  71.0 1.5 %collective-permute-start.21 = (bf16[256,512]{1,0:T(8,128)(2,1)S(1)}, bf16[256,512]{1,0:T(8,128)(2,1)S(1)}, u32[]{:S(2)}, u32[]{:S(2)}) collective-permute-start(bf16[256,512]{1,0:T(8,128)(2,1)S(1)} %get-tuple-element.60), channel_id=1, source_target_pairs={{0,224},{1,225},{2,226},{3,227},{4,228},{5,229},{6,230},{7,231},{8... | collective-permute-start | bytes 786440 | tf_op jit(solution)/shard_map/ppermute | solution.py:31
  72.5 3.2 %collective-permute-start.23 = (bf16[64,512]{1,0:T(8,128)(2,1)S(1)}, bf16[64,512]{1,0:T(8,128)(2,1)S(1)}, u32[]{:S(2)}, u32[]{:S(2)}) collective-permute-start(bf16[64,512]{1,0:T(8,128)(2,1)S(1)} %get-tuple-element.61.refs_4_), channel_id=1, source_target_pairs={{0,16},{1,17},{2,18},{3,19},{4,20},{5,21},{6,22},{7,23},{8,24},{9,... | collective-permute-start | bytes 196616 | tf_op jit(solution)/shard_map/ppermute | solution.py:31
  75.6 0.9 collective-permute-start.22
  76.8 1.5 %collective-permute-done.23.refs_6_ = bf16[64,512]{1,0:T(8,128)(2,1)S(1)} collective-permute-done((bf16[64,512]{1,0:T(8,128)(2,1)S(1)}, bf16[64,512]{1,0:T(8,128)(2,1)S(1)}, u32[]{:S(2)}, u32[]{:S(2)}) %collective-permute-start.23) | collective-permute-done | bytes 65568 | tf_op jit(solution)/shard_map/ppermute | solution.py:31
  78.3 1.7 %collective-permute-done.22.refs_5_ = bf16[64,512]{1,0:T(8,128)(2,1)S(1)} collective-permute-done((bf16[64,512]{1,0:T(8,128)(2,1)S(1)}, bf16[64,512]{1,0:T(8,128)(2,1)S(1)}, u32[]{:S(2)}, u32[]{:S(2)}) %collective-permute-start.22) | collective-permute-done | bytes 65568 | tf_op jit(solution)/shard_map/ppermute | solution.py:31
  79.9 0.9 s3.1
  80.9 3.1 %collective-permute-start.26 = (bf16[256,512]{1,0:T(8,128)(2,1)}, bf16[256,512]{1,0:T(8,128)(2,1)S(1)}, u32[]{:S(2)}, u32[]{:S(2)}) collective-permute-start(bf16[256,512]{1,0:T(8,128)(2,1)} %get-tuple-element.64), channel_id=1, source_target_pairs={{0,224},{1,225},{2,226},{3,227},{4,228},{5,229},{6,230},{7,231},{8... | collective-permute-start | bytes 786440 | tf_op jit(solution)/shard_map/ppermute | solution.py:31
  84.0 3.3 %collective-permute-start.32 = (bf16[64,512]{1,0:T(8,128)(2,1)S(1)}, bf16[64,512]{1,0:T(8,128)(2,1)S(1)}, u32[]{:S(2)}, u32[]{:S(2)}) collective-permute-start(bf16[64,512]{1,0:T(8,128)(2,1)S(1)} %get-tuple-element.69.refs_0_), channel_id=1, source_target_pairs={{0,6},{1,7},{2,4},{3,5},{4,2},{5,3},{6,0},{7,1},{8,14},{9,15},{10,... | collective-permute-start | bytes 196616 | tf_op jit(solution)/shard_map/ppermute | solution.py:31
  87.3 1.0 collective-permute-start.31
  88.8 1.0 collective-permute-done.32.refs_3_
  89.9 3.3 %collective-permute-done.31.refs_2_ = bf16[64,512]{1,0:T(8,128)(2,1)S(1)} collective-permute-done((bf16[64,512]{1,0:T(8,128)(2,1)S(1)}, bf16[64,512]{1,0:T(8,128)(2,1)S(1)}, u32[]{:S(2)}, u32[]{:S(2)}) %collective-permute-start.31) | collective-permute-done | bytes 65568 | tf_op jit(solution)/shard_map/ppermute | solution.py:31
  93.5 3.2 %collective-permute-start.28 = (bf16[256,512]{1,0:T(8,128)(2,1)}, bf16[256,512]{1,0:T(8,128)(2,1)S(1)}, u32[]{:S(2)}, u32[]{:S(2)}) collective-permute-start(bf16[256,512]{1,0:T(8,128)(2,1)} %copy-done.7), channel_id=1, source_target_pairs={{0,224},{1,225},{2,226},{3,227},{4,228},{5,229},{6,230},{7,231},{8... | collective-permute-start | bytes 786440 | tf_op jit(solution)/shard_map/ppermute | solution.py:31
  96.7 1.5 %collective-permute-start.29 = (bf16[256,512]{1,0:T(8,128)(2,1)}, bf16[256,512]{1,0:T(8,128)(2,1)S(1)}, u32[]{:S(2)}, u32[]{:S(2)}) collective-permute-start(bf16[256,512]{1,0:T(8,128)(2,1)} %copy-done.6), channel_id=1, source_target_pairs={{0,16},{1,17},{2,18},{3,19},{4,20},{5,21},{6,22},{7,23},{8,24},{9,... | collective-permute-start | bytes 786440 | tf_op jit(solution)/shard_map/ppermute | solution.py:31
  98.3 1.1 %maximum_convert_fusion = f32[512,512]{1,0:T(8,128)} fusion(bf16[256,512]{1,0:T(8,128)(2,1)S(1)} %get-tuple-element.78, bf16[256,512]{1,0:T(8,128)(2,1)S(1)} %get-tuple-element.77), kind=kLoop, calls=%fused_computation.1 | loop fusion | flops 1048576 | bytes 1572864 | tf_op jit(solution)/shard_map/convert_element_type | solution.py:314
  99.4 3.5 %collective-permute-done.28.refs_2_ = bf16[256,512]{1,0:T(8,128)(2,1)S(1)} collective-permute-done((bf16[256,512]{1,0:T(8,128)(2,1)}, bf16[256,512]{1,0:T(8,128)(2,1)S(1)}, u32[]{:S(2)}, u32[]{:S(2)}) %collective-permute-start.28) | collective-permute-done | bytes 262176 | tf_op jit(solution)/shard_map/ppermute | solution.py:31
  102.9 3.6 %collective-permute-done.29.refs_3_ = bf16[256,512]{1,0:T(8,128)(2,1)S(1)} collective-permute-done((bf16[256,512]{1,0:T(8,128)(2,1)}, bf16[256,512]{1,0:T(8,128)(2,1)S(1)}, u32[]{:S(2)}, u32[]{:S(2)}) %collective-permute-start.29) | collective-permute-done | bytes 262176 | tf_op jit(solution)/shard_map/ppermute | solution.py:31
  106.5 0.8 s5.1
  (63 shorter events, 3.5 us)
Async XLA Ops:
  0.6 1.0 copy-start
  0.6 14.4 %copy-start.4 = (s32[16]{0:T(128)S(1)}, s32[16]{0:T(128)}, u32[]{:S(2)}) copy-start(s32[16]{0:T(128)} %constant.80.clone.order_ref) | copy-start | bytes 196
  0.7 14.4 %copy-start.3 = (s32[1,1,4]{2,1,0:T(1,128)S(1)}, s32[1,1,4]{2,1,0:T(1,128)}, u32[]{:S(2)}) copy-start(s32[1,1,4]{2,1,0:T(1,128)} %param.16) | copy-start | bytes 52
  0.7 14.4 %copy-start.2 = (s32[1,1,4,24]{3,2,1,0:T(4,128)S(1)}, s32[1,1,4,24]{3,2,1,0:T(4,128)}, u32[]{:S(2)}) copy-start(s32[1,1,4,24]{3,2,1,0:T(4,128)} %param.15) | copy-start | bytes 1156
  0.7 14.4 %copy-start.1 = (s32[1,1,4,24]{3,2,1,0:T(4,128)S(1)}, s32[1,1,4,24]{3,2,1,0:T(4,128)}, u32[]{:S(2)}) copy-start(s32[1,1,4,24]{3,2,1,0:T(4,128)} %param.14) | copy-start | bytes 1156
  3.2 10.0 %collective-permute-start.5 = (bf16[256,512]{1,0:T(8,128)(2,1)S(1)}, bf16[256,512]{1,0:T(8,128)(2,1)}, u32[]{:S(2)}, u32[]{:S(2)}) collective-permute-start(bf16[256,512]{1,0:T(8,128)(2,1)S(1)} %convolution_convert_fusion), channel_id=1, source_target_pairs={{0,8},{1,9},{2,10},{3,11},{16,24},{17,25},{18,26},{19,27},{32,40},... | collective-permute-start | bytes 786440 | tf_op jit(solution)/shard_map/ppermute | solution.py:31
  4.5 3.2 %collective-permute-start.2 = (bf16[256,512]{1,0:T(8,128)(2,1)S(1)}, bf16[256,512]{1,0:T(8,128)(2,1)S(1)}, u32[]{:S(2)}, u32[]{:S(2)}) collective-permute-start(bf16[256,512]{1,0:T(8,128)(2,1)S(1)} %convolution_convert_fusion), channel_id=1, source_target_pairs={{0,6},{1,7},{2,4},{3,5},{16,22},{17,23},{18,20},{19,21},{32,38},{3... | collective-permute-start | bytes 786440 | tf_op jit(solution)/shard_map/ppermute | solution.py:31
  5.1 2.5 %collective-permute-start.1 = (bf16[256,512]{1,0:T(8,128)(2,1)S(1)}, bf16[256,512]{1,0:T(8,128)(2,1)S(1)}, u32[]{:S(2)}, u32[]{:S(2)}) collective-permute-start(bf16[256,512]{1,0:T(8,128)(2,1)S(1)} %convolution_convert_fusion), channel_id=1, source_target_pairs={{0,2},{1,3},{2,0},{3,1},{16,18},{17,19},{18,16},{19,17},{32,34},{3... | collective-permute-start | bytes 786440 | tf_op jit(solution)/shard_map/ppermute | solution.py:31
  7.4 7.5 %collective-permute-start = (bf16[256,512]{1,0:T(8,128)(2,1)S(1)}, bf16[256,512]{1,0:T(8,128)(2,1)S(1)}, u32[]{:S(2)}, u32[]{:S(2)}) collective-permute-start(bf16[256,512]{1,0:T(8,128)(2,1)S(1)} %fusion), channel_id=1, source_target_pairs={{0,1},{1,0},{2,3},{3,2},{4,5},{5,4},{6,7},{7,6},{8,9},{9,8},{10,11... | collective-permute-start | bytes 786440 | tf_op jit(solution)/shard_map/ppermute | solution.py:31
  7.7 18.4 %collective-permute-start.4 = (bf16[256,512]{1,0:T(8,128)(2,1)S(1)}, bf16[256,512]{1,0:T(8,128)(2,1)S(1)}, u32[]{:S(2)}, u32[]{:S(2)}) collective-permute-start(bf16[256,512]{1,0:T(8,128)(2,1)S(1)} %broadcast_select_fusion.2), channel_id=1, source_target_pairs={{0,8},{1,9},{2,10},{3,11},{4,12},{5,13},{6,14},{7,15},{16,24},{17,... | collective-permute-start | bytes 786440 | tf_op jit(solution)/shard_map/ppermute | solution.py:31
  9.0 12.8 %collective-permute-start.3 = (bf16[256,512]{1,0:T(8,128)(2,1)S(1)}, bf16[256,512]{1,0:T(8,128)(2,1)S(1)}, u32[]{:S(2)}, u32[]{:S(2)}) collective-permute-start(bf16[256,512]{1,0:T(8,128)(2,1)S(1)} %collective-permute-done.2), channel_id=1, source_target_pairs={{4,6},{5,7},{6,4},{7,5},{20,22},{21,23},{22,20},{23,21},{36,38},{3... | collective-permute-start | bytes 786440 | tf_op jit(solution)/shard_map/ppermute | solution.py:31
  13.2 8.6 %collective-permute-start.6 = (bf16[256,512]{1,0:T(8,128)(2,1)}, bf16[256,512]{1,0:T(8,128)(2,1)S(1)}, u32[]{:S(2)}, u32[]{:S(2)}) collective-permute-start(bf16[256,512]{1,0:T(8,128)(2,1)} %collective-permute-done.5), channel_id=1, source_target_pairs={{8,12},{9,13},{10,14},{11,15},{24,28},{25,29},{26,30},{27,31},{40,... | collective-permute-start | bytes 786440 | tf_op jit(solution)/shard_map/ppermute | solution.py:31
  17.5 10.3 %collective-permute-start.9 = (bf16[128,512]{1,0:T(8,128)(2,1)S(1)}, bf16[128,512]{1,0:T(8,128)(2,1)S(1)}, u32[]{:S(2)}, u32[]{:S(2)}) collective-permute-start(bf16[128,512]{1,0:T(8,128)(2,1)S(1)} %get-tuple-element.39), channel_id=1, source_target_pairs={{0,2},{1,3},{2,0},{3,1},{4,6},{5,7},{6,4},{7,5},{8,10},{9,11},{10,... | collective-permute-start | bytes 393224 | tf_op jit(solution)/shard_map/ppermute | solution.py:31
  27.2 6.4 %collective-permute-start.7 = (bf16[256,512]{1,0:T(8,128)(2,1)S(1)}, bf16[256,512]{1,0:T(8,128)(2,1)S(1)}, u32[]{:S(2)}, u32[]{:S(2)}) collective-permute-start(bf16[256,512]{1,0:T(8,128)(2,1)S(1)} %broadcast_select_fusion.4.refs_0_), channel_id=1, source_target_pairs={{0,1},{1,0},{2,3},{3,2},{4,5},{5,4},{6,7},{7,6},{8,9},{9,8},{10,11... | collective-permute-start | bytes 786440 | tf_op jit(solution)/shard_map/ppermute | solution.py:31
  27.3 6.3 %collective-permute-start.8 = (bf16[256,512]{1,0:T(8,128)(2,1)S(1)}, bf16[256,512]{1,0:T(8,128)(2,1)S(1)}, u32[]{:S(2)}, u32[]{:S(2)}) collective-permute-start(bf16[256,512]{1,0:T(8,128)(2,1)S(1)} %get-tuple-element.74.refs_1_), channel_id=1, source_target_pairs={{0,1},{1,0},{2,3},{3,2},{4,5},{5,4},{6,7},{7,6},{8,9},{9,8},{10,11... | collective-permute-start | bytes 786440 | tf_op jit(solution)/shard_map/ppermute | solution.py:31
  27.8 5.8 %collective-permute-start.10 = (bf16[128,512]{1,0:T(8,128)(2,1)S(1)}, bf16[128,512]{1,0:T(8,128)(2,1)S(1)}, u32[]{:S(2)}, u32[]{:S(2)}) collective-permute-start(bf16[128,512]{1,0:T(8,128)(2,1)S(1)} %add_convert_fusion.refs_4_), channel_id=1, source_target_pairs={{0,32},{1,33},{2,34},{3,35},{4,36},{5,37},{6,38},{7,39},{8,40},{9,... | collective-permute-start | bytes 393224 | tf_op jit(solution)/shard_map/ppermute | solution.py:31
  33.7 1.9 %copy-start.5 = (bf16[1,1,4,24,128,128]{5,4,3,2,1,0:T(8,128)(2,1)S(1)}, bf16[1,1,4,24,128,128]{5,4,3,2,1,0:T(8,128)(2,1)}, u32[]{:S(2)}) copy-start(bf16[1,1,4,24,128,128]{5,4,3,2,1,0:T(8,128)(2,1)} %param.13) | copy-start | bytes 9437188
  37.1 14.8 %collective-permute-start.11 = (bf16[256,512]{1,0:T(8,128)(2,1)S(1)}, bf16[256,512]{1,0:T(8,128)(2,1)S(1)}, u32[]{:S(2)}, u32[]{:S(2)}) collective-permute-start(bf16[256,512]{1,0:T(8,128)(2,1)S(1)} %get-tuple-element.46), channel_id=1, source_target_pairs={{0,32},{1,33},{2,34},{3,35},{4,36},{5,37},{6,38},{7,39},{8,40},{9,... | collective-permute-start | bytes 786440 | tf_op jit(solution)/shard_map/ppermute | solution.py:31
  39.6 12.3 %collective-permute-start.12 = (bf16[256,512]{1,0:T(8,128)(2,1)S(1)}, bf16[256,512]{1,0:T(8,128)(2,1)S(1)}, u32[]{:S(2)}, u32[]{:S(2)}) collective-permute-start(bf16[256,512]{1,0:T(8,128)(2,1)S(1)} %get-tuple-element.48), channel_id=1, source_target_pairs={{0,16},{1,17},{2,18},{3,19},{4,20},{5,21},{6,22},{7,23},{8,24},{9,... | collective-permute-start | bytes 786440 | tf_op jit(solution)/shard_map/ppermute | solution.py:31
  41.3 10.6 %collective-permute-start.13 = (bf16[256,512]{1,0:T(8,128)(2,1)S(1)}, bf16[256,512]{1,0:T(8,128)(2,1)S(1)}, u32[]{:S(2)}, u32[]{:S(2)}) collective-permute-start(bf16[256,512]{1,0:T(8,128)(2,1)S(1)} %get-tuple-element.50), channel_id=1, source_target_pairs={{0,224},{1,225},{2,226},{3,227},{4,228},{5,229},{6,230},{7,231},{8... | collective-permute-start | bytes 786440 | tf_op jit(solution)/shard_map/ppermute | solution.py:31
  46.0 5.9 %collective-permute-start.14 = (bf16[64,512]{1,0:T(8,128)(2,1)S(1)}, bf16[64,512]{1,0:T(8,128)(2,1)S(1)}, u32[]{:S(2)}, u32[]{:S(2)}) collective-permute-start(bf16[64,512]{1,0:T(8,128)(2,1)S(1)} %get-tuple-element.85), channel_id=1, source_target_pairs={{0,4},{1,5},{2,6},{3,7},{4,0},{5,1},{6,2},{7,3},{8,12},{9,13},{10,... | collective-permute-start | bytes 196616 | tf_op jit(solution)/shard_map/ppermute | solution.py:31
  52.1 6.4 %collective-permute-start.18 = (bf16[64,512]{1,0:T(8,128)(2,1)S(1)}, bf16[64,512]{1,0:T(8,128)(2,1)S(1)}, u32[]{:S(2)}, u32[]{:S(2)}) collective-permute-start(bf16[64,512]{1,0:T(8,128)(2,1)S(1)} %get-tuple-element.57), channel_id=1, source_target_pairs={{0,64},{1,65},{2,66},{3,67},{4,68},{5,69},{6,70},{7,71},{8,72},{9,... | collective-permute-start | bytes 196616 | tf_op jit(solution)/shard_map/ppermute | solution.py:31
  53.7 14.6 %collective-permute-start.16 = (bf16[384,512]{1,0:T(8,128)(2,1)S(1)}, bf16[384,512]{1,0:T(8,128)(2,1)S(1)}, u32[]{:S(2)}, u32[]{:S(2)}) collective-permute-start(bf16[384,512]{1,0:T(8,128)(2,1)S(1)} %get-tuple-element.54), channel_id=1, source_target_pairs={{0,32},{1,33},{2,34},{3,35},{4,36},{5,37},{6,38},{7,39},{8,40},{9,... | collective-permute-start | bytes 1179656 | tf_op jit(solution)/shard_map/ppermute | solution.py:31
  56.6 11.7 %collective-permute-start.17 = (bf16[384,512]{1,0:T(8,128)(2,1)S(1)}, bf16[384,512]{1,0:T(8,128)(2,1)S(1)}, u32[]{:S(2)}, u32[]{:S(2)}) collective-permute-start(bf16[384,512]{1,0:T(8,128)(2,1)S(1)} %get-tuple-element.56), channel_id=1, source_target_pairs={{0,224},{1,225},{2,226},{3,227},{4,228},{5,229},{6,230},{7,231},{8... | collective-permute-start | bytes 1179656 | tf_op jit(solution)/shard_map/ppermute | solution.py:31
  56.9 12.1 %collective-permute-start.15 = (bf16[512,512]{1,0:T(8,128)(2,1)S(1)}, bf16[512,512]{1,0:T(8,128)(2,1)S(1)}, u32[]{:S(2)}, u32[]{:S(2)}) collective-permute-start(bf16[512,512]{1,0:T(8,128)(2,1)S(1)} %get-tuple-element.53), channel_id=1, source_target_pairs={{0,16},{1,17},{2,18},{3,19},{4,20},{5,21},{6,22},{7,23},{8,24},{9,... | collective-permute-start | bytes 1572872 | tf_op jit(solution)/shard_map/ppermute | solution.py:31
  58.6 9.7 %collective-permute-start.19 = (bf16[64,512]{1,0:T(8,128)(2,1)S(1)}, bf16[64,512]{1,0:T(8,128)(2,1)S(1)}, u32[]{:S(2)}, u32[]{:S(2)}) collective-permute-start(bf16[64,512]{1,0:T(8,128)(2,1)S(1)} %add_convert_fusion.1.refs_5_), channel_id=1, source_target_pairs={{0,128},{1,129},{2,130},{3,131},{4,132},{5,133},{6,134},{7,135},{8... | collective-permute-start | bytes 196616 | tf_op jit(solution)/shard_map/ppermute | solution.py:31
  69.2 10.7 %collective-permute-start.20 = (bf16[256,512]{1,0:T(8,128)(2,1)S(1)}, bf16[256,512]{1,0:T(8,128)(2,1)S(1)}, u32[]{:S(2)}, u32[]{:S(2)}) collective-permute-start(bf16[256,512]{1,0:T(8,128)(2,1)S(1)} %get-tuple-element.58), channel_id=1, source_target_pairs={{0,32},{1,33},{2,34},{3,35},{4,36},{5,37},{6,38},{7,39},{8,40},{9,... | collective-permute-start | bytes 786440 | tf_op jit(solution)/shard_map/ppermute | solution.py:31
  71.0 8.9 %collective-permute-start.21 = (bf16[256,512]{1,0:T(8,128)(2,1)S(1)}, bf16[256,512]{1,0:T(8,128)(2,1)S(1)}, u32[]{:S(2)}, u32[]{:S(2)}) collective-permute-start(bf16[256,512]{1,0:T(8,128)(2,1)S(1)} %get-tuple-element.60), channel_id=1, source_target_pairs={{0,224},{1,225},{2,226},{3,227},{4,228},{5,229},{6,230},{7,231},{8... | collective-permute-start | bytes 786440 | tf_op jit(solution)/shard_map/ppermute | solution.py:31
  72.5 4.3 %collective-permute-start.24 = (bf16[64,512]{1,0:T(8,128)(2,1)S(1)}, bf16[64,512]{1,0:T(8,128)(2,1)S(1)}, u32[]{:S(2)}, u32[]{:S(2)}) collective-permute-start(bf16[64,512]{1,0:T(8,128)(2,1)S(1)} %get-tuple-element.61.refs_4_), channel_id=1, source_target_pairs={{0,24},{1,25},{2,26},{3,27},{4,28},{5,29},{6,30},{7,31},{8,16},{9,... | collective-permute-start | bytes 196616 | tf_op jit(solution)/shard_map/ppermute | solution.py:31
  72.5 5.8 %collective-permute-start.23 = (bf16[64,512]{1,0:T(8,128)(2,1)S(1)}, bf16[64,512]{1,0:T(8,128)(2,1)S(1)}, u32[]{:S(2)}, u32[]{:S(2)}) collective-permute-start(bf16[64,512]{1,0:T(8,128)(2,1)S(1)} %get-tuple-element.61.refs_4_), channel_id=1, source_target_pairs={{0,16},{1,17},{2,18},{3,19},{4,20},{5,21},{6,22},{7,23},{8,24},{9,... | collective-permute-start | bytes 196616 | tf_op jit(solution)/shard_map/ppermute | solution.py:31
  75.6 4.3 %collective-permute-start.22 = (bf16[64,512]{1,0:T(8,128)(2,1)S(1)}, bf16[64,512]{1,0:T(8,128)(2,1)S(1)}, u32[]{:S(2)}, u32[]{:S(2)}) collective-permute-start(bf16[64,512]{1,0:T(8,128)(2,1)S(1)} %get-tuple-element.61.refs_4_), channel_id=1, source_target_pairs={{0,8},{1,9},{2,10},{3,11},{4,12},{5,13},{6,14},{7,15},{8,0},{9,1},... | collective-permute-start | bytes 196616 | tf_op jit(solution)/shard_map/ppermute | solution.py:31
  80.8 7.8 %collective-permute-start.25 = (bf16[256,512]{1,0:T(8,128)(2,1)}, bf16[256,512]{1,0:T(8,128)(2,1)S(1)}, u32[]{:S(2)}, u32[]{:S(2)}) collective-permute-start(bf16[256,512]{1,0:T(8,128)(2,1)} %get-tuple-element.62), channel_id=1, source_target_pairs={{0,32},{1,33},{2,34},{3,35},{4,36},{5,37},{6,38},{7,39},{8,40},{9,... | collective-permute-start | bytes 786440 | tf_op jit(solution)/shard_map/ppermute | solution.py:31
  80.9 7.7 %collective-permute-start.26 = (bf16[256,512]{1,0:T(8,128)(2,1)}, bf16[256,512]{1,0:T(8,128)(2,1)S(1)}, u32[]{:S(2)}, u32[]{:S(2)}) collective-permute-start(bf16[256,512]{1,0:T(8,128)(2,1)} %get-tuple-element.64), channel_id=1, source_target_pairs={{0,224},{1,225},{2,226},{3,227},{4,228},{5,229},{6,230},{7,231},{8... | collective-permute-start | bytes 786440 | tf_op jit(solution)/shard_map/ppermute | solution.py:31
  84.0 5.8 %collective-permute-start.32 = (bf16[64,512]{1,0:T(8,128)(2,1)S(1)}, bf16[64,512]{1,0:T(8,128)(2,1)S(1)}, u32[]{:S(2)}, u32[]{:S(2)}) collective-permute-start(bf16[64,512]{1,0:T(8,128)(2,1)S(1)} %get-tuple-element.69.refs_0_), channel_id=1, source_target_pairs={{0,6},{1,7},{2,4},{3,5},{4,2},{5,3},{6,0},{7,1},{8,14},{9,15},{10,... | collective-permute-start | bytes 196616 | tf_op jit(solution)/shard_map/ppermute | solution.py:31
  87.3 5.8 %collective-permute-start.31 = (bf16[64,512]{1,0:T(8,128)(2,1)S(1)}, bf16[64,512]{1,0:T(8,128)(2,1)S(1)}, u32[]{:S(2)}, u32[]{:S(2)}) collective-permute-start(bf16[64,512]{1,0:T(8,128)(2,1)S(1)} %get-tuple-element.69.refs_0_), channel_id=1, source_target_pairs={{0,4},{1,5},{2,6},{3,7},{4,0},{5,1},{6,2},{7,3},{8,12},{9,13},{10,... | collective-permute-start | bytes 196616 | tf_op jit(solution)/shard_map/ppermute | solution.py:31
  88.3 4.8 %collective-permute-start.30 = (bf16[64,512]{1,0:T(8,128)(2,1)S(1)}, bf16[64,512]{1,0:T(8,128)(2,1)S(1)}, u32[]{:S(2)}, u32[]{:S(2)}) collective-permute-start(bf16[64,512]{1,0:T(8,128)(2,1)S(1)} %get-tuple-element.69.refs_0_), channel_id=1, source_target_pairs={{0,2},{1,3},{2,0},{3,1},{4,6},{5,7},{6,4},{7,5},{8,10},{9,11},{10,... | collective-permute-start | bytes 196616 | tf_op jit(solution)/shard_map/ppermute | solution.py:31
  88.8 4.3 %copy-start.6 = (bf16[256,512]{1,0:T(8,128)(2,1)}, bf16[256,512]{1,0:T(8,128)(2,1)S(1)}, u32[]{:S(2)}) copy-start(bf16[256,512]{1,0:T(8,128)(2,1)S(1)} %get-tuple-element.68) | copy-start | bytes 786436
  88.8 4.3 %copy-start.7 = (bf16[256,512]{1,0:T(8,128)(2,1)}, bf16[256,512]{1,0:T(8,128)(2,1)S(1)}, u32[]{:S(2)}) copy-start(bf16[256,512]{1,0:T(8,128)(2,1)S(1)} %get-tuple-element.67) | copy-start | bytes 786436
  93.3 4.9 %collective-permute-start.33 = (bf16[256,512]{1,0:T(8,128)(2,1)S(1)}, bf16[256,512]{1,0:T(8,128)(2,1)S(1)}, u32[]{:S(2)}, u32[]{:S(2)}) collective-permute-start(bf16[256,512]{1,0:T(8,128)(2,1)S(1)} %pad_maximum_fusion), channel_id=1, source_target_pairs={{0,1},{1,0},{2,3},{3,2},{4,5},{5,4},{6,7},{7,6},{8,9},{9,8},{10,11... | collective-permute-start | bytes 786440 | tf_op jit(solution)/shard_map/ppermute | solution.py:31
  93.4 13.1 %collective-permute-start.27 = (bf16[256,512]{1,0:T(8,128)(2,1)S(1)}, bf16[256,512]{1,0:T(8,128)(2,1)S(1)}, u32[]{:S(2)}, u32[]{:S(2)}) collective-permute-start(bf16[256,512]{1,0:T(8,128)(2,1)S(1)} %get-tuple-element.66.refs_4_), channel_id=1, source_target_pairs={{0,32},{1,33},{2,34},{3,35},{4,36},{5,37},{6,38},{7,39},{8,40},{9,... | collective-permute-start | bytes 786440 | tf_op jit(solution)/shard_map/ppermute | solution.py:31
  93.5 9.4 %collective-permute-start.28 = (bf16[256,512]{1,0:T(8,128)(2,1)}, bf16[256,512]{1,0:T(8,128)(2,1)S(1)}, u32[]{:S(2)}, u32[]{:S(2)}) collective-permute-start(bf16[256,512]{1,0:T(8,128)(2,1)} %copy-done.7), channel_id=1, source_target_pairs={{0,224},{1,225},{2,226},{3,227},{4,228},{5,229},{6,230},{7,231},{8... | collective-permute-start | bytes 786440 | tf_op jit(solution)/shard_map/ppermute | solution.py:31
  96.7 9.8 %collective-permute-start.29 = (bf16[256,512]{1,0:T(8,128)(2,1)}, bf16[256,512]{1,0:T(8,128)(2,1)S(1)}, u32[]{:S(2)}, u32[]{:S(2)}) collective-permute-start(bf16[256,512]{1,0:T(8,128)(2,1)} %copy-done.6), channel_id=1, source_target_pairs={{0,16},{1,17},{2,18},{3,19},{4,20},{5,21},{6,22},{7,23},{8,24},{9,... | collective-permute-start | bytes 786440 | tf_op jit(solution)/shard_map/ppermute | solution.py:31

commit v4 on v3

--- a/solution.py
+++ b/solution.py
@@ -117,41 +117,42 @@
 def rows_kernel(base, sizes, table_ref, tiles_ref, sources_ref, *rest):
     outs, acc = rest[: len(sizes)], rest[len(sizes)]
 
+    def masked(at, slot, n):
+        live = slot < n
+        code = jnp.where(live, table_ref[at, slot], 0)
+        tile = tiles_ref[code >> 3]
+        return jnp.where(live, tile, jnp.zeros_like(tile)), sources_ref[code & 7]
+
     def pair(at, p, n):
-        one = table_ref[at, 2 * p]
-        paired = 2 * p + 1 < n
-        two = jnp.where(paired, table_ref[at, 2 * p + 1], 0)
-        second = tiles_ref[two // 8]
-        left = jnp.concatenate([tiles_ref[one // 8], jnp.where(paired, second, jnp.zeros_like(second))], axis=0)
-        right = jnp.concatenate([sources_ref[lax.rem(one, 8)], sources_ref[lax.rem(two, 8)]], axis=0)
-        return lax.dot_general(left, right, (((0,), (0,)), ((), ())), preferred_element_type=jnp.float32)
+        (left, right), (left2, right2) = masked(at, 2 * p, n), masked(at, 2 * p + 1, n)
+        return lax.dot_general(
+            jnp.concatenate([left, left2], axis=0),
+            jnp.concatenate([right, right2], axis=0),
+            (((0,), (0,)), ((), ())),
+            preferred_element_type=jnp.float32,
+        )
 
     for g, size in enumerate(sizes):
         first = base + 2 * sum(sizes[:g])
 
-        def block(j, carry):
-            at = first + j
-            n = table_ref[at, COUNT]
-            out = outs[g].at[pl.ds(pl.multiple_of(j * 128, 128), 128), :]
-
-            @pl.when(n == 0)
-            def _():
-                out[...] = jnp.zeros((128, 512), jnp.bfloat16)
-
-            @pl.when(n > 0)
-            def _():
-                acc[...] = pair(at, 0, n)
-
-                def more(p, c):
-                    acc[...] += pair(at, p, n)
-                    return c
-
-                lax.fori_loop(1, (n + 1) // 2, more, 0)
-                out[...] = acc[...].astype(jnp.bfloat16)
-
+        def blocks(j, carry):
+            at = first + 2 * j
+            n, n2 = table_ref[at, COUNT], table_ref[at + 1, COUNT]
+            acc[0] = pair(at, 0, n)
+            acc[1] = pair(at + 1, 0, n2)
+
+            def more(p, c):
+                acc[0] += pair(at, p, n)
+                acc[1] += pair(at + 1, p, n2)
+                return c
+
+            lax.fori_loop(1, (jnp.maximum(n, n2) + 1) // 2, more, 0)
+            start = pl.multiple_of(j * 256, 256)
+            outs[g][pl.ds(start, 128), :] = acc[0].astype(jnp.bfloat16)
+            outs[g][pl.ds(start + 128, 128), :] = acc[1].astype(jnp.bfloat16)
             return carry
 
-        lax.fori_loop(0, 2 * size, block, 0)
+        lax.fori_loop(0, size, blocks, 0)
 
 
 def rows(base, sizes, table, tiles, sources, name):
@@ -162,7 +163,7 @@
         out_shape=[jax.ShapeDtypeStruct((256 * size, 512), jnp.bfloat16) for size in sizes],
         in_specs=[smem, vmem, vmem],
         out_specs=[vmem] * len(sizes),
-        scratch_shapes=[pltpu.VMEM((128, 512), jnp.float32)],
+        scratch_shapes=[pltpu.VMEM((2, 128, 512), jnp.float32)],
         compiler_params=pltpu.CompilerParams(vmem_limit_bytes=10 * 1024 * 1024),
         cost_estimate=pl.CostEstimate(flops=sum(sizes) * 400_000_000, bytes_accessed=1_000_000, transcendentals=0),
         name=name,
@@ -252,10 +253,10 @@
     ).astype(jnp.bfloat16)
     w = lax.dot_general(aggregated, masked, (((0,), (0,)), ((), ())), preferred_element_type=jnp.float32)
     kept, given = halves(w, core)
+    table, given = plan(tile_src[0, 0], tile_dst[0, 0], tile_count[0, 0], given)
     by_x, by_y, swapped = send(node_grad, across), send(node_grad, outward), send(node_grad, swap)
     w = add(kept, send(given, other))
     kept, given = halves(w, y % 2)
-    table, given = plan(tile_src[0, 0], tile_dst[0, 0], tile_count[0, 0], given)
     onward = jnp.where(y < 2, swapped, by_y)
     by_x2, by_far, by_swap = send(onward, across_all), send(by_x, distant), send(by_y, swap_rest)
     w = add(kept, send(given, flipped("y", 1)))
@@ -265,16 +266,13 @@
     even, odd = jnp.where(flip, second, first), jnp.where(flip, first, second)
 
     even2, odd2 = send(even, other), send(odd, other)
-    w = narrow(w)
+    sources, w = stage("s0", [(256, even), (256, odd), (256, even2), (256, odd2)], [(128, narrow(w))])
+    sources = sources.reshape(8, 128, 512)
+
     w_got = send(w, flipped("z", 1))
-    sources, w = stage(
-        "s0", [(256, even), (256, odd), (256, even2), (256, odd2)], [(128, w, w_got)]
-    )
-    sources = sources.reshape(8, 128, 512)
-
     t4, t2, t6 = rows(0, [1, 1, 1], table, tiles, sources, "rows_first")
     x4, up_got, down_got = send(t4, cross), send(t2, up), send(t6, down)
-    kept, given = halves(w, y // 2)
+    kept, given = halves(later("v1", t4, w, w_got), y // 2)
     w_got = send(given, flipped("y", 2))
     t35, m4, t1, t7 = rows(6, [2, 1, 1, 1], table, tiles, sources, "rows_second")
     to_up, to_down, t35, w = stage(

time: 108 us -> 105 us (0.972)
  waiting for transfers between devices: 33.9 us -> 30.8 us
  Pallas kernels: 13.5 us -> 11.8 us
  local copies, waits for them, and re-layouts: 2.99 us -> 4.23 us
    ppermute x34, waiting for transfers between devices: 33.9 us -> 30.8 us  [send(): return lax.ppermute(value, AXES, pairs(move))]
    pallas_call x3, Pallas kernels: 8.65 us -> 6.95 us  [rows(): pl.pallas_call(functools.partial(rows_kernel, base, tuple(sizes)), out_sh...]
    unnamed x16 -> x20, local copies, waits for them, and re-layouts: 2.91 us -> 4.15 us
    pallas_call x7 -> x8, Pallas kernels: 2.42 us -> 2.43 us  [stage(): pl.pallas_call(functools.partial(stage_kernel, tuple(plans), len(arrays),...]
  transfers between devices with their start and end apart: 34 -> 34, of which waited for: 16 -> 18; matrix products, arithmetic and copies ran while one was open for 4% -> 5% of each run, Pallas kernels for 9% -> 9%
where the time goes in v4:
time: 105 us
  starting transfers between devices  50.2 us (48%)
  waiting for transfers between devices  30.8 us (29%)
  Pallas kernels  11.8 us (11%)
  local copies, waits for them, and re-layouts  4.23 us (4%)
  other arithmetic  3.5 us (3%)
  matrix products  3 us (3%)
  between operations  1.15 us (1%)
    ppermute x34, starting transfers between devices, send(): return lax.ppermute(value, AXES, pairs(move))  50.2 us
    ppermute x34, waiting for transfers between devices, send(): return lax.ppermute(value, AXES, pairs(move))  30.8 us
    pallas_call x3, Pallas kernels, rows(): pl.pallas_call(functools.partial(rows_kernel, base, tuple(sizes)), out_sh...  6.95 us
    unnamed x20, local copies, waits for them, and re-layouts  4.15 us
    pallas_call x8, Pallas kernels, stage(): pl.pallas_call(functools.partial(stage_kernel, tuple(plans), len(arrays),...  2.43 us
    pallas_call x1, Pallas kernels, plan(): pl.pallas_call(plan_kernel, out_shape=[jax.ShapeDtypeStruct((SPARE + 1, 1...  2.4 us
  transfers between devices with their start and end apart: 34, of which 18 were waited for; matrix products, arithmetic and copies ran while one was open for 5% of the time, Pallas kernels for 9%

profile of v4, /device:TPU:2, one launch (start us, length us, event | category | flops | bytes accessed | tf_op | source)
XLA Modules:
  0.0 104.7 jit_solution(13879900613651180209)
XLA Ops:
  0.7 1.0 copy-done
  1.7 1.5 %convolution_convert_fusion = bf16[256,512]{1,0:T(8,128)(2,1)S(1)} fusion(bf16[512,512]{1,0:T(8,128)(2,1)S(1)} %copy-done, bf16[256,512]{1,0:T(8,128)(2,1)} %param.9, s32[256,512]{1,0:T(8,128)} %param.10), kind=kOutput, calls=%fused_computation | convolution fusion | flops 134610944 | bytes 1572864 | tf_op jit(solution)/shard_map/dot_general | solution.py:251
  3.2 1.3 %collective-permute-start.4 = (bf16[256,512]{1,0:T(8,128)(2,1)S(1)}, bf16[256,512]{1,0:T(8,128)(2,1)}, u32[]{:S(2)}, u32[]{:S(2)}) collective-permute-start(bf16[256,512]{1,0:T(8,128)(2,1)S(1)} %convolution_convert_fusion), channel_id=1, source_target_pairs={{0,8},{1,9},{2,10},{3,11},{16,24},{17,25},{18,26},{19,27},{32,40},... | collective-permute-start | bytes 786440 | tf_op jit(solution)/shard_map/ppermute | solution.py:31
  5.8 1.5 %fusion.1 = f32[512,512]{0,1:T(8,128)S(1)} fusion(bf16[256,512]{1,0:T(8,128)(2,1)} %param.11, bf16[256,512]{1,0:T(8,128)(2,1)} %param.9, s32[256,512]{1,0:T(8,128)} %param.10), kind=kOutput, calls=%fused_computation.27 | convolution fusion | flops 134479872 | bytes 2097152 | tf_op jit(solution)/shard_map/dot_general | solution.py:254
  7.5 2.4 %plan.1 = (s32[33,16]{1,0:T(8,128)S(1)}, bf16[256,512]{1,0:T(8,128)(2,1)S(1)}) custom-call(s32[4,24]{1,0:T(4,128)S(1)} %bitcast.11, s32[4,24]{1,0:T(4,128)S(1)} %bitcast.12, s32[4]{0:T(128)S(1)} %bitcast.13, s32[16]{0:T(128)S(1)} %copy-done.4, bf16[256,512]{1,0:T(8,128)(2,1)S(1)} %fusion.given_ref), custom_call_target="tpu_custom_call" | custom-call | tf_op jit(solution)/shard_map/plan/pallas_call | solution.py:107
  10.1 1.3 %collective-permute-start.3 = (bf16[256,512]{1,0:T(8,128)(2,1)S(1)}, bf16[256,512]{1,0:T(8,128)(2,1)S(1)}, u32[]{:S(2)}, u32[]{:S(2)}) collective-permute-start(bf16[256,512]{1,0:T(8,128)(2,1)S(1)} %broadcast_select_fusion.2), channel_id=1, source_target_pairs={{0,8},{1,9},{2,10},{3,11},{4,12},{5,13},{6,14},{7,15},{16,24},{17,... | collective-permute-start | bytes 786440 | tf_op jit(solution)/shard_map/ppermute | solution.py:31
  12.1 1.1 %collective-permute-done.4 = bf16[256,512]{1,0:T(8,128)(2,1)} collective-permute-done((bf16[256,512]{1,0:T(8,128)(2,1)S(1)}, bf16[256,512]{1,0:T(8,128)(2,1)}, u32[]{:S(2)}, u32[]{:S(2)}) %collective-permute-start.4) | collective-permute-done | bytes 262176 | tf_op jit(solution)/shard_map/ppermute | solution.py:31
  13.2 4.1 %collective-permute-start.5 = (bf16[256,512]{1,0:T(8,128)(2,1)}, bf16[256,512]{1,0:T(8,128)(2,1)S(1)}, u32[]{:S(2)}, u32[]{:S(2)}) collective-permute-start(bf16[256,512]{1,0:T(8,128)(2,1)} %collective-permute-done.4), channel_id=1, source_target_pairs={{8,12},{9,13},{10,14},{11,15},{24,28},{25,29},{26,30},{27,31},{40,... | collective-permute-start | bytes 786440 | tf_op jit(solution)/shard_map/ppermute | solution.py:31
  17.3 1.0 bitcast_add_fusion
  18.4 0.8 collective-permute-start.9
  19.1 5.1 %collective-permute-done.5 = bf16[256,512]{1,0:T(8,128)(2,1)S(1)} collective-permute-done((bf16[256,512]{1,0:T(8,128)(2,1)}, bf16[256,512]{1,0:T(8,128)(2,1)S(1)}, u32[]{:S(2)}, u32[]{:S(2)}) %collective-permute-start.5) | collective-permute-done | bytes 262176 | tf_op jit(solution)/shard_map/ppermute | solution.py:31
  24.2 1.9 %collective-permute-done.3 = bf16[256,512]{1,0:T(8,128)(2,1)S(1)} collective-permute-done((bf16[256,512]{1,0:T(8,128)(2,1)S(1)}, bf16[256,512]{1,0:T(8,128)(2,1)S(1)}, u32[]{:S(2)}, u32[]{:S(2)}) %collective-permute-start.3) | collective-permute-done | bytes 262176 | tf_op jit(solution)/shard_map/ppermute | solution.py:31
  26.1 1.1 %broadcast_select_fusion.3 = (bf16[256,512]{1,0:T(8,128)(2,1)S(1)}, bf16[256,512]{1,0:T(8,128)(2,1)S(1)}, bf16[256,512]{1,0:T(8,128)(2,1)S(1)}) fusion(pred[]{:T(512)S(6)} %or.3, bf16[256,512]{1,0:T(8,128)(2,1)} %collective-permute-done.4, bf16[256,512]{1,0:T(8,128)(2,1)S(1)} %collective-permute-done.3, bf16[256,512]{1,0:T(8,128)(2,1)S(1)} %convolution_convert_fusion, ...), kind=kLoop, calls=%fused_computation.14 | loop fusion | flops 917504 | bytes 2621443 | tf_op jit(solution)/shard_map/jit(_where)/select_n | solution.py:266
  27.8 1.0 collective-permute-done.6.refs_2_
  29.3 2.0 %collective-permute-start.13 = (bf16[128,512]{1,0:T(8,128)(2,1)S(1)}, bf16[128,512]{1,0:T(8,128)(2,1)S(1)}, u32[]{:S(2)}, u32[]{:S(2)}) collective-permute-start(bf16[128,512]{1,0:T(8,128)(2,1)S(1)} %get-tuple-element.52.refs_0_), channel_id=1, source_target_pairs={{0,32},{1,33},{2,34},{3,35},{4,36},{5,37},{6,38},{7,39},{8,40},{9,... | collective-permute-start | bytes 393224 | tf_op jit(solution)/shard_map/ppermute | solution.py:31
  31.3 1.9 %copy-done.5 = bf16[1,1,4,24,128,128]{5,4,3,2,1,0:T(8,128)(2,1)S(1)} copy-done((bf16[1,1,4,24,128,128]{5,4,3,2,1,0:T(8,128)(2,1)S(1)}, bf16[1,1,4,24,128,128]{5,4,3,2,1,0:T(8,128)(2,1)}, u32[]{:S(2)}) %copy-start.5) | copy-done | bytes 3145752
  33.2 1.7 %rows_first.1 = (bf16[256,512]{1,0:T(8,128)(2,1)S(1)}, bf16[256,512]{1,0:T(8,128)(2,1)S(1)}, bf16[256,512]{1,0:T(8,128)(2,1)S(1)}) custom-call(s32[33,16]{1,0:T(8,128)S(1)} %get-tuple-element.38.table_ref, bf16[96,128,128]{2,1,0:T(8,128)(2,1)S(1)} %bitcast.14, bf16[8,128,512]{2,1,0:T(8,128)(2,1)S(1)} %bitcast.17), custom_call_target="tpu_custom_call" | custom-call | flops 1200000000 | bytes 1000000 | tf_op jit(solution)/shard_map/rows_first/pallas_call | solution.py:161
  35.2 4.8 %collective-permute-start.12 = (bf16[256,512]{1,0:T(8,128)(2,1)S(1)}, bf16[256,512]{1,0:T(8,128)(2,1)S(1)}, u32[]{:S(2)}, u32[]{:S(2)}) collective-permute-start(bf16[256,512]{1,0:T(8,128)(2,1)S(1)} %get-tuple-element.50), channel_id=1, source_target_pairs={{0,224},{1,225},{2,226},{3,227},{4,228},{5,229},{6,230},{7,231},{8... | collective-permute-start | bytes 786440 | tf_op jit(solution)/shard_map/ppermute | solution.py:31
  40.0 2.9 %collective-permute-start.11 = (bf16[256,512]{1,0:T(8,128)(2,1)S(1)}, bf16[256,512]{1,0:T(8,128)(2,1)S(1)}, u32[]{:S(2)}, u32[]{:S(2)}) collective-permute-start(bf16[256,512]{1,0:T(8,128)(2,1)S(1)} %get-tuple-element.48.refs_2_), channel_id=1, source_target_pairs={{0,16},{1,17},{2,18},{3,19},{4,20},{5,21},{6,22},{7,23},{8,24},{9,... | collective-permute-start | bytes 786440 | tf_op jit(solution)/shard_map/ppermute | solution.py:31
  43.3 2.3 %rows_second.1 = (bf16[512,512]{1,0:T(8,128)(2,1)S(1)}, bf16[256,512]{1,0:T(8,128)(2,1)S(1)}, bf16[256,512]{1,0:T(8,128)(2,1)S(1)}, bf16[256,512]{1,0:T(8,128)(2,1)S(1)}) custom-call(s32[33,16]{1,0:T(8,128)S(1)} %get-tuple-element.38.table_ref, bf16[96,128,128]{2,1,0:T(8,128)(2,1)S(1)} %bitcast.15, bf16[8,128,512]{2,1,0:T(8,128)(2,1)S(1)} %bitcast.18), custom_call_target="tpu_custom_call" | custom-call | flops 2000000000 | bytes 1000000 | tf_op jit(solution)/shard_map/rows_second/pallas_call | solution.py:161
  45.6 3.2 %collective-permute-done.14.refs_8_ = bf16[64,512]{1,0:T(8,128)(2,1)S(1)} collective-permute-done((bf16[64,512]{1,0:T(8,128)(2,1)S(1)}, bf16[64,512]{1,0:T(8,128)(2,1)S(1)}, u32[]{:S(2)}, u32[]{:S(2)}) %collective-permute-start.14) | collective-permute-done | bytes 65568 | tf_op jit(solution)/shard_map/ppermute | solution.py:31
  48.8 1.2 %collective-permute-done.11.refs_3_ = bf16[256,512]{1,0:T(8,128)(2,1)S(1)} collective-permute-done((bf16[256,512]{1,0:T(8,128)(2,1)S(1)}, bf16[256,512]{1,0:T(8,128)(2,1)S(1)}, u32[]{:S(2)}, u32[]{:S(2)}) %collective-permute-start.11) | collective-permute-done | bytes 262176 | tf_op jit(solution)/shard_map/ppermute | solution.py:31
  50.4 2.4 %collective-permute-start.16 = (bf16[384,512]{1,0:T(8,128)(2,1)S(1)}, bf16[384,512]{1,0:T(8,128)(2,1)S(1)}, u32[]{:S(2)}, u32[]{:S(2)}) collective-permute-start(bf16[384,512]{1,0:T(8,128)(2,1)S(1)} %get-tuple-element.54), channel_id=1, source_target_pairs={{0,32},{1,33},{2,34},{3,35},{4,36},{5,37},{6,38},{7,39},{8,40},{9,... | collective-permute-start | bytes 1179656 | tf_op jit(solution)/shard_map/ppermute | solution.py:31
  52.7 0.9 collective-permute-start.17
  53.7 1.8 %collective-permute-start.15 = (bf16[512,512]{1,0:T(8,128)(2,1)S(1)}, bf16[512,512]{1,0:T(8,128)(2,1)S(1)}, u32[]{:S(2)}, u32[]{:S(2)}) collective-permute-start(bf16[512,512]{1,0:T(8,128)(2,1)S(1)} %get-tuple-element.53), channel_id=1, source_target_pairs={{0,16},{1,17},{2,18},{3,19},{4,20},{5,21},{6,22},{7,23},{8,24},{9,... | collective-permute-start | bytes 1572872 | tf_op jit(solution)/shard_map/ppermute | solution.py:31
  55.5 0.7 collective-permute-done.18
  56.2 4.3 %collective-permute-start.19 = (bf16[64,512]{1,0:T(8,128)(2,1)S(1)}, bf16[64,512]{1,0:T(8,128)(2,1)S(1)}, u32[]{:S(2)}, u32[]{:S(2)}) collective-permute-start(bf16[64,512]{1,0:T(8,128)(2,1)S(1)} %add_convert_fusion.1.refs_5_), channel_id=1, source_target_pairs={{0,128},{1,129},{2,130},{3,131},{4,132},{5,133},{6,134},{7,135},{8... | collective-permute-start | bytes 196616 | tf_op jit(solution)/shard_map/ppermute | solution.py:31
  60.5 1.2 %copy-done.7 = bf16[1024,512]{1,0:T(8,128)(2,1)S(1)} copy-done((bf16[1024,512]{1,0:T(8,128)(2,1)S(1)}, bf16[1024,512]{1,0:T(8,128)(2,1)}, u32[]{:S(2)}) %copy-start.7) | copy-done | bytes 1048600
  61.7 3.0 %rows_third.1 = (bf16[256,512]{1,0:T(8,128)(2,1)S(1)}, bf16[256,512]{1,0:T(8,128)(2,1)S(1)}, bf16[256,512]{1,0:T(8,128)(2,1)S(1)}, bf16[256,512]{1,0:T(8,128)(2,...) custom-call(s32[33,16]{1,0:T(8,128)S(1)} %get-tuple-element.38.table, ...), custom_call_target="tpu_custom_call" | custom-call | flops 3200000000 | bytes 1000000 | tf_op jit(solution)/shard_map/rows_third/pallas_call | solution.py:161
  64.7 1.3 %collective-permute-done.19.refs_6_ = bf16[64,512]{1,0:T(8,128)(2,1)S(1)} collective-permute-done((bf16[64,512]{1,0:T(8,128)(2,1)S(1)}, bf16[64,512]{1,0:T(8,128)(2,1)S(1)}, u32[]{:S(2)}, u32[]{:S(2)}) %collective-permute-start.19) | collective-permute-done | bytes 65568 | tf_op jit(solution)/shard_map/ppermute | solution.py:31
  66.1 2.0 %collective-permute-done.15.refs_1_ = bf16[512,512]{1,0:T(8,128)(2,1)S(1)} collective-permute-done((bf16[512,512]{1,0:T(8,128)(2,1)S(1)}, bf16[512,512]{1,0:T(8,128)(2,1)S(1)}, u32[]{:S(2)}, u32[]{:S(2)}) %collective-permute-start.15) | collective-permute-done | bytes 524320 | tf_op jit(solution)/shard_map/ppermute | solution.py:31
  68.2 1.7 %collective-permute-start.20 = (bf16[256,512]{1,0:T(8,128)(2,1)S(1)}, bf16[256,512]{1,0:T(8,128)(2,1)S(1)}, u32[]{:S(2)}, u32[]{:S(2)}) collective-permute-start(bf16[256,512]{1,0:T(8,128)(2,1)S(1)} %get-tuple-element.58), channel_id=1, source_target_pairs={{0,32},{1,33},{2,34},{3,35},{4,36},{5,37},{6,38},{7,39},{8,40},{9,... | collective-permute-start | bytes 786440 | tf_op jit(solution)/shard_map/ppermute | solution.py:31
  69.9 1.6 %collective-permute-start.21 = (bf16[256,512]{1,0:T(8,128)(2,1)S(1)}, bf16[256,512]{1,0:T(8,128)(2,1)S(1)}, u32[]{:S(2)}, u32[]{:S(2)}) collective-permute-start(bf16[256,512]{1,0:T(8,128)(2,1)S(1)} %get-tuple-element.60), channel_id=1, source_target_pairs={{0,224},{1,225},{2,226},{3,227},{4,228},{5,229},{6,230},{7,231},{8... | collective-permute-start | bytes 786440 | tf_op jit(solution)/shard_map/ppermute | solution.py:31
  71.5 1.5 %collective-permute-start.23 = (bf16[64,512]{1,0:T(8,128)(2,1)S(1)}, bf16[64,512]{1,0:T(8,128)(2,1)S(1)}, u32[]{:S(2)}, u32[]{:S(2)}) collective-permute-start(bf16[64,512]{1,0:T(8,128)(2,1)S(1)} %get-tuple-element.61.refs_4_), channel_id=1, source_target_pairs={{0,16},{1,17},{2,18},{3,19},{4,20},{5,21},{6,22},{7,23},{8,24},{9,... | collective-permute-start | bytes 196616 | tf_op jit(solution)/shard_map/ppermute | solution.py:31
  73.1 2.5 %collective-permute-start.22 = (bf16[64,512]{1,0:T(8,128)(2,1)S(1)}, bf16[64,512]{1,0:T(8,128)(2,1)S(1)}, u32[]{:S(2)}, u32[]{:S(2)}) collective-permute-start(bf16[64,512]{1,0:T(8,128)(2,1)S(1)} %get-tuple-element.61.refs_4_), channel_id=1, source_target_pairs={{0,8},{1,9},{2,10},{3,11},{4,12},{5,13},{6,14},{7,15},{8,0},{9,1},... | collective-permute-start | bytes 196616 | tf_op jit(solution)/shard_map/ppermute | solution.py:31
  75.8 1.5 %collective-permute-done.23.refs_6_ = bf16[64,512]{1,0:T(8,128)(2,1)S(1)} collective-permute-done((bf16[64,512]{1,0:T(8,128)(2,1)S(1)}, bf16[64,512]{1,0:T(8,128)(2,1)S(1)}, u32[]{:S(2)}, u32[]{:S(2)}) %collective-permute-start.23) | collective-permute-done | bytes 65568 | tf_op jit(solution)/shard_map/ppermute | solution.py:31
  77.3 1.3 %collective-permute-done.22.refs_5_ = bf16[64,512]{1,0:T(8,128)(2,1)S(1)} collective-permute-done((bf16[64,512]{1,0:T(8,128)(2,1)S(1)}, bf16[64,512]{1,0:T(8,128)(2,1)S(1)}, u32[]{:S(2)}, u32[]{:S(2)}) %collective-permute-start.22) | collective-permute-done | bytes 65568 | tf_op jit(solution)/shard_map/ppermute | solution.py:31
  78.5 0.9 s3.1
  79.8 2.8 %collective-permute-start.26 = (bf16[256,512]{1,0:T(8,128)(2,1)}, bf16[256,512]{1,0:T(8,128)(2,1)S(1)}, u32[]{:S(2)}, u32[]{:S(2)}) collective-permute-start(bf16[256,512]{1,0:T(8,128)(2,1)} %get-tuple-element.64), channel_id=1, source_target_pairs={{0,224},{1,225},{2,226},{3,227},{4,228},{5,229},{6,230},{7,231},{8... | collective-permute-start | bytes 786440 | tf_op jit(solution)/shard_map/ppermute | solution.py:31
  82.7 2.0 %collective-permute-start.32 = (bf16[64,512]{1,0:T(8,128)(2,1)S(1)}, bf16[64,512]{1,0:T(8,128)(2,1)S(1)}, u32[]{:S(2)}, u32[]{:S(2)}) collective-permute-start(bf16[64,512]{1,0:T(8,128)(2,1)S(1)} %get-tuple-element.69.refs_0_), channel_id=1, source_target_pairs={{0,6},{1,7},{2,4},{3,5},{4,2},{5,3},{6,0},{7,1},{8,14},{9,15},{10,... | collective-permute-start | bytes 196616 | tf_op jit(solution)/shard_map/ppermute | solution.py:31
  84.7 2.1 %collective-permute-start.30 = (bf16[64,512]{1,0:T(8,128)(2,1)S(1)}, bf16[64,512]{1,0:T(8,128)(2,1)S(1)}, u32[]{:S(2)}, u32[]{:S(2)}) collective-permute-start(bf16[64,512]{1,0:T(8,128)(2,1)S(1)} %get-tuple-element.69.refs_0_), channel_id=1, source_target_pairs={{0,2},{1,3},{2,0},{3,1},{4,6},{5,7},{6,4},{7,5},{8,10},{9,11},{10,... | collective-permute-start | bytes 196616 | tf_op jit(solution)/shard_map/ppermute | solution.py:31
  88.1 2.3 %collective-permute-done.31.refs_2_ = bf16[64,512]{1,0:T(8,128)(2,1)S(1)} collective-permute-done((bf16[64,512]{1,0:T(8,128)(2,1)S(1)}, bf16[64,512]{1,0:T(8,128)(2,1)S(1)}, u32[]{:S(2)}, u32[]{:S(2)}) %collective-permute-start.31) | collective-permute-done | bytes 65568 | tf_op jit(solution)/shard_map/ppermute | solution.py:31
  90.8 3.2 %collective-permute-start.28 = (bf16[256,512]{1,0:T(8,128)(2,1)}, bf16[256,512]{1,0:T(8,128)(2,1)S(1)}, u32[]{:S(2)}, u32[]{:S(2)}) collective-permute-start(bf16[256,512]{1,0:T(8,128)(2,1)} %copy-done.9), channel_id=1, source_target_pairs={{0,224},{1,225},{2,226},{3,227},{4,228},{5,229},{6,230},{7,231},{8... | collective-permute-start | bytes 786440 | tf_op jit(solution)/shard_map/ppermute | solution.py:31
  94.0 2.0 %collective-permute-start.29 = (bf16[256,512]{1,0:T(8,128)(2,1)}, bf16[256,512]{1,0:T(8,128)(2,1)S(1)}, u32[]{:S(2)}, u32[]{:S(2)}) collective-permute-start(bf16[256,512]{1,0:T(8,128)(2,1)} %copy-done.8), channel_id=1, source_target_pairs={{0,16},{1,17},{2,18},{3,19},{4,20},{5,21},{6,22},{7,23},{8,24},{9,... | collective-permute-start | bytes 786440 | tf_op jit(solution)/shard_map/ppermute | solution.py:31
  96.2 1.1 %maximum_convert_fusion = f32[512,512]{1,0:T(8,128)} fusion(bf16[256,512]{1,0:T(8,128)(2,1)S(1)} %get-tuple-element.78, bf16[256,512]{1,0:T(8,128)(2,1)S(1)} %get-tuple-element.77), kind=kLoop, calls=%fused_computation.1 | loop fusion | flops 1048576 | bytes 1572864 | tf_op jit(solution)/shard_map/convert_element_type | solution.py:312
  97.3 3.0 %collective-permute-done.28.refs_2_ = bf16[256,512]{1,0:T(8,128)(2,1)S(1)} collective-permute-done((bf16[256,512]{1,0:T(8,128)(2,1)}, bf16[256,512]{1,0:T(8,128)(2,1)S(1)}, u32[]{:S(2)}, u32[]{:S(2)}) %collective-permute-start.28) | collective-permute-done | bytes 262176 | tf_op jit(solution)/shard_map/ppermute | solution.py:31
  100.2 3.6 %collective-permute-done.29.refs_3_ = bf16[256,512]{1,0:T(8,128)(2,1)S(1)} collective-permute-done((bf16[256,512]{1,0:T(8,128)(2,1)}, bf16[256,512]{1,0:T(8,128)(2,1)S(1)}, u32[]{:S(2)}, u32[]{:S(2)}) %collective-permute-start.29) | collective-permute-done | bytes 262176 | tf_op jit(solution)/shard_map/ppermute | solution.py:31
  103.8 0.8 s5.1
  (68 shorter events, 7.0 us)
Async XLA Ops:
  0.6 1.0 %copy-start = (bf16[512,512]{1,0:T(8,128)(2,1)S(1)}, bf16[512,512]{1,0:T(8,128)(2,1)}, u32[]{:S(2)}) copy-start(bf16[512,512]{1,0:T(8,128)(2,1)} %param.12) | copy-start | bytes 1572868
  0.6 6.8 %copy-start.4 = (s32[16]{0:T(128)S(1)}, s32[16]{0:T(128)}, u32[]{:S(2)}) copy-start(s32[16]{0:T(128)} %constant.80.clone.order_ref) | copy-start | bytes 196
  0.7 6.8 %copy-start.3 = (s32[1,1,4]{2,1,0:T(1,128)S(1)}, s32[1,1,4]{2,1,0:T(1,128)}, u32[]{:S(2)}) copy-start(s32[1,1,4]{2,1,0:T(1,128)} %param.16) | copy-start | bytes 52
  0.7 6.8 %copy-start.2 = (s32[1,1,4,24]{3,2,1,0:T(4,128)S(1)}, s32[1,1,4,24]{3,2,1,0:T(4,128)}, u32[]{:S(2)}) copy-start(s32[1,1,4,24]{3,2,1,0:T(4,128)} %param.15) | copy-start | bytes 1156
  0.7 6.8 %copy-start.1 = (s32[1,1,4,24]{3,2,1,0:T(4,128)S(1)}, s32[1,1,4,24]{3,2,1,0:T(4,128)}, u32[]{:S(2)}) copy-start(s32[1,1,4,24]{3,2,1,0:T(4,128)} %param.14) | copy-start | bytes 1156
  3.2 10.0 %collective-permute-start.4 = (bf16[256,512]{1,0:T(8,128)(2,1)S(1)}, bf16[256,512]{1,0:T(8,128)(2,1)}, u32[]{:S(2)}, u32[]{:S(2)}) collective-permute-start(bf16[256,512]{1,0:T(8,128)(2,1)S(1)} %convolution_convert_fusion), channel_id=1, source_target_pairs={{0,8},{1,9},{2,10},{3,11},{16,24},{17,25},{18,26},{19,27},{32,40},... | collective-permute-start | bytes 786440 | tf_op jit(solution)/shard_map/ppermute | solution.py:31
  4.5 5.6 %collective-permute-start.1 = (bf16[256,512]{1,0:T(8,128)(2,1)S(1)}, bf16[256,512]{1,0:T(8,128)(2,1)S(1)}, u32[]{:S(2)}, u32[]{:S(2)}) collective-permute-start(bf16[256,512]{1,0:T(8,128)(2,1)S(1)} %convolution_convert_fusion), channel_id=1, source_target_pairs={{0,6},{1,7},{2,4},{3,5},{16,22},{17,23},{18,20},{19,21},{32,38},{3... | collective-permute-start | bytes 786440 | tf_op jit(solution)/shard_map/ppermute | solution.py:31
  5.1 4.9 %collective-permute-start = (bf16[256,512]{1,0:T(8,128)(2,1)S(1)}, bf16[256,512]{1,0:T(8,128)(2,1)S(1)}, u32[]{:S(2)}, u32[]{:S(2)}) collective-permute-start(bf16[256,512]{1,0:T(8,128)(2,1)S(1)} %convolution_convert_fusion), channel_id=1, source_target_pairs={{0,2},{1,3},{2,0},{3,1},{16,18},{17,19},{18,16},{19,17},{32,34},{3... | collective-permute-start | bytes 786440 | tf_op jit(solution)/shard_map/ppermute | solution.py:31
  9.9 7.4 %collective-permute-start.8 = (bf16[256,512]{1,0:T(8,128)(2,1)S(1)}, bf16[256,512]{1,0:T(8,128)(2,1)}, u32[]{:S(2)}, u32[]{:S(2)}) collective-permute-start(bf16[256,512]{1,0:T(8,128)(2,1)S(1)} %get-tuple-element.39), channel_id=1, source_target_pairs={{0,1},{1,0},{2,3},{3,2},{4,5},{5,4},{6,7},{7,6},{8,9},{9,8},{10,11... | collective-permute-start | bytes 786440 | tf_op jit(solution)/shard_map/ppermute | solution.py:31
  10.1 15.9 %collective-permute-start.3 = (bf16[256,512]{1,0:T(8,128)(2,1)S(1)}, bf16[256,512]{1,0:T(8,128)(2,1)S(1)}, u32[]{:S(2)}, u32[]{:S(2)}) collective-permute-start(bf16[256,512]{1,0:T(8,128)(2,1)S(1)} %broadcast_select_fusion.2), channel_id=1, source_target_pairs={{0,8},{1,9},{2,10},{3,11},{4,12},{5,13},{6,14},{7,15},{16,24},{17,... | collective-permute-start | bytes 786440 | tf_op jit(solution)/shard_map/ppermute | solution.py:31
  11.4 12.8 %collective-permute-start.2 = (bf16[256,512]{1,0:T(8,128)(2,1)S(1)}, bf16[256,512]{1,0:T(8,128)(2,1)S(1)}, u32[]{:S(2)}, u32[]{:S(2)}) collective-permute-start(bf16[256,512]{1,0:T(8,128)(2,1)S(1)} %collective-permute-done.1), channel_id=1, source_target_pairs={{4,6},{5,7},{6,4},{7,5},{20,22},{21,23},{22,20},{23,21},{36,38},{3... | collective-permute-start | bytes 786440 | tf_op jit(solution)/shard_map/ppermute | solution.py:31
  13.2 11.0 %collective-permute-start.5 = (bf16[256,512]{1,0:T(8,128)(2,1)}, bf16[256,512]{1,0:T(8,128)(2,1)S(1)}, u32[]{:S(2)}, u32[]{:S(2)}) collective-permute-start(bf16[256,512]{1,0:T(8,128)(2,1)} %collective-permute-done.4), channel_id=1, source_target_pairs={{8,12},{9,13},{10,14},{11,15},{24,28},{25,29},{26,30},{27,31},{40,... | collective-permute-start | bytes 786440 | tf_op jit(solution)/shard_map/ppermute | solution.py:31
  18.4 9.4 %collective-permute-start.9 = (bf16[128,512]{1,0:T(8,128)(2,1)S(1)}, bf16[128,512]{1,0:T(8,128)(2,1)S(1)}, u32[]{:S(2)}, u32[]{:S(2)}) collective-permute-start(bf16[128,512]{1,0:T(8,128)(2,1)S(1)} %dynamic-slice_convert_fusion.1), channel_id=1, source_target_pairs={{0,2},{1,3},{2,0},{3,1},{4,6},{5,7},{6,4},{7,5},{8,10},{9,11},{10,... | collective-permute-start | bytes 393224 | tf_op jit(solution)/shard_map/ppermute | solution.py:31
  27.2 1.6 %collective-permute-start.6 = (bf16[256,512]{1,0:T(8,128)(2,1)S(1)}, bf16[256,512]{1,0:T(8,128)(2,1)S(1)}, u32[]{:S(2)}, u32[]{:S(2)}) collective-permute-start(bf16[256,512]{1,0:T(8,128)(2,1)S(1)} %broadcast_select_fusion.4.refs_0_), channel_id=1, source_target_pairs={{0,1},{1,0},{2,3},{3,2},{4,5},{5,4},{6,7},{7,6},{8,9},{9,8},{10,11... | collective-permute-start | bytes 786440 | tf_op jit(solution)/shard_map/ppermute | solution.py:31
  27.3 1.9 %collective-permute-start.7 = (bf16[256,512]{1,0:T(8,128)(2,1)S(1)}, bf16[256,512]{1,0:T(8,128)(2,1)S(1)}, u32[]{:S(2)}, u32[]{:S(2)}) collective-permute-start(bf16[256,512]{1,0:T(8,128)(2,1)S(1)} %get-tuple-element.74.refs_1_), channel_id=1, source_target_pairs={{0,1},{1,0},{2,3},{3,2},{4,5},{5,4},{6,7},{7,6},{8,9},{9,8},{10,11... | collective-permute-start | bytes 786440 | tf_op jit(solution)/shard_map/ppermute | solution.py:31
  29.3 16.3 %copy-start.6 = (bf16[1024,512]{1,0:T(8,128)(2,1)}, bf16[1024,512]{1,0:T(8,128)(2,1)S(1)}, u32[]{:S(2)}) copy-start(bf16[1024,512]{1,0:T(8,128)(2,1)S(1)} %get-tuple-element.40) | copy-start | bytes 3145732
  29.3 13.6 %collective-permute-start.13 = (bf16[128,512]{1,0:T(8,128)(2,1)S(1)}, bf16[128,512]{1,0:T(8,128)(2,1)S(1)}, u32[]{:S(2)}, u32[]{:S(2)}) collective-permute-start(bf16[128,512]{1,0:T(8,128)(2,1)S(1)} %get-tuple-element.52.refs_0_), channel_id=1, source_target_pairs={{0,32},{1,33},{2,34},{3,35},{4,36},{5,37},{6,38},{7,39},{8,40},{9,... | collective-permute-start | bytes 393224 | tf_op jit(solution)/shard_map/ppermute | solution.py:31
  31.3 1.9 %copy-start.5 = (bf16[1,1,4,24,128,128]{5,4,3,2,1,0:T(8,128)(2,1)S(1)}, bf16[1,1,4,24,128,128]{5,4,3,2,1,0:T(8,128)(2,1)}, u32[]{:S(2)}) copy-start(bf16[1,1,4,24,128,128]{5,4,3,2,1,0:T(8,128)(2,1)} %param.13) | copy-start | bytes 9437188
  34.9 14.0 %collective-permute-start.10 = (bf16[256,512]{1,0:T(8,128)(2,1)S(1)}, bf16[256,512]{1,0:T(8,128)(2,1)S(1)}, u32[]{:S(2)}, u32[]{:S(2)}) collective-permute-start(bf16[256,512]{1,0:T(8,128)(2,1)S(1)} %get-tuple-element.46), channel_id=1, source_target_pairs={{0,32},{1,33},{2,34},{3,35},{4,36},{5,37},{6,38},{7,39},{8,40},{9,... | collective-permute-start | bytes 786440 | tf_op jit(solution)/shard_map/ppermute | solution.py:31
  35.2 13.6 %collective-permute-start.12 = (bf16[256,512]{1,0:T(8,128)(2,1)S(1)}, bf16[256,512]{1,0:T(8,128)(2,1)S(1)}, u32[]{:S(2)}, u32[]{:S(2)}) collective-permute-start(bf16[256,512]{1,0:T(8,128)(2,1)S(1)} %get-tuple-element.50), channel_id=1, source_target_pairs={{0,224},{1,225},{2,226},{3,227},{4,228},{5,229},{6,230},{7,231},{8... | collective-permute-start | bytes 786440 | tf_op jit(solution)/shard_map/ppermute | solution.py:31
  40.0 10.1 %collective-permute-start.11 = (bf16[256,512]{1,0:T(8,128)(2,1)S(1)}, bf16[256,512]{1,0:T(8,128)(2,1)S(1)}, u32[]{:S(2)}, u32[]{:S(2)}) collective-permute-start(bf16[256,512]{1,0:T(8,128)(2,1)S(1)} %get-tuple-element.48.refs_2_), channel_id=1, source_target_pairs={{0,16},{1,17},{2,18},{3,19},{4,20},{5,21},{6,22},{7,23},{8,24},{9,... | collective-permute-start | bytes 786440 | tf_op jit(solution)/shard_map/ppermute | solution.py:31
  43.0 5.9 %collective-permute-start.14 = (bf16[64,512]{1,0:T(8,128)(2,1)S(1)}, bf16[64,512]{1,0:T(8,128)(2,1)S(1)}, u32[]{:S(2)}, u32[]{:S(2)}) collective-permute-start(bf16[64,512]{1,0:T(8,128)(2,1)S(1)} %get-tuple-element.85), channel_id=1, source_target_pairs={{0,4},{1,5},{2,6},{3,7},{4,0},{5,1},{6,2},{7,3},{8,12},{9,13},{10,... | collective-permute-start | bytes 196616 | tf_op jit(solution)/shard_map/ppermute | solution.py:31
  50.3 5.9 %collective-permute-start.18 = (bf16[64,512]{1,0:T(8,128)(2,1)S(1)}, bf16[64,512]{1,0:T(8,128)(2,1)S(1)}, u32[]{:S(2)}, u32[]{:S(2)}) collective-permute-start(bf16[64,512]{1,0:T(8,128)(2,1)S(1)} %get-tuple-element.57), channel_id=1, source_target_pairs={{0,64},{1,65},{2,66},{3,67},{4,68},{5,69},{6,70},{7,71},{8,72},{9,... | collective-permute-start | bytes 196616 | tf_op jit(solution)/shard_map/ppermute | solution.py:31
  50.4 15.7 %collective-permute-start.16 = (bf16[384,512]{1,0:T(8,128)(2,1)S(1)}, bf16[384,512]{1,0:T(8,128)(2,1)S(1)}, u32[]{:S(2)}, u32[]{:S(2)}) collective-permute-start(bf16[384,512]{1,0:T(8,128)(2,1)S(1)} %get-tuple-element.54), channel_id=1, source_target_pairs={{0,32},{1,33},{2,34},{3,35},{4,36},{5,37},{6,38},{7,39},{8,40},{9,... | collective-permute-start | bytes 1179656 | tf_op jit(solution)/shard_map/ppermute | solution.py:31
  52.7 13.3 %collective-permute-start.17 = (bf16[384,512]{1,0:T(8,128)(2,1)S(1)}, bf16[384,512]{1,0:T(8,128)(2,1)S(1)}, u32[]{:S(2)}, u32[]{:S(2)}) collective-permute-start(bf16[384,512]{1,0:T(8,128)(2,1)S(1)} %get-tuple-element.56), channel_id=1, source_target_pairs={{0,224},{1,225},{2,226},{3,227},{4,228},{5,229},{6,230},{7,231},{8... | collective-permute-start | bytes 1179656 | tf_op jit(solution)/shard_map/ppermute | solution.py:31
  53.7 14.3 %collective-permute-start.15 = (bf16[512,512]{1,0:T(8,128)(2,1)S(1)}, bf16[512,512]{1,0:T(8,128)(2,1)S(1)}, u32[]{:S(2)}, u32[]{:S(2)}) collective-permute-start(bf16[512,512]{1,0:T(8,128)(2,1)S(1)} %get-tuple-element.53), channel_id=1, source_target_pairs={{0,16},{1,17},{2,18},{3,19},{4,20},{5,21},{6,22},{7,23},{8,24},{9,... | collective-permute-start | bytes 1572872 | tf_op jit(solution)/shard_map/ppermute | solution.py:31
  56.2 9.9 %collective-permute-start.19 = (bf16[64,512]{1,0:T(8,128)(2,1)S(1)}, bf16[64,512]{1,0:T(8,128)(2,1)S(1)}, u32[]{:S(2)}, u32[]{:S(2)}) collective-permute-start(bf16[64,512]{1,0:T(8,128)(2,1)S(1)} %add_convert_fusion.1.refs_5_), channel_id=1, source_target_pairs={{0,128},{1,129},{2,130},{3,131},{4,132},{5,133},{6,134},{7,135},{8... | collective-permute-start | bytes 196616 | tf_op jit(solution)/shard_map/ppermute | solution.py:31
  60.5 1.2 %copy-start.7 = (bf16[1024,512]{1,0:T(8,128)(2,1)S(1)}, bf16[1024,512]{1,0:T(8,128)(2,1)}, u32[]{:S(2)}) copy-start(bf16[1024,512]{1,0:T(8,128)(2,1)} %copy-done.6) | copy-start | bytes 3145732
  68.2 10.4 %collective-permute-start.20 = (bf16[256,512]{1,0:T(8,128)(2,1)S(1)}, bf16[256,512]{1,0:T(8,128)(2,1)S(1)}, u32[]{:S(2)}, u32[]{:S(2)}) collective-permute-start(bf16[256,512]{1,0:T(8,128)(2,1)S(1)} %get-tuple-element.58), channel_id=1, source_target_pairs={{0,32},{1,33},{2,34},{3,35},{4,36},{5,37},{6,38},{7,39},{8,40},{9,... | collective-permute-start | bytes 786440 | tf_op jit(solution)/shard_map/ppermute | solution.py:31
  69.9 8.6 %collective-permute-start.21 = (bf16[256,512]{1,0:T(8,128)(2,1)S(1)}, bf16[256,512]{1,0:T(8,128)(2,1)S(1)}, u32[]{:S(2)}, u32[]{:S(2)}) collective-permute-start(bf16[256,512]{1,0:T(8,128)(2,1)S(1)} %get-tuple-element.60), channel_id=1, source_target_pairs={{0,224},{1,225},{2,226},{3,227},{4,228},{5,229},{6,230},{7,231},{8... | collective-permute-start | bytes 786440 | tf_op jit(solution)/shard_map/ppermute | solution.py:31
  71.5 4.3 %collective-permute-start.24 = (bf16[64,512]{1,0:T(8,128)(2,1)S(1)}, bf16[64,512]{1,0:T(8,128)(2,1)S(1)}, u32[]{:S(2)}, u32[]{:S(2)}) collective-permute-start(bf16[64,512]{1,0:T(8,128)(2,1)S(1)} %get-tuple-element.61.refs_4_), channel_id=1, source_target_pairs={{0,24},{1,25},{2,26},{3,27},{4,28},{5,29},{6,30},{7,31},{8,16},{9,... | collective-permute-start | bytes 196616 | tf_op jit(solution)/shard_map/ppermute | solution.py:31
  71.5 5.8 %collective-permute-start.23 = (bf16[64,512]{1,0:T(8,128)(2,1)S(1)}, bf16[64,512]{1,0:T(8,128)(2,1)S(1)}, u32[]{:S(2)}, u32[]{:S(2)}) collective-permute-start(bf16[64,512]{1,0:T(8,128)(2,1)S(1)} %get-tuple-element.61.refs_4_), channel_id=1, source_target_pairs={{0,16},{1,17},{2,18},{3,19},{4,20},{5,21},{6,22},{7,23},{8,24},{9,... | collective-permute-start | bytes 196616 | tf_op jit(solution)/shard_map/ppermute | solution.py:31
  73.1 5.5 %collective-permute-start.22 = (bf16[64,512]{1,0:T(8,128)(2,1)S(1)}, bf16[64,512]{1,0:T(8,128)(2,1)S(1)}, u32[]{:S(2)}, u32[]{:S(2)}) collective-permute-start(bf16[64,512]{1,0:T(8,128)(2,1)S(1)} %get-tuple-element.61.refs_4_), channel_id=1, source_target_pairs={{0,8},{1,9},{2,10},{3,11},{4,12},{5,13},{6,14},{7,15},{8,0},{9,1},... | collective-permute-start | bytes 196616 | tf_op jit(solution)/shard_map/ppermute | solution.py:31
  79.4 7.8 %collective-permute-start.25 = (bf16[256,512]{1,0:T(8,128)(2,1)}, bf16[256,512]{1,0:T(8,128)(2,1)S(1)}, u32[]{:S(2)}, u32[]{:S(2)}) collective-permute-start(bf16[256,512]{1,0:T(8,128)(2,1)} %get-tuple-element.62), channel_id=1, source_target_pairs={{0,32},{1,33},{2,34},{3,35},{4,36},{5,37},{6,38},{7,39},{8,40},{9,... | collective-permute-start | bytes 786440 | tf_op jit(solution)/shard_map/ppermute | solution.py:31
  79.8 7.4 %collective-permute-start.26 = (bf16[256,512]{1,0:T(8,128)(2,1)}, bf16[256,512]{1,0:T(8,128)(2,1)S(1)}, u32[]{:S(2)}, u32[]{:S(2)}) collective-permute-start(bf16[256,512]{1,0:T(8,128)(2,1)} %get-tuple-element.64), channel_id=1, source_target_pairs={{0,224},{1,225},{2,226},{3,227},{4,228},{5,229},{6,230},{7,231},{8... | collective-permute-start | bytes 786440 | tf_op jit(solution)/shard_map/ppermute | solution.py:31
  82.7 5.5 %collective-permute-start.32 = (bf16[64,512]{1,0:T(8,128)(2,1)S(1)}, bf16[64,512]{1,0:T(8,128)(2,1)S(1)}, u32[]{:S(2)}, u32[]{:S(2)}) collective-permute-start(bf16[64,512]{1,0:T(8,128)(2,1)S(1)} %get-tuple-element.69.refs_0_), channel_id=1, source_target_pairs={{0,6},{1,7},{2,4},{3,5},{4,2},{5,3},{6,0},{7,1},{8,14},{9,15},{10,... | collective-permute-start | bytes 196616 | tf_op jit(solution)/shard_map/ppermute | solution.py:31
  84.7 5.8 %collective-permute-start.31 = (bf16[64,512]{1,0:T(8,128)(2,1)S(1)}, bf16[64,512]{1,0:T(8,128)(2,1)S(1)}, u32[]{:S(2)}, u32[]{:S(2)}) collective-permute-start(bf16[64,512]{1,0:T(8,128)(2,1)S(1)} %get-tuple-element.69.refs_0_), channel_id=1, source_target_pairs={{0,4},{1,5},{2,6},{3,7},{4,0},{5,1},{6,2},{7,3},{8,12},{9,13},{10,... | collective-permute-start | bytes 196616 | tf_op jit(solution)/shard_map/ppermute | solution.py:31
  84.7 5.8 %collective-permute-start.30 = (bf16[64,512]{1,0:T(8,128)(2,1)S(1)}, bf16[64,512]{1,0:T(8,128)(2,1)S(1)}, u32[]{:S(2)}, u32[]{:S(2)}) collective-permute-start(bf16[64,512]{1,0:T(8,128)(2,1)S(1)} %get-tuple-element.69.refs_0_), channel_id=1, source_target_pairs={{0,2},{1,3},{2,0},{3,1},{4,6},{5,7},{6,4},{7,5},{8,10},{9,11},{10,... | collective-permute-start | bytes 196616 | tf_op jit(solution)/shard_map/ppermute | solution.py:31
  87.4 3.0 %copy-start.8 = (bf16[256,512]{1,0:T(8,128)(2,1)}, bf16[256,512]{1,0:T(8,128)(2,1)S(1)}, u32[]{:S(2)}) copy-start(bf16[256,512]{1,0:T(8,128)(2,1)S(1)} %get-tuple-element.68) | copy-start | bytes 786436
  87.4 3.0 %copy-start.9 = (bf16[256,512]{1,0:T(8,128)(2,1)}, bf16[256,512]{1,0:T(8,128)(2,1)S(1)}, u32[]{:S(2)}) copy-start(bf16[256,512]{1,0:T(8,128)(2,1)S(1)} %get-tuple-element.67) | copy-start | bytes 786436
  90.6 5.4 %collective-permute-start.33 = (bf16[256,512]{1,0:T(8,128)(2,1)S(1)}, bf16[256,512]{1,0:T(8,128)(2,1)S(1)}, u32[]{:S(2)}, u32[]{:S(2)}) collective-permute-start(bf16[256,512]{1,0:T(8,128)(2,1)S(1)} %pad_maximum_fusion), channel_id=1, source_target_pairs={{0,1},{1,0},{2,3},{3,2},{4,5},{5,4},{6,7},{7,6},{8,9},{9,8},{10,11... | collective-permute-start | bytes 786440 | tf_op jit(solution)/shard_map/ppermute | solution.py:31
  90.7 13.1 %collective-permute-start.27 = (bf16[256,512]{1,0:T(8,128)(2,1)S(1)}, bf16[256,512]{1,0:T(8,128)(2,1)S(1)}, u32[]{:S(2)}, u32[]{:S(2)}) collective-permute-start(bf16[256,512]{1,0:T(8,128)(2,1)S(1)} %get-tuple-element.66.refs_4_), channel_id=1, source_target_pairs={{0,32},{1,33},{2,34},{3,35},{4,36},{5,37},{6,38},{7,39},{8,40},{9,... | collective-permute-start | bytes 786440 | tf_op jit(solution)/shard_map/ppermute | solution.py:31
  90.8 9.4 %collective-permute-start.28 = (bf16[256,512]{1,0:T(8,128)(2,1)}, bf16[256,512]{1,0:T(8,128)(2,1)S(1)}, u32[]{:S(2)}, u32[]{:S(2)}) collective-permute-start(bf16[256,512]{1,0:T(8,128)(2,1)} %copy-done.9), channel_id=1, source_target_pairs={{0,224},{1,225},{2,226},{3,227},{4,228},{5,229},{6,230},{7,231},{8... | collective-permute-start | bytes 786440 | tf_op jit(solution)/shard_map/ppermute | solution.py:31
  94.0 9.8 %collective-permute-start.29 = (bf16[256,512]{1,0:T(8,128)(2,1)}, bf16[256,512]{1,0:T(8,128)(2,1)S(1)}, u32[]{:S(2)}, u32[]{:S(2)}) collective-permute-start(bf16[256,512]{1,0:T(8,128)(2,1)} %copy-done.8), channel_id=1, source_target_pairs={{0,16},{1,17},{2,18},{3,19},{4,20},{5,21},{6,22},{7,23},{8,24},{9,... | collective-permute-start | bytes 786440 | tf_op jit(solution)/shard_map/ppermute | solution.py:31

commit v5 on v4

--- a/solution.py
+++ b/solution.py
@@ -182,7 +182,16 @@
             at += count
 
 
-def stage(name, *outputs, anchors=()):
+def collect_kernel(plans, n_in, pieces, *refs):
+    stage_kernel(plans, n_in, pieces, *refs[:-1])
+    y = lax.rem(lax.axis_index("rep") // 2, 4)
+    for step in range(pieces):
+        owner = y ^ step
+        start = pl.multiple_of((owner & 1) * 128 + (owner >> 1) * 64, 64)
+        refs[-1][pl.ds(start, 64), :] = refs[n_in + step][...]
+
+
+def stage(name, *outputs, anchors=(), collect=False):
     arrays, plans, shapes = [], [], []
     for segments in outputs:
         planned = []
@@ -198,9 +207,11 @@
             planned.append((count, tuple(numbered)))
         plans.append(tuple(planned))
         shapes.append(jax.ShapeDtypeStruct((sum(count for count, _ in planned), 512), jnp.bfloat16))
+    if collect:
+        shapes.append(jax.ShapeDtypeStruct((256, 512), jnp.bfloat16))
     vmem, anywhere = pl.BlockSpec(memory_space=pltpu.VMEM), pl.BlockSpec(memory_space=pl.ANY)
     return pl.pallas_call(
-        functools.partial(stage_kernel, tuple(plans), len(arrays), len(anchors)),
+        functools.partial(collect_kernel if collect else stage_kernel, tuple(plans), len(arrays), len(anchors)),
         out_shape=shapes,
         in_specs=[vmem] * len(arrays) + [anywhere if anchor.dtype == jnp.int32 else vmem for anchor in anchors],
         out_specs=[vmem] * len(shapes),
@@ -300,11 +311,14 @@
 
     up_got, down_got = send(to_up, up), send(to_down, down)
     w_got = [send(w, flipped("y", step)) for step in (1, 2, 3)]
-    to_up, to_down, crossing = stage(
-        "s4", [(256, m1, up_got)], [(256, m7, down_got)], [(256, t0, up_t, down_t)]
+    to_up, to_down, crossing, w = stage(
+        "s4",
+        [(256, m1, up_got)],
+        [(256, m7, down_got)],
+        [(256, t0, up_t, down_t)],
+        anchors=(w, *w_got),
+        collect=True,
     )
-    w = stage("v5", *[[(64, piece)] for piece in (w, *w_got)], anchors=(to_up,))
-    w = joined(y % 2, joined(y // 2, w[0], w[2]), joined(y // 2, w[1], w[3]))
 
     up_got, down_got, crossed = send(to_up, up), send(to_down, down), send(crossing, cross)
     w_got = send(w, other)

time: 105 us -> 105 us (level)
  starting transfers between devices: 50.2 us -> 52 us
  waiting for transfers between devices: 30.8 us -> 29.4 us
  local copies, waits for them, and re-layouts: 4.23 us -> 2.99 us
    ppermute x34, starting transfers between devices: 50.2 us -> 52 us  [send(): return lax.ppermute(value, AXES, pairs(move))]
    ppermute x34, waiting for transfers between devices: 30.8 us -> 29.4 us  [send(): return lax.ppermute(value, AXES, pairs(move))]
    unnamed x20 -> x12, local copies, waits for them, and re-layouts: 4.15 us -> 2.91 us
    pallas_call x8 -> x7, Pallas kernels: 2.43 us -> 1.7 us  [stage(): pl.pallas_call(functools.partial(collect_kernel if collect else stage_ker...]
  transfers between devices with their start and end apart: 34 -> 34, of which waited for: 18 -> 16; matrix products, arithmetic and copies ran while one was open for 5% -> 5% of each run, Pallas kernels for 9% -> 10%
where the time goes in v5:
time: 105 us; the launch traced here: 104 us
  starting transfers between devices  52 us (50%)
  waiting for transfers between devices  29.4 us (28%)
  Pallas kernels  11.9 us (11%)
  other arithmetic  3.36 us (3%)
  matrix products  3 us (3%)
  local copies, waits for them, and re-layouts  2.99 us (3%)
  between operations  1.07 us (1%)
    ppermute x34, starting transfers between devices, send(): return lax.ppermute(value, AXES, pairs(move))  52 us
    ppermute x34, waiting for transfers between devices, send(): return lax.ppermute(value, AXES, pairs(move))  29.4 us
    pallas_call x3, Pallas kernels, rows(): pl.pallas_call(functools.partial(rows_kernel, base, tuple(sizes)), out_sh...  7.76 us
    unnamed x12, local copies, waits for them, and re-layouts  2.91 us
    pallas_call x1, Pallas kernels, plan(): pl.pallas_call(plan_kernel, out_shape=[jax.ShapeDtypeStruct((SPARE + 1, 1...  2.4 us
  transfers between devices with their start and end apart: 34, of which 16 were waited for; matrix products, arithmetic and copies ran while one was open for 5% of the time, Pallas kernels for 10%

profile of v5, /device:TPU:2, one launch (start us, length us, event | category | flops | bytes accessed | tf_op | source)
XLA Modules:
  0.0 103.7 jit_solution(8205844121811693754)
XLA Ops:
  0.7 1.0 copy-done
  1.7 1.5 %convolution_convert_fusion = bf16[256,512]{1,0:T(8,128)(2,1)S(1)} fusion(bf16[512,512]{1,0:T(8,128)(2,1)S(1)} %copy-done, bf16[256,512]{1,0:T(8,128)(2,1)} %param.9, s32[256,512]{1,0:T(8,128)} %param.10), kind=kOutput, calls=%fused_computation | convolution fusion | flops 134610944 | bytes 1572864 | tf_op jit(solution)/shard_map/dot_general | solution.py:262
  3.2 1.3 %collective-permute-start.4 = (bf16[256,512]{1,0:T(8,128)(2,1)S(1)}, bf16[256,512]{1,0:T(8,128)(2,1)}, u32[]{:S(2)}, u32[]{:S(2)}) collective-permute-start(bf16[256,512]{1,0:T(8,128)(2,1)S(1)} %convolution_convert_fusion), channel_id=1, source_target_pairs={{0,8},{1,9},{2,10},{3,11},{16,24},{17,25},{18,26},{19,27},{32,40},... | collective-permute-start | bytes 786440 | tf_op jit(solution)/shard_map/ppermute | solution.py:31
  5.1 0.7 collective-permute-start
  5.8 1.5 %fusion.1 = f32[512,512]{0,1:T(8,128)S(1)} fusion(bf16[256,512]{1,0:T(8,128)(2,1)} %param.11, bf16[256,512]{1,0:T(8,128)(2,1)} %param.9, s32[256,512]{1,0:T(8,128)} %param.10), kind=kOutput, calls=%fused_computation.18 | convolution fusion | flops 134479872 | bytes 2097152 | tf_op jit(solution)/shard_map/dot_general | solution.py:265
  7.5 2.4 %plan.1 = (s32[33,16]{1,0:T(8,128)S(1)}, bf16[256,512]{1,0:T(8,128)(2,1)S(1)}) custom-call(s32[4,24]{1,0:T(4,128)S(1)} %bitcast.11, s32[4,24]{1,0:T(4,128)S(1)} %bitcast.12, s32[4]{0:T(128)S(1)} %bitcast.13, s32[16]{0:T(128)S(1)} %copy-done.4, bf16[256,512]{1,0:T(8,128)(2,1)S(1)} %fusion.given_ref), custom_call_target="tpu_custom_call" | custom-call | tf_op jit(solution)/shard_map/plan/pallas_call | solution.py:107
  10.1 1.3 %collective-permute-start.3 = (bf16[256,512]{1,0:T(8,128)(2,1)S(1)}, bf16[256,512]{1,0:T(8,128)(2,1)S(1)}, u32[]{:S(2)}, u32[]{:S(2)}) collective-permute-start(bf16[256,512]{1,0:T(8,128)(2,1)S(1)} %broadcast_select_fusion.2), channel_id=1, source_target_pairs={{0,8},{1,9},{2,10},{3,11},{4,12},{5,13},{6,14},{7,15},{16,24},{17,... | collective-permute-start | bytes 786440 | tf_op jit(solution)/shard_map/ppermute | solution.py:31
  11.4 0.7 collective-permute-start.2
  12.1 1.1 %collective-permute-done.4 = bf16[256,512]{1,0:T(8,128)(2,1)} collective-permute-done((bf16[256,512]{1,0:T(8,128)(2,1)S(1)}, bf16[256,512]{1,0:T(8,128)(2,1)}, u32[]{:S(2)}, u32[]{:S(2)}) %collective-permute-start.4) | collective-permute-done | bytes 262176 | tf_op jit(solution)/shard_map/ppermute | solution.py:31
  13.2 4.1 %collective-permute-start.5 = (bf16[256,512]{1,0:T(8,128)(2,1)}, bf16[256,512]{1,0:T(8,128)(2,1)S(1)}, u32[]{:S(2)}, u32[]{:S(2)}) collective-permute-start(bf16[256,512]{1,0:T(8,128)(2,1)} %collective-permute-done.4), channel_id=1, source_target_pairs={{8,12},{9,13},{10,14},{11,15},{24,28},{25,29},{26,30},{27,31},{40,... | collective-permute-start | bytes 786440 | tf_op jit(solution)/shard_map/ppermute | solution.py:31
  17.3 1.0 bitcast_add_fusion
  18.4 0.8 collective-permute-start.9
  19.1 5.1 %collective-permute-done.5 = bf16[256,512]{1,0:T(8,128)(2,1)S(1)} collective-permute-done((bf16[256,512]{1,0:T(8,128)(2,1)}, bf16[256,512]{1,0:T(8,128)(2,1)S(1)}, u32[]{:S(2)}, u32[]{:S(2)}) %collective-permute-start.5) | collective-permute-done | bytes 262176 | tf_op jit(solution)/shard_map/ppermute | solution.py:31
  24.2 1.9 %collective-permute-done.3 = bf16[256,512]{1,0:T(8,128)(2,1)S(1)} collective-permute-done((bf16[256,512]{1,0:T(8,128)(2,1)S(1)}, bf16[256,512]{1,0:T(8,128)(2,1)S(1)}, u32[]{:S(2)}, u32[]{:S(2)}) %collective-permute-start.3) | collective-permute-done | bytes 262176 | tf_op jit(solution)/shard_map/ppermute | solution.py:31
  26.1 1.1 %broadcast_select_fusion.3 = (bf16[256,512]{1,0:T(8,128)(2,1)S(1)}, bf16[256,512]{1,0:T(8,128)(2,1)S(1)}, bf16[256,512]{1,0:T(8,128)(2,1)S(1)}) fusion(pred[]{:T(512)S(6)} %or.3, bf16[256,512]{1,0:T(8,128)(2,1)} %collective-permute-done.4, bf16[256,512]{1,0:T(8,128)(2,1)S(1)} %collective-permute-done.3, bf16[256,512]{1,0:T(8,128)(2,1)S(1)} %convolution_convert_fusion, ...), kind=kLoop, calls=%fused_computation.13 | loop fusion | flops 917504 | bytes 2621443 | tf_op jit(solution)/shard_map/jit(_where)/select_n | solution.py:277
  27.8 1.0 collective-permute-done.6.refs_2_
  29.3 2.0 %collective-permute-start.13 = (bf16[128,512]{1,0:T(8,128)(2,1)S(1)}, bf16[128,512]{1,0:T(8,128)(2,1)S(1)}, u32[]{:S(2)}, u32[]{:S(2)}) collective-permute-start(bf16[128,512]{1,0:T(8,128)(2,1)S(1)} %get-tuple-element.49.refs_0_), channel_id=1, source_target_pairs={{0,32},{1,33},{2,34},{3,35},{4,36},{5,37},{6,38},{7,39},{8,40},{9,... | collective-permute-start | bytes 393224 | tf_op jit(solution)/shard_map/ppermute | solution.py:31
  31.3 1.9 %copy-done.5 = bf16[1,1,4,24,128,128]{5,4,3,2,1,0:T(8,128)(2,1)S(1)} copy-done((bf16[1,1,4,24,128,128]{5,4,3,2,1,0:T(8,128)(2,1)S(1)}, bf16[1,1,4,24,128,128]{5,4,3,2,1,0:T(8,128)(2,1)}, u32[]{:S(2)}) %copy-start.5) | copy-done | bytes 3145752
  33.2 1.7 %rows_first.1 = (bf16[256,512]{1,0:T(8,128)(2,1)S(1)}, bf16[256,512]{1,0:T(8,128)(2,1)S(1)}, bf16[256,512]{1,0:T(8,128)(2,1)S(1)}) custom-call(s32[33,16]{1,0:T(8,128)S(1)} %get-tuple-element.35.table_ref, bf16[96,128,128]{2,1,0:T(8,128)(2,1)S(1)} %bitcast.14, bf16[8,128,512]{2,1,0:T(8,128)(2,1)S(1)} %bitcast.17), custom_call_target="tpu_custom_call" | custom-call | flops 1200000000 | bytes 1000000 | tf_op jit(solution)/shard_map/rows_first/pallas_call | solution.py:161
  34.8 0.7 collective-permute-start.10
  35.6 4.7 %collective-permute-start.12 = (bf16[256,512]{1,0:T(8,128)(2,1)S(1)}, bf16[256,512]{1,0:T(8,128)(2,1)S(1)}, u32[]{:S(2)}, u32[]{:S(2)}) collective-permute-start(bf16[256,512]{1,0:T(8,128)(2,1)S(1)} %get-tuple-element.47), channel_id=1, source_target_pairs={{0,224},{1,225},{2,226},{3,227},{4,228},{5,229},{6,230},{7,231},{8... | collective-permute-start | bytes 786440 | tf_op jit(solution)/shard_map/ppermute | solution.py:31
  40.2 2.2 %collective-permute-start.11 = (bf16[256,512]{1,0:T(8,128)(2,1)S(1)}, bf16[256,512]{1,0:T(8,128)(2,1)S(1)}, u32[]{:S(2)}, u32[]{:S(2)}) collective-permute-start(bf16[256,512]{1,0:T(8,128)(2,1)S(1)} %get-tuple-element.45.refs_2_), channel_id=1, source_target_pairs={{0,16},{1,17},{2,18},{3,19},{4,20},{5,21},{6,22},{7,23},{8,24},{9,... | collective-permute-start | bytes 786440 | tf_op jit(solution)/shard_map/ppermute | solution.py:31
  42.5 1.4 %collective-permute-start.14 = (bf16[64,512]{1,0:T(8,128)(2,1)S(1)}, bf16[64,512]{1,0:T(8,128)(2,1)S(1)}, u32[]{:S(2)}, u32[]{:S(2)}) collective-permute-start(bf16[64,512]{1,0:T(8,128)(2,1)S(1)} %get-tuple-element.73), channel_id=1, source_target_pairs={{0,4},{1,5},{2,6},{3,7},{4,0},{5,1},{6,2},{7,3},{8,12},{9,13},{10,... | collective-permute-start | bytes 196616 | tf_op jit(solution)/shard_map/ppermute | solution.py:31
  43.9 2.3 %rows_second.1 = (bf16[512,512]{1,0:T(8,128)(2,1)S(1)}, bf16[256,512]{1,0:T(8,128)(2,1)S(1)}, bf16[256,512]{1,0:T(8,128)(2,1)S(1)}, bf16[256,512]{1,0:T(8,128)(2,1)S(1)}) custom-call(s32[33,16]{1,0:T(8,128)S(1)} %get-tuple-element.35.table_ref, bf16[96,128,128]{2,1,0:T(8,128)(2,1)S(1)} %bitcast.15, bf16[8,128,512]{2,1,0:T(8,128)(2,1)S(1)} %bitcast.18), custom_call_target="tpu_custom_call" | custom-call | flops 2000000000 | bytes 1000000 | tf_op jit(solution)/shard_map/rows_second/pallas_call | solution.py:161
  46.1 2.2 %collective-permute-done.14.refs_8_ = bf16[64,512]{1,0:T(8,128)(2,1)S(1)} collective-permute-done((bf16[64,512]{1,0:T(8,128)(2,1)S(1)}, bf16[64,512]{1,0:T(8,128)(2,1)S(1)}, u32[]{:S(2)}, u32[]{:S(2)}) %collective-permute-start.14) | collective-permute-done | bytes 65568 | tf_op jit(solution)/shard_map/ppermute | solution.py:31
  48.3 1.2 %collective-permute-done.11.refs_3_ = bf16[256,512]{1,0:T(8,128)(2,1)S(1)} collective-permute-done((bf16[256,512]{1,0:T(8,128)(2,1)S(1)}, bf16[256,512]{1,0:T(8,128)(2,1)S(1)}, u32[]{:S(2)}, u32[]{:S(2)}) %collective-permute-start.11) | collective-permute-done | bytes 262176 | tf_op jit(solution)/shard_map/ppermute | solution.py:31
  49.8 2.9 %collective-permute-start.16 = (bf16[384,512]{1,0:T(8,128)(2,1)S(1)}, bf16[384,512]{1,0:T(8,128)(2,1)S(1)}, u32[]{:S(2)}, u32[]{:S(2)}) collective-permute-start(bf16[384,512]{1,0:T(8,128)(2,1)S(1)} %get-tuple-element.51), channel_id=1, source_target_pairs={{0,32},{1,33},{2,34},{3,35},{4,36},{5,37},{6,38},{7,39},{8,40},{9,... | collective-permute-start | bytes 1179656 | tf_op jit(solution)/shard_map/ppermute | solution.py:31
  53.2 2.7 %collective-permute-start.15 = (bf16[512,512]{1,0:T(8,128)(2,1)S(1)}, bf16[512,512]{1,0:T(8,128)(2,1)S(1)}, u32[]{:S(2)}, u32[]{:S(2)}) collective-permute-start(bf16[512,512]{1,0:T(8,128)(2,1)S(1)} %get-tuple-element.50), channel_id=1, source_target_pairs={{0,16},{1,17},{2,18},{3,19},{4,20},{5,21},{6,22},{7,23},{8,24},{9,... | collective-permute-start | bytes 1572872 | tf_op jit(solution)/shard_map/ppermute | solution.py:31
  55.9 4.7 %collective-permute-start.19 = (bf16[64,512]{1,0:T(8,128)(2,1)S(1)}, bf16[64,512]{1,0:T(8,128)(2,1)S(1)}, u32[]{:S(2)}, u32[]{:S(2)}) collective-permute-start(bf16[64,512]{1,0:T(8,128)(2,1)S(1)} %add_convert_fusion.1.refs_5_), channel_id=1, source_target_pairs={{0,128},{1,129},{2,130},{3,131},{4,132},{5,133},{6,134},{7,135},{8... | collective-permute-start | bytes 196616 | tf_op jit(solution)/shard_map/ppermute | solution.py:31
  60.5 3.8 %rows_third.1 = (bf16[256,512]{1,0:T(8,128)(2,1)S(1)}, bf16[256,512]{1,0:T(8,128)(2,1)S(1)}, bf16[256,512]{1,0:T(8,128)(2,1)S(1)}, bf16[256,512]{1,0:T(8,128)(2,...) custom-call(s32[33,16]{1,0:T(8,128)S(1)} %get-tuple-element.35.table, ...), custom_call_target="tpu_custom_call" | custom-call | flops 3200000000 | bytes 1000000 | tf_op jit(solution)/shard_map/rows_third/pallas_call | solution.py:161
  64.3 2.3 %collective-permute-done.19.refs_6_ = bf16[64,512]{1,0:T(8,128)(2,1)S(1)} collective-permute-done((bf16[64,512]{1,0:T(8,128)(2,1)S(1)}, bf16[64,512]{1,0:T(8,128)(2,1)S(1)}, u32[]{:S(2)}, u32[]{:S(2)}) %collective-permute-start.19) | collective-permute-done | bytes 65568 | tf_op jit(solution)/shard_map/ppermute | solution.py:31
  67.2 3.0 %collective-permute-start.20 = (bf16[256,512]{1,0:T(8,128)(2,1)S(1)}, bf16[256,512]{1,0:T(8,128)(2,1)S(1)}, u32[]{:S(2)}, u32[]{:S(2)}) collective-permute-start(bf16[256,512]{1,0:T(8,128)(2,1)S(1)} %get-tuple-element.55), channel_id=1, source_target_pairs={{0,32},{1,33},{2,34},{3,35},{4,36},{5,37},{6,38},{7,39},{8,40},{9,... | collective-permute-start | bytes 786440 | tf_op jit(solution)/shard_map/ppermute | solution.py:31
  70.5 2.8 %collective-permute-start.23 = (bf16[64,512]{1,0:T(8,128)(2,1)S(1)}, bf16[64,512]{1,0:T(8,128)(2,1)S(1)}, u32[]{:S(2)}, u32[]{:S(2)}) collective-permute-start(bf16[64,512]{1,0:T(8,128)(2,1)S(1)} %get-tuple-element.58.refs_4_), channel_id=1, source_target_pairs={{0,16},{1,17},{2,18},{3,19},{4,20},{5,21},{6,22},{7,23},{8,24},{9,... | collective-permute-start | bytes 196616 | tf_op jit(solution)/shard_map/ppermute | solution.py:31
  73.3 1.3 %collective-permute-start.22 = (bf16[64,512]{1,0:T(8,128)(2,1)S(1)}, bf16[64,512]{1,0:T(8,128)(2,1)S(1)}, u32[]{:S(2)}, u32[]{:S(2)}) collective-permute-start(bf16[64,512]{1,0:T(8,128)(2,1)S(1)} %get-tuple-element.58.refs_4_), channel_id=1, source_target_pairs={{0,8},{1,9},{2,10},{3,11},{4,12},{5,13},{6,14},{7,15},{8,0},{9,1},... | collective-permute-start | bytes 196616 | tf_op jit(solution)/shard_map/ppermute | solution.py:31
  74.8 1.5 %collective-permute-done.23.refs_6_ = bf16[64,512]{1,0:T(8,128)(2,1)S(1)} collective-permute-done((bf16[64,512]{1,0:T(8,128)(2,1)S(1)}, bf16[64,512]{1,0:T(8,128)(2,1)S(1)}, u32[]{:S(2)}, u32[]{:S(2)}) %collective-permute-start.23) | collective-permute-done | bytes 65568 | tf_op jit(solution)/shard_map/ppermute | solution.py:31
  76.3 1.3 %collective-permute-done.22.refs_5_ = bf16[64,512]{1,0:T(8,128)(2,1)S(1)} collective-permute-done((bf16[64,512]{1,0:T(8,128)(2,1)S(1)}, bf16[64,512]{1,0:T(8,128)(2,1)S(1)}, u32[]{:S(2)}, u32[]{:S(2)}) %collective-permute-start.22) | collective-permute-done | bytes 65568 | tf_op jit(solution)/shard_map/ppermute | solution.py:31
  77.8 1.7 %collective-permute-start.25 = (bf16[256,512]{1,0:T(8,128)(2,1)S(1)}, bf16[256,512]{1,0:T(8,128)(2,1)S(1)}, u32[]{:S(2)}, u32[]{:S(2)}) collective-permute-start(bf16[256,512]{1,0:T(8,128)(2,1)S(1)} %get-tuple-element.59), channel_id=1, source_target_pairs={{0,32},{1,33},{2,34},{3,35},{4,36},{5,37},{6,38},{7,39},{8,40},{9,... | collective-permute-start | bytes 786440 | tf_op jit(solution)/shard_map/ppermute | solution.py:31
  79.5 1.6 %collective-permute-start.26 = (bf16[256,512]{1,0:T(8,128)(2,1)S(1)}, bf16[256,512]{1,0:T(8,128)(2,1)S(1)}, u32[]{:S(2)}, u32[]{:S(2)}) collective-permute-start(bf16[256,512]{1,0:T(8,128)(2,1)S(1)} %get-tuple-element.61), channel_id=1, source_target_pairs={{0,224},{1,225},{2,226},{3,227},{4,228},{5,229},{6,230},{7,231},{8... | collective-permute-start | bytes 786440 | tf_op jit(solution)/shard_map/ppermute | solution.py:31
  81.1 2.8 %collective-permute-start.29 = (bf16[64,512]{1,0:T(8,128)(2,1)S(1)}, bf16[64,512]{1,0:T(8,128)(2,1)S(1)}, u32[]{:S(2)}, u32[]{:S(2)}) collective-permute-start(bf16[64,512]{1,0:T(8,128)(2,1)S(1)} %get-tuple-element.63.refs_7_), channel_id=1, source_target_pairs={{0,6},{1,7},{2,4},{3,5},{4,2},{5,3},{6,0},{7,1},{8,14},{9,15},{10,... | collective-permute-start | bytes 196616 | tf_op jit(solution)/shard_map/ppermute | solution.py:31
  83.8 1.3 %collective-permute-start.27 = (bf16[64,512]{1,0:T(8,128)(2,1)S(1)}, bf16[64,512]{1,0:T(8,128)(2,1)S(1)}, u32[]{:S(2)}, u32[]{:S(2)}) collective-permute-start(bf16[64,512]{1,0:T(8,128)(2,1)S(1)} %get-tuple-element.63.refs_7_), channel_id=1, source_target_pairs={{0,2},{1,3},{2,0},{3,1},{4,6},{5,7},{6,4},{7,5},{8,10},{9,11},{10,... | collective-permute-start | bytes 196616 | tf_op jit(solution)/shard_map/ppermute | solution.py:31
  85.2 1.4 %collective-permute-done.29.refs_10_ = bf16[64,512]{1,0:T(8,128)(2,1)S(1)} collective-permute-done((bf16[64,512]{1,0:T(8,128)(2,1)S(1)}, bf16[64,512]{1,0:T(8,128)(2,1)S(1)}, u32[]{:S(2)}, u32[]{:S(2)}) %collective-permute-start.29) | collective-permute-done | bytes 65568 | tf_op jit(solution)/shard_map/ppermute | solution.py:31
  86.5 3.0 %collective-permute-done.28.refs_9_ = bf16[64,512]{1,0:T(8,128)(2,1)S(1)} collective-permute-done((bf16[64,512]{1,0:T(8,128)(2,1)S(1)}, bf16[64,512]{1,0:T(8,128)(2,1)S(1)}, u32[]{:S(2)}, u32[]{:S(2)}) %collective-permute-start.28) | collective-permute-done | bytes 65568 | tf_op jit(solution)/shard_map/ppermute | solution.py:31
  90.5 2.8 %collective-permute-start.31 = (bf16[256,512]{1,0:T(8,128)(2,1)S(1)}, bf16[256,512]{1,0:T(8,128)(2,1)S(1)}, u32[]{:S(2)}, u32[]{:S(2)}) collective-permute-start(bf16[256,512]{1,0:T(8,128)(2,1)S(1)} %get-tuple-element.65), channel_id=1, source_target_pairs={{0,224},{1,225},{2,226},{3,227},{4,228},{5,229},{6,230},{7,231},{8... | collective-permute-start | bytes 786440 | tf_op jit(solution)/shard_map/ppermute | solution.py:31
  93.3 2.0 %collective-permute-start.32 = (bf16[256,512]{1,0:T(8,128)(2,1)S(1)}, bf16[256,512]{1,0:T(8,128)(2,1)S(1)}, u32[]{:S(2)}, u32[]{:S(2)}) collective-permute-start(bf16[256,512]{1,0:T(8,128)(2,1)S(1)} %get-tuple-element.66), channel_id=1, source_target_pairs={{0,16},{1,17},{2,18},{3,19},{4,20},{5,21},{6,22},{7,23},{8,24},{9,... | collective-permute-start | bytes 786440 | tf_op jit(solution)/shard_map/ppermute | solution.py:31
  95.3 1.1 %maximum_convert_fusion = f32[512,512]{1,0:T(8,128)} fusion(bf16[256,512]{1,0:T(8,128)(2,1)S(1)} %get-tuple-element.72, bf16[256,512]{1,0:T(8,128)(2,1)S(1)} %get-tuple-element.71), kind=kLoop, calls=%fused_computation.1 | loop fusion | flops 1048576 | bytes 1572864 | tf_op jit(solution)/shard_map/convert_element_type | solution.py:326
  96.4 3.5 %collective-permute-done.30.refs_1_ = bf16[256,512]{1,0:T(8,128)(2,1)S(1)} collective-permute-done((bf16[256,512]{1,0:T(8,128)(2,1)S(1)}, bf16[256,512]{1,0:T(8,128)(2,1)S(1)}, u32[]{:S(2)}, u32[]{:S(2)}) %collective-permute-start.30) | collective-permute-done | bytes 262176 | tf_op jit(solution)/shard_map/ppermute | solution.py:31
  99.9 3.0 %collective-permute-done.32.refs_3_ = bf16[256,512]{1,0:T(8,128)(2,1)S(1)} collective-permute-done((bf16[256,512]{1,0:T(8,128)(2,1)S(1)}, bf16[256,512]{1,0:T(8,128)(2,1)S(1)}, u32[]{:S(2)}, u32[]{:S(2)}) %collective-permute-start.32) | collective-permute-done | bytes 262176 | tf_op jit(solution)/shard_map/ppermute | solution.py:31
  102.8 0.8 s5.1
  (56 shorter events, 4.9 us)
Async XLA Ops:
  0.6 1.0 %copy-start = (bf16[512,512]{1,0:T(8,128)(2,1)S(1)}, bf16[512,512]{1,0:T(8,128)(2,1)}, u32[]{:S(2)}) copy-start(bf16[512,512]{1,0:T(8,128)(2,1)} %param.12) | copy-start | bytes 1572868
  0.6 6.8 %copy-start.4 = (s32[16]{0:T(128)S(1)}, s32[16]{0:T(128)}, u32[]{:S(2)}) copy-start(s32[16]{0:T(128)} %constant.74.clone.order_ref) | copy-start | bytes 196
  0.7 6.8 %copy-start.3 = (s32[1,1,4]{2,1,0:T(1,128)S(1)}, s32[1,1,4]{2,1,0:T(1,128)}, u32[]{:S(2)}) copy-start(s32[1,1,4]{2,1,0:T(1,128)} %param.16) | copy-start | bytes 52
  0.7 6.8 %copy-start.2 = (s32[1,1,4,24]{3,2,1,0:T(4,128)S(1)}, s32[1,1,4,24]{3,2,1,0:T(4,128)}, u32[]{:S(2)}) copy-start(s32[1,1,4,24]{3,2,1,0:T(4,128)} %param.15) | copy-start | bytes 1156
  0.7 6.8 %copy-start.1 = (s32[1,1,4,24]{3,2,1,0:T(4,128)S(1)}, s32[1,1,4,24]{3,2,1,0:T(4,128)}, u32[]{:S(2)}) copy-start(s32[1,1,4,24]{3,2,1,0:T(4,128)} %param.14) | copy-start | bytes 1156
  3.2 10.0 %collective-permute-start.4 = (bf16[256,512]{1,0:T(8,128)(2,1)S(1)}, bf16[256,512]{1,0:T(8,128)(2,1)}, u32[]{:S(2)}, u32[]{:S(2)}) collective-permute-start(bf16[256,512]{1,0:T(8,128)(2,1)S(1)} %convolution_convert_fusion), channel_id=1, source_target_pairs={{0,8},{1,9},{2,10},{3,11},{16,24},{17,25},{18,26},{19,27},{32,40},... | collective-permute-start | bytes 786440 | tf_op jit(solution)/shard_map/ppermute | solution.py:31
  4.5 5.6 %collective-permute-start.1 = (bf16[256,512]{1,0:T(8,128)(2,1)S(1)}, bf16[256,512]{1,0:T(8,128)(2,1)S(1)}, u32[]{:S(2)}, u32[]{:S(2)}) collective-permute-start(bf16[256,512]{1,0:T(8,128)(2,1)S(1)} %convolution_convert_fusion), channel_id=1, source_target_pairs={{0,6},{1,7},{2,4},{3,5},{16,22},{17,23},{18,20},{19,21},{32,38},{3... | collective-permute-start | bytes 786440 | tf_op jit(solution)/shard_map/ppermute | solution.py:31
  5.1 4.9 %collective-permute-start = (bf16[256,512]{1,0:T(8,128)(2,1)S(1)}, bf16[256,512]{1,0:T(8,128)(2,1)S(1)}, u32[]{:S(2)}, u32[]{:S(2)}) collective-permute-start(bf16[256,512]{1,0:T(8,128)(2,1)S(1)} %convolution_convert_fusion), channel_id=1, source_target_pairs={{0,2},{1,3},{2,0},{3,1},{16,18},{17,19},{18,16},{19,17},{32,34},{3... | collective-permute-start | bytes 786440 | tf_op jit(solution)/shard_map/ppermute | solution.py:31
  9.9 7.4 %collective-permute-start.8 = (bf16[256,512]{1,0:T(8,128)(2,1)S(1)}, bf16[256,512]{1,0:T(8,128)(2,1)}, u32[]{:S(2)}, u32[]{:S(2)}) collective-permute-start(bf16[256,512]{1,0:T(8,128)(2,1)S(1)} %get-tuple-element.36), channel_id=1, source_target_pairs={{0,1},{1,0},{2,3},{3,2},{4,5},{5,4},{6,7},{7,6},{8,9},{9,8},{10,11... | collective-permute-start | bytes 786440 | tf_op jit(solution)/shard_map/ppermute | solution.py:31
  10.1 15.9 %collective-permute-start.3 = (bf16[256,512]{1,0:T(8,128)(2,1)S(1)}, bf16[256,512]{1,0:T(8,128)(2,1)S(1)}, u32[]{:S(2)}, u32[]{:S(2)}) collective-permute-start(bf16[256,512]{1,0:T(8,128)(2,1)S(1)} %broadcast_select_fusion.2), channel_id=1, source_target_pairs={{0,8},{1,9},{2,10},{3,11},{4,12},{5,13},{6,14},{7,15},{16,24},{17,... | collective-permute-start | bytes 786440 | tf_op jit(solution)/shard_map/ppermute | solution.py:31
  11.4 12.8 %collective-permute-start.2 = (bf16[256,512]{1,0:T(8,128)(2,1)S(1)}, bf16[256,512]{1,0:T(8,128)(2,1)S(1)}, u32[]{:S(2)}, u32[]{:S(2)}) collective-permute-start(bf16[256,512]{1,0:T(8,128)(2,1)S(1)} %collective-permute-done.1), channel_id=1, source_target_pairs={{4,6},{5,7},{6,4},{7,5},{20,22},{21,23},{22,20},{23,21},{36,38},{3... | collective-permute-start | bytes 786440 | tf_op jit(solution)/shard_map/ppermute | solution.py:31
  13.2 11.0 %collective-permute-start.5 = (bf16[256,512]{1,0:T(8,128)(2,1)}, bf16[256,512]{1,0:T(8,128)(2,1)S(1)}, u32[]{:S(2)}, u32[]{:S(2)}) collective-permute-start(bf16[256,512]{1,0:T(8,128)(2,1)} %collective-permute-done.4), channel_id=1, source_target_pairs={{8,12},{9,13},{10,14},{11,15},{24,28},{25,29},{26,30},{27,31},{40,... | collective-permute-start | bytes 786440 | tf_op jit(solution)/shard_map/ppermute | solution.py:31
  18.4 9.4 %collective-permute-start.9 = (bf16[128,512]{1,0:T(8,128)(2,1)S(1)}, bf16[128,512]{1,0:T(8,128)(2,1)S(1)}, u32[]{:S(2)}, u32[]{:S(2)}) collective-permute-start(bf16[128,512]{1,0:T(8,128)(2,1)S(1)} %dynamic-slice_convert_fusion.1), channel_id=1, source_target_pairs={{0,2},{1,3},{2,0},{3,1},{4,6},{5,7},{6,4},{7,5},{8,10},{9,11},{10,... | collective-permute-start | bytes 393224 | tf_op jit(solution)/shard_map/ppermute | solution.py:31
  27.2 1.6 %collective-permute-start.6 = (bf16[256,512]{1,0:T(8,128)(2,1)S(1)}, bf16[256,512]{1,0:T(8,128)(2,1)S(1)}, u32[]{:S(2)}, u32[]{:S(2)}) collective-permute-start(bf16[256,512]{1,0:T(8,128)(2,1)S(1)} %broadcast_select_fusion.4.refs_0_), channel_id=1, source_target_pairs={{0,1},{1,0},{2,3},{3,2},{4,5},{5,4},{6,7},{7,6},{8,9},{9,8},{10,11... | collective-permute-start | bytes 786440 | tf_op jit(solution)/shard_map/ppermute | solution.py:31
  27.3 1.9 %collective-permute-start.7 = (bf16[256,512]{1,0:T(8,128)(2,1)S(1)}, bf16[256,512]{1,0:T(8,128)(2,1)S(1)}, u32[]{:S(2)}, u32[]{:S(2)}) collective-permute-start(bf16[256,512]{1,0:T(8,128)(2,1)S(1)} %get-tuple-element.68.refs_1_), channel_id=1, source_target_pairs={{0,1},{1,0},{2,3},{3,2},{4,5},{5,4},{6,7},{7,6},{8,9},{9,8},{10,11... | collective-permute-start | bytes 786440 | tf_op jit(solution)/shard_map/ppermute | solution.py:31
  29.3 13.1 %collective-permute-start.13 = (bf16[128,512]{1,0:T(8,128)(2,1)S(1)}, bf16[128,512]{1,0:T(8,128)(2,1)S(1)}, u32[]{:S(2)}, u32[]{:S(2)}) collective-permute-start(bf16[128,512]{1,0:T(8,128)(2,1)S(1)} %get-tuple-element.49.refs_0_), channel_id=1, source_target_pairs={{0,32},{1,33},{2,34},{3,35},{4,36},{5,37},{6,38},{7,39},{8,40},{9,... | collective-permute-start | bytes 393224 | tf_op jit(solution)/shard_map/ppermute | solution.py:31
  31.3 1.9 %copy-start.5 = (bf16[1,1,4,24,128,128]{5,4,3,2,1,0:T(8,128)(2,1)S(1)}, bf16[1,1,4,24,128,128]{5,4,3,2,1,0:T(8,128)(2,1)}, u32[]{:S(2)}) copy-start(bf16[1,1,4,24,128,128]{5,4,3,2,1,0:T(8,128)(2,1)} %param.13) | copy-start | bytes 9437188
  34.8 13.5 %collective-permute-start.10 = (bf16[256,512]{1,0:T(8,128)(2,1)S(1)}, bf16[256,512]{1,0:T(8,128)(2,1)S(1)}, u32[]{:S(2)}, u32[]{:S(2)}) collective-permute-start(bf16[256,512]{1,0:T(8,128)(2,1)S(1)} %get-tuple-element.43), channel_id=1, source_target_pairs={{0,32},{1,33},{2,34},{3,35},{4,36},{5,37},{6,38},{7,39},{8,40},{9,... | collective-permute-start | bytes 786440 | tf_op jit(solution)/shard_map/ppermute | solution.py:31
  35.6 12.8 %collective-permute-start.12 = (bf16[256,512]{1,0:T(8,128)(2,1)S(1)}, bf16[256,512]{1,0:T(8,128)(2,1)S(1)}, u32[]{:S(2)}, u32[]{:S(2)}) collective-permute-start(bf16[256,512]{1,0:T(8,128)(2,1)S(1)} %get-tuple-element.47), channel_id=1, source_target_pairs={{0,224},{1,225},{2,226},{3,227},{4,228},{5,229},{6,230},{7,231},{8... | collective-permute-start | bytes 786440 | tf_op jit(solution)/shard_map/ppermute | solution.py:31
  40.2 9.3 %collective-permute-start.11 = (bf16[256,512]{1,0:T(8,128)(2,1)S(1)}, bf16[256,512]{1,0:T(8,128)(2,1)S(1)}, u32[]{:S(2)}, u32[]{:S(2)}) collective-permute-start(bf16[256,512]{1,0:T(8,128)(2,1)S(1)} %get-tuple-element.45.refs_2_), channel_id=1, source_target_pairs={{0,16},{1,17},{2,18},{3,19},{4,20},{5,21},{6,22},{7,23},{8,24},{9,... | collective-permute-start | bytes 786440 | tf_op jit(solution)/shard_map/ppermute | solution.py:31
  42.5 5.9 %collective-permute-start.14 = (bf16[64,512]{1,0:T(8,128)(2,1)S(1)}, bf16[64,512]{1,0:T(8,128)(2,1)S(1)}, u32[]{:S(2)}, u32[]{:S(2)}) collective-permute-start(bf16[64,512]{1,0:T(8,128)(2,1)S(1)} %get-tuple-element.73), channel_id=1, source_target_pairs={{0,4},{1,5},{2,6},{3,7},{4,0},{5,1},{6,2},{7,3},{8,12},{9,13},{10,... | collective-permute-start | bytes 196616 | tf_op jit(solution)/shard_map/ppermute | solution.py:31
  49.7 6.1 %collective-permute-start.18 = (bf16[64,512]{1,0:T(8,128)(2,1)S(1)}, bf16[64,512]{1,0:T(8,128)(2,1)S(1)}, u32[]{:S(2)}, u32[]{:S(2)}) collective-permute-start(bf16[64,512]{1,0:T(8,128)(2,1)S(1)} %get-tuple-element.54), channel_id=1, source_target_pairs={{0,64},{1,65},{2,66},{3,67},{4,68},{5,69},{6,70},{7,71},{8,72},{9,... | collective-permute-start | bytes 196616 | tf_op jit(solution)/shard_map/ppermute | solution.py:31
  49.8 16.9 %collective-permute-start.16 = (bf16[384,512]{1,0:T(8,128)(2,1)S(1)}, bf16[384,512]{1,0:T(8,128)(2,1)S(1)}, u32[]{:S(2)}, u32[]{:S(2)}) collective-permute-start(bf16[384,512]{1,0:T(8,128)(2,1)S(1)} %get-tuple-element.51), channel_id=1, source_target_pairs={{0,32},{1,33},{2,34},{3,35},{4,36},{5,37},{6,38},{7,39},{8,40},{9,... | collective-permute-start | bytes 1179656 | tf_op jit(solution)/shard_map/ppermute | solution.py:31
  52.7 14.0 %collective-permute-start.17 = (bf16[384,512]{1,0:T(8,128)(2,1)S(1)}, bf16[384,512]{1,0:T(8,128)(2,1)S(1)}, u32[]{:S(2)}, u32[]{:S(2)}) collective-permute-start(bf16[384,512]{1,0:T(8,128)(2,1)S(1)} %get-tuple-element.53), channel_id=1, source_target_pairs={{0,224},{1,225},{2,226},{3,227},{4,228},{5,229},{6,230},{7,231},{8... | collective-permute-start | bytes 1179656 | tf_op jit(solution)/shard_map/ppermute | solution.py:31
  53.2 13.9 %collective-permute-start.15 = (bf16[512,512]{1,0:T(8,128)(2,1)S(1)}, bf16[512,512]{1,0:T(8,128)(2,1)S(1)}, u32[]{:S(2)}, u32[]{:S(2)}) collective-permute-start(bf16[512,512]{1,0:T(8,128)(2,1)S(1)} %get-tuple-element.50), channel_id=1, source_target_pairs={{0,16},{1,17},{2,18},{3,19},{4,20},{5,21},{6,22},{7,23},{8,24},{9,... | collective-permute-start | bytes 1572872 | tf_op jit(solution)/shard_map/ppermute | solution.py:31
  55.9 10.8 %collective-permute-start.19 = (bf16[64,512]{1,0:T(8,128)(2,1)S(1)}, bf16[64,512]{1,0:T(8,128)(2,1)S(1)}, u32[]{:S(2)}, u32[]{:S(2)}) collective-permute-start(bf16[64,512]{1,0:T(8,128)(2,1)S(1)} %add_convert_fusion.1.refs_5_), channel_id=1, source_target_pairs={{0,128},{1,129},{2,130},{3,131},{4,132},{5,133},{6,134},{7,135},{8... | collective-permute-start | bytes 196616 | tf_op jit(solution)/shard_map/ppermute | solution.py:31
  67.2 10.4 %collective-permute-start.20 = (bf16[256,512]{1,0:T(8,128)(2,1)S(1)}, bf16[256,512]{1,0:T(8,128)(2,1)S(1)}, u32[]{:S(2)}, u32[]{:S(2)}) collective-permute-start(bf16[256,512]{1,0:T(8,128)(2,1)S(1)} %get-tuple-element.55), channel_id=1, source_target_pairs={{0,32},{1,33},{2,34},{3,35},{4,36},{5,37},{6,38},{7,39},{8,40},{9,... | collective-permute-start | bytes 786440 | tf_op jit(solution)/shard_map/ppermute | solution.py:31
  70.2 7.4 %collective-permute-start.21 = (bf16[256,512]{1,0:T(8,128)(2,1)S(1)}, bf16[256,512]{1,0:T(8,128)(2,1)S(1)}, u32[]{:S(2)}, u32[]{:S(2)}) collective-permute-start(bf16[256,512]{1,0:T(8,128)(2,1)S(1)} %get-tuple-element.57), channel_id=1, source_target_pairs={{0,224},{1,225},{2,226},{3,227},{4,228},{5,229},{6,230},{7,231},{8... | collective-permute-start | bytes 786440 | tf_op jit(solution)/shard_map/ppermute | solution.py:31
  70.5 4.3 %collective-permute-start.24 = (bf16[64,512]{1,0:T(8,128)(2,1)S(1)}, bf16[64,512]{1,0:T(8,128)(2,1)S(1)}, u32[]{:S(2)}, u32[]{:S(2)}) collective-permute-start(bf16[64,512]{1,0:T(8,128)(2,1)S(1)} %get-tuple-element.58.refs_4_), channel_id=1, source_target_pairs={{0,24},{1,25},{2,26},{3,27},{4,28},{5,29},{6,30},{7,31},{8,16},{9,... | collective-permute-start | bytes 196616 | tf_op jit(solution)/shard_map/ppermute | solution.py:31
  70.5 5.8 %collective-permute-start.23 = (bf16[64,512]{1,0:T(8,128)(2,1)S(1)}, bf16[64,512]{1,0:T(8,128)(2,1)S(1)}, u32[]{:S(2)}, u32[]{:S(2)}) collective-permute-start(bf16[64,512]{1,0:T(8,128)(2,1)S(1)} %get-tuple-element.58.refs_4_), channel_id=1, source_target_pairs={{0,16},{1,17},{2,18},{3,19},{4,20},{5,21},{6,22},{7,23},{8,24},{9,... | collective-permute-start | bytes 196616 | tf_op jit(solution)/shard_map/ppermute | solution.py:31
  73.3 4.3 %collective-permute-start.22 = (bf16[64,512]{1,0:T(8,128)(2,1)S(1)}, bf16[64,512]{1,0:T(8,128)(2,1)S(1)}, u32[]{:S(2)}, u32[]{:S(2)}) collective-permute-start(bf16[64,512]{1,0:T(8,128)(2,1)S(1)} %get-tuple-element.58.refs_4_), channel_id=1, source_target_pairs={{0,8},{1,9},{2,10},{3,11},{4,12},{5,13},{6,14},{7,15},{8,0},{9,1},... | collective-permute-start | bytes 196616 | tf_op jit(solution)/shard_map/ppermute | solution.py:31
  77.8 11.8 %collective-permute-start.25 = (bf16[256,512]{1,0:T(8,128)(2,1)S(1)}, bf16[256,512]{1,0:T(8,128)(2,1)S(1)}, u32[]{:S(2)}, u32[]{:S(2)}) collective-permute-start(bf16[256,512]{1,0:T(8,128)(2,1)S(1)} %get-tuple-element.59), channel_id=1, source_target_pairs={{0,32},{1,33},{2,34},{3,35},{4,36},{5,37},{6,38},{7,39},{8,40},{9,... | collective-permute-start | bytes 786440 | tf_op jit(solution)/shard_map/ppermute | solution.py:31
  79.5 10.1 %collective-permute-start.26 = (bf16[256,512]{1,0:T(8,128)(2,1)S(1)}, bf16[256,512]{1,0:T(8,128)(2,1)S(1)}, u32[]{:S(2)}, u32[]{:S(2)}) collective-permute-start(bf16[256,512]{1,0:T(8,128)(2,1)S(1)} %get-tuple-element.61), channel_id=1, source_target_pairs={{0,224},{1,225},{2,226},{3,227},{4,228},{5,229},{6,230},{7,231},{8... | collective-permute-start | bytes 786440 | tf_op jit(solution)/shard_map/ppermute | solution.py:31
  81.1 5.5 %collective-permute-start.29 = (bf16[64,512]{1,0:T(8,128)(2,1)S(1)}, bf16[64,512]{1,0:T(8,128)(2,1)S(1)}, u32[]{:S(2)}, u32[]{:S(2)}) collective-permute-start(bf16[64,512]{1,0:T(8,128)(2,1)S(1)} %get-tuple-element.63.refs_7_), channel_id=1, source_target_pairs={{0,6},{1,7},{2,4},{3,5},{4,2},{5,3},{6,0},{7,1},{8,14},{9,15},{10,... | collective-permute-start | bytes 196616 | tf_op jit(solution)/shard_map/ppermute | solution.py:31
  83.8 5.8 %collective-permute-start.28 = (bf16[64,512]{1,0:T(8,128)(2,1)S(1)}, bf16[64,512]{1,0:T(8,128)(2,1)S(1)}, u32[]{:S(2)}, u32[]{:S(2)}) collective-permute-start(bf16[64,512]{1,0:T(8,128)(2,1)S(1)} %get-tuple-element.63.refs_7_), channel_id=1, source_target_pairs={{0,4},{1,5},{2,6},{3,7},{4,0},{5,1},{6,2},{7,3},{8,12},{9,13},{10,... | collective-permute-start | bytes 196616 | tf_op jit(solution)/shard_map/ppermute | solution.py:31
  83.8 5.8 %collective-permute-start.27 = (bf16[64,512]{1,0:T(8,128)(2,1)S(1)}, bf16[64,512]{1,0:T(8,128)(2,1)S(1)}, u32[]{:S(2)}, u32[]{:S(2)}) collective-permute-start(bf16[64,512]{1,0:T(8,128)(2,1)S(1)} %get-tuple-element.63.refs_7_), channel_id=1, source_target_pairs={{0,2},{1,3},{2,0},{3,1},{4,6},{5,7},{6,4},{7,5},{8,10},{9,11},{10,... | collective-permute-start | bytes 196616 | tf_op jit(solution)/shard_map/ppermute | solution.py:31
  89.8 5.4 %collective-permute-start.33 = (bf16[256,512]{1,0:T(8,128)(2,1)S(1)}, bf16[256,512]{1,0:T(8,128)(2,1)S(1)}, u32[]{:S(2)}, u32[]{:S(2)}) collective-permute-start(bf16[256,512]{1,0:T(8,128)(2,1)S(1)} %get-tuple-element.67), channel_id=1, source_target_pairs={{0,1},{1,0},{2,3},{3,2},{4,5},{5,4},{6,7},{7,6},{8,9},{9,8},{10,11... | collective-permute-start | bytes 786440 | tf_op jit(solution)/shard_map/ppermute | solution.py:31
  89.9 9.9 %collective-permute-start.30 = (bf16[256,512]{1,0:T(8,128)(2,1)S(1)}, bf16[256,512]{1,0:T(8,128)(2,1)S(1)}, u32[]{:S(2)}, u32[]{:S(2)}) collective-permute-start(bf16[256,512]{1,0:T(8,128)(2,1)S(1)} %get-tuple-element.64), channel_id=1, source_target_pairs={{0,32},{1,33},{2,34},{3,35},{4,36},{5,37},{6,38},{7,39},{8,40},{9,... | collective-permute-start | bytes 786440 | tf_op jit(solution)/shard_map/ppermute | solution.py:31
  90.5 9.4 %collective-permute-start.31 = (bf16[256,512]{1,0:T(8,128)(2,1)S(1)}, bf16[256,512]{1,0:T(8,128)(2,1)S(1)}, u32[]{:S(2)}, u32[]{:S(2)}) collective-permute-start(bf16[256,512]{1,0:T(8,128)(2,1)S(1)} %get-tuple-element.65), channel_id=1, source_target_pairs={{0,224},{1,225},{2,226},{3,227},{4,228},{5,229},{6,230},{7,231},{8... | collective-permute-start | bytes 786440 | tf_op jit(solution)/shard_map/ppermute | solution.py:31
  93.3 9.6 %collective-permute-start.32 = (bf16[256,512]{1,0:T(8,128)(2,1)S(1)}, bf16[256,512]{1,0:T(8,128)(2,1)S(1)}, u32[]{:S(2)}, u32[]{:S(2)}) collective-permute-start(bf16[256,512]{1,0:T(8,128)(2,1)S(1)} %get-tuple-element.66), channel_id=1, source_target_pairs={{0,16},{1,17},{2,18},{3,19},{4,20},{5,21},{6,22},{7,23},{8,24},{9,... | collective-permute-start | bytes 786440 | tf_op jit(solution)/shard_map/ppermute | solution.py:31

commit v6 on v5

--- a/solution.py
+++ b/solution.py
@@ -298,29 +298,30 @@
     w = narrow(add(w, send(w, flipped("z", 2))))
     w_got = send(w, flipped("z", 4))
     m3, m5, t0, m2, m6, m1, m7, m0 = rows(16, [1] * 8, table, tiles, sources, "rows_third")
-    to_up, to_down, w = stage(
+    to_up, to_down, crossing, w = stage(
         "s2",
         [(128, m3, x35, (up_t, 256)), (128, (m3, 128), (x35, 128))],
         [(128, m5, (x35, 256)), (128, (m5, 128), (x35, 384), (down_t, 256))],
+        [(256, t0, up_t, down_t)],
         [(64, w, w_got)],
     )
 
     up_got, down_got = send(to_up, up), send(to_down, down)
+    crossed = send(crossing, cross)
     w_got = [send(w, flipped("x", step)) for step in (1, 2, 3)]
     to_up, to_down, w = stage("s3", [(256, m2, up_got)], [(256, m6, down_got)], [(64, w, *w_got)])
 
     up_got, down_got = send(to_up, up), send(to_down, down)
     w_got = [send(w, flipped("y", step)) for step in (1, 2, 3)]
-    to_up, to_down, crossing, w = stage(
+    to_up, to_down, w = stage(
         "s4",
         [(256, m1, up_got)],
         [(256, m7, down_got)],
-        [(256, t0, up_t, down_t)],
         anchors=(w, *w_got),
         collect=True,
     )
 
-    up_got, down_got, crossed = send(to_up, up), send(to_down, down), send(crossing, cross)
+    up_got, down_got = send(to_up, up), send(to_down, down)
     w_got = send(w, other)
     (input_grad,) = stage("s5", [(256, m0, up_got, down_got, crossed)])
     return (input_grad, joined(core, w, w_got).astype(jnp.float32))

time: 105 us -> 104 us (level)
  waiting for transfers between devices: 29.4 us -> 27.6 us
  Pallas kernels: 11.9 us -> 13.2 us
    ppermute x34, waiting for transfers between devices: 29.4 us -> 27.6 us  [send(): return lax.ppermute(value, AXES, pairs(move))]
    pallas_call x3, Pallas kernels: 7.76 us -> 9.07 us  [rows(): pl.pallas_call(functools.partial(rows_kernel, base, tuple(sizes)), out_sh...]
  transfers between devices with their start and end apart: 34 -> 34, of which waited for: 16 -> 16; matrix products, arithmetic and copies ran while one was open for 5% -> 5% of each run, Pallas kernels for 10% -> 11%
where the time goes in v6:
time: 104 us; the launch traced here: 103 us
  starting transfers between devices  51.8 us (50%)
  waiting for transfers between devices  27.6 us (27%)
  Pallas kernels  13.2 us (13%)
  other arithmetic  3.36 us (3%)
  matrix products  3 us (3%)
  local copies, waits for them, and re-layouts  2.99 us (3%)
  between operations  1.07 us (1%)
    ppermute x34, starting transfers between devices, send(): return lax.ppermute(value, AXES, pairs(move))  51.8 us
    ppermute x34, waiting for transfers between devices, send(): return lax.ppermute(value, AXES, pairs(move))  27.6 us
    pallas_call x3, Pallas kernels, rows(): pl.pallas_call(functools.partial(rows_kernel, base, tuple(sizes)), out_sh...  9.07 us
    unnamed x12, local copies, waits for them, and re-layouts  2.91 us
    pallas_call x1, Pallas kernels, plan(): pl.pallas_call(plan_kernel, out_shape=[jax.ShapeDtypeStruct((SPARE + 1, 1...  2.4 us
  transfers between devices with their start and end apart: 34, of which 16 were waited for; matrix products, arithmetic and copies ran while one was open for 5% of the time, Pallas kernels for 11%

profile of v6, /device:TPU:2, one launch (start us, length us, event | category | flops | bytes accessed | tf_op | source)
XLA Modules:
  0.0 103.0 jit_solution(3496792779880768742)
XLA Ops:
  0.7 1.0 copy-done
  1.7 1.5 %convolution_convert_fusion = bf16[256,512]{1,0:T(8,128)(2,1)S(1)} fusion(bf16[512,512]{1,0:T(8,128)(2,1)S(1)} %copy-done, bf16[256,512]{1,0:T(8,128)(2,1)} %param.9, s32[256,512]{1,0:T(8,128)} %param.10), kind=kOutput, calls=%fused_computation | convolution fusion | flops 134610944 | bytes 1572864 | tf_op jit(solution)/shard_map/dot_general | solution.py:262
  3.2 1.3 %collective-permute-start.4 = (bf16[256,512]{1,0:T(8,128)(2,1)S(1)}, bf16[256,512]{1,0:T(8,128)(2,1)}, u32[]{:S(2)}, u32[]{:S(2)}) collective-permute-start(bf16[256,512]{1,0:T(8,128)(2,1)S(1)} %convolution_convert_fusion), channel_id=1, source_target_pairs={{0,8},{1,9},{2,10},{3,11},{16,24},{17,25},{18,26},{19,27},{32,40},... | collective-permute-start | bytes 786440 | tf_op jit(solution)/shard_map/ppermute | solution.py:31
  5.8 1.5 %fusion.1 = f32[512,512]{0,1:T(8,128)S(1)} fusion(bf16[256,512]{1,0:T(8,128)(2,1)} %param.11, bf16[256,512]{1,0:T(8,128)(2,1)} %param.9, s32[256,512]{1,0:T(8,128)} %param.10), kind=kOutput, calls=%fused_computation.18 | convolution fusion | flops 134479872 | bytes 2097152 | tf_op jit(solution)/shard_map/dot_general | solution.py:265
  7.5 2.4 %plan.1 = (s32[33,16]{1,0:T(8,128)S(1)}, bf16[256,512]{1,0:T(8,128)(2,1)S(1)}) custom-call(s32[4,24]{1,0:T(4,128)S(1)} %bitcast.11, s32[4,24]{1,0:T(4,128)S(1)} %bitcast.12, s32[4]{0:T(128)S(1)} %bitcast.13, s32[16]{0:T(128)S(1)} %copy-done.4, bf16[256,512]{1,0:T(8,128)(2,1)S(1)} %fusion.given_ref), custom_call_target="tpu_custom_call" | custom-call | tf_op jit(solution)/shard_map/plan/pallas_call | solution.py:107
  10.1 1.3 %collective-permute-start.3 = (bf16[256,512]{1,0:T(8,128)(2,1)S(1)}, bf16[256,512]{1,0:T(8,128)(2,1)S(1)}, u32[]{:S(2)}, u32[]{:S(2)}) collective-permute-start(bf16[256,512]{1,0:T(8,128)(2,1)S(1)} %broadcast_select_fusion.2), channel_id=1, source_target_pairs={{0,8},{1,9},{2,10},{3,11},{4,12},{5,13},{6,14},{7,15},{16,24},{17,... | collective-permute-start | bytes 786440 | tf_op jit(solution)/shard_map/ppermute | solution.py:31
  12.1 1.1 %collective-permute-done.4 = bf16[256,512]{1,0:T(8,128)(2,1)} collective-permute-done((bf16[256,512]{1,0:T(8,128)(2,1)S(1)}, bf16[256,512]{1,0:T(8,128)(2,1)}, u32[]{:S(2)}, u32[]{:S(2)}) %collective-permute-start.4) | collective-permute-done | bytes 262176 | tf_op jit(solution)/shard_map/ppermute | solution.py:31
  13.2 4.1 %collective-permute-start.5 = (bf16[256,512]{1,0:T(8,128)(2,1)}, bf16[256,512]{1,0:T(8,128)(2,1)S(1)}, u32[]{:S(2)}, u32[]{:S(2)}) collective-permute-start(bf16[256,512]{1,0:T(8,128)(2,1)} %collective-permute-done.4), channel_id=1, source_target_pairs={{8,12},{9,13},{10,14},{11,15},{24,28},{25,29},{26,30},{27,31},{40,... | collective-permute-start | bytes 786440 | tf_op jit(solution)/shard_map/ppermute | solution.py:31
  17.3 1.0 bitcast_add_fusion
  18.4 0.8 collective-permute-start.9
  19.1 5.1 %collective-permute-done.5 = bf16[256,512]{1,0:T(8,128)(2,1)S(1)} collective-permute-done((bf16[256,512]{1,0:T(8,128)(2,1)}, bf16[256,512]{1,0:T(8,128)(2,1)S(1)}, u32[]{:S(2)}, u32[]{:S(2)}) %collective-permute-start.5) | collective-permute-done | bytes 262176 | tf_op jit(solution)/shard_map/ppermute | solution.py:31
  24.2 1.9 %collective-permute-done.3 = bf16[256,512]{1,0:T(8,128)(2,1)S(1)} collective-permute-done((bf16[256,512]{1,0:T(8,128)(2,1)S(1)}, bf16[256,512]{1,0:T(8,128)(2,1)S(1)}, u32[]{:S(2)}, u32[]{:S(2)}) %collective-permute-start.3) | collective-permute-done | bytes 262176 | tf_op jit(solution)/shard_map/ppermute | solution.py:31
  26.1 1.1 %broadcast_select_fusion.3 = (bf16[256,512]{1,0:T(8,128)(2,1)S(1)}, bf16[256,512]{1,0:T(8,128)(2,1)S(1)}, bf16[256,512]{1,0:T(8,128)(2,1)S(1)}) fusion(pred[]{:T(512)S(6)} %or.3, bf16[256,512]{1,0:T(8,128)(2,1)} %collective-permute-done.4, bf16[256,512]{1,0:T(8,128)(2,1)S(1)} %collective-permute-done.3, bf16[256,512]{1,0:T(8,128)(2,1)S(1)} %convolution_convert_fusion, ...), kind=kLoop, calls=%fused_computation.13 | loop fusion | flops 917504 | bytes 2621443 | tf_op jit(solution)/shard_map/jit(_where)/select_n | solution.py:277
  27.8 1.0 collective-permute-done.6.refs_2_
  29.3 2.0 %collective-permute-start.13 = (bf16[128,512]{1,0:T(8,128)(2,1)S(1)}, bf16[128,512]{1,0:T(8,128)(2,1)S(1)}, u32[]{:S(2)}, u32[]{:S(2)}) collective-permute-start(bf16[128,512]{1,0:T(8,128)(2,1)S(1)} %get-tuple-element.49.refs_0_), channel_id=1, source_target_pairs={{0,32},{1,33},{2,34},{3,35},{4,36},{5,37},{6,38},{7,39},{8,40},{9,... | collective-permute-start | bytes 393224 | tf_op jit(solution)/shard_map/ppermute | solution.py:31
  31.3 1.9 %copy-done.5 = bf16[1,1,4,24,128,128]{5,4,3,2,1,0:T(8,128)(2,1)S(1)} copy-done((bf16[1,1,4,24,128,128]{5,4,3,2,1,0:T(8,128)(2,1)S(1)}, bf16[1,1,4,24,128,128]{5,4,3,2,1,0:T(8,128)(2,1)}, u32[]{:S(2)}) %copy-start.5) | copy-done | bytes 3145752
  33.2 2.5 %rows_first.1 = (bf16[256,512]{1,0:T(8,128)(2,1)S(1)}, bf16[256,512]{1,0:T(8,128)(2,1)S(1)}, bf16[256,512]{1,0:T(8,128)(2,1)S(1)}) custom-call(s32[33,16]{1,0:T(8,128)S(1)} %get-tuple-element.35.table_ref, bf16[96,128,128]{2,1,0:T(8,128)(2,1)S(1)} %bitcast.14, bf16[8,128,512]{2,1,0:T(8,128)(2,1)S(1)} %bitcast.17), custom_call_target="tpu_custom_call" | custom-call | flops 1200000000 | bytes 1000000 | tf_op jit(solution)/shard_map/rows_first/pallas_call | solution.py:161
  35.7 4.2 %collective-permute-start.12 = (bf16[256,512]{1,0:T(8,128)(2,1)S(1)}, bf16[256,512]{1,0:T(8,128)(2,1)S(1)}, u32[]{:S(2)}, u32[]{:S(2)}) collective-permute-start(bf16[256,512]{1,0:T(8,128)(2,1)S(1)} %get-tuple-element.47), channel_id=1, source_target_pairs={{0,224},{1,225},{2,226},{3,227},{4,228},{5,229},{6,230},{7,231},{8... | collective-permute-start | bytes 786440 | tf_op jit(solution)/shard_map/ppermute | solution.py:31
  40.0 2.7 %collective-permute-start.11 = (bf16[256,512]{1,0:T(8,128)(2,1)S(1)}, bf16[256,512]{1,0:T(8,128)(2,1)S(1)}, u32[]{:S(2)}, u32[]{:S(2)}) collective-permute-start(bf16[256,512]{1,0:T(8,128)(2,1)S(1)} %get-tuple-element.45.refs_2_), channel_id=1, source_target_pairs={{0,16},{1,17},{2,18},{3,19},{4,20},{5,21},{6,22},{7,23},{8,24},{9,... | collective-permute-start | bytes 786440 | tf_op jit(solution)/shard_map/ppermute | solution.py:31
  42.7 1.1 %collective-permute-start.14 = (bf16[64,512]{1,0:T(8,128)(2,1)S(1)}, bf16[64,512]{1,0:T(8,128)(2,1)S(1)}, u32[]{:S(2)}, u32[]{:S(2)}) collective-permute-start(bf16[64,512]{1,0:T(8,128)(2,1)S(1)} %get-tuple-element.73), channel_id=1, source_target_pairs={{0,4},{1,5},{2,6},{3,7},{4,0},{5,1},{6,2},{7,3},{8,12},{9,13},{10,... | collective-permute-start | bytes 196616 | tf_op jit(solution)/shard_map/ppermute | solution.py:31
  43.8 3.1 %rows_second.1 = (bf16[512,512]{1,0:T(8,128)(2,1)S(1)}, bf16[256,512]{1,0:T(8,128)(2,1)S(1)}, bf16[256,512]{1,0:T(8,128)(2,1)S(1)}, bf16[256,512]{1,0:T(8,128)(2,1)S(1)}) custom-call(s32[33,16]{1,0:T(8,128)S(1)} %get-tuple-element.35.table_ref, bf16[96,128,128]{2,1,0:T(8,128)(2,1)S(1)} %bitcast.15, bf16[8,128,512]{2,1,0:T(8,128)(2,1)S(1)} %bitcast.18), custom_call_target="tpu_custom_call" | custom-call | flops 2000000000 | bytes 1000000 | tf_op jit(solution)/shard_map/rows_second/pallas_call | solution.py:161
  46.9 1.6 %collective-permute-done.14.refs_8_ = bf16[64,512]{1,0:T(8,128)(2,1)S(1)} collective-permute-done((bf16[64,512]{1,0:T(8,128)(2,1)S(1)}, bf16[64,512]{1,0:T(8,128)(2,1)S(1)}, u32[]{:S(2)}, u32[]{:S(2)}) %collective-permute-start.14) | collective-permute-done | bytes 65568 | tf_op jit(solution)/shard_map/ppermute | solution.py:31
  48.6 0.7 collective-permute-done.11.refs_3_
  49.8 2.1 %collective-permute-start.16 = (bf16[384,512]{1,0:T(8,128)(2,1)S(1)}, bf16[384,512]{1,0:T(8,128)(2,1)S(1)}, u32[]{:S(2)}, u32[]{:S(2)}) collective-permute-start(bf16[384,512]{1,0:T(8,128)(2,1)S(1)} %get-tuple-element.51), channel_id=1, source_target_pairs={{0,32},{1,33},{2,34},{3,35},{4,36},{5,37},{6,38},{7,39},{8,40},{9,... | collective-permute-start | bytes 1179656 | tf_op jit(solution)/shard_map/ppermute | solution.py:31
  51.9 1.1 %collective-permute-start.17 = (bf16[384,512]{1,0:T(8,128)(2,1)S(1)}, bf16[384,512]{1,0:T(8,128)(2,1)S(1)}, u32[]{:S(2)}, u32[]{:S(2)}) collective-permute-start(bf16[384,512]{1,0:T(8,128)(2,1)S(1)} %get-tuple-element.53), channel_id=1, source_target_pairs={{0,224},{1,225},{2,226},{3,227},{4,228},{5,229},{6,230},{7,231},{8... | collective-permute-start | bytes 1179656 | tf_op jit(solution)/shard_map/ppermute | solution.py:31
  53.0 2.5 %collective-permute-start.15 = (bf16[512,512]{1,0:T(8,128)(2,1)S(1)}, bf16[512,512]{1,0:T(8,128)(2,1)S(1)}, u32[]{:S(2)}, u32[]{:S(2)}) collective-permute-start(bf16[512,512]{1,0:T(8,128)(2,1)S(1)} %get-tuple-element.50), channel_id=1, source_target_pairs={{0,16},{1,17},{2,18},{3,19},{4,20},{5,21},{6,22},{7,23},{8,24},{9,... | collective-permute-start | bytes 1572872 | tf_op jit(solution)/shard_map/ppermute | solution.py:31
  55.6 4.6 %collective-permute-start.19 = (bf16[64,512]{1,0:T(8,128)(2,1)S(1)}, bf16[64,512]{1,0:T(8,128)(2,1)S(1)}, u32[]{:S(2)}, u32[]{:S(2)}) collective-permute-start(bf16[64,512]{1,0:T(8,128)(2,1)S(1)} %add_convert_fusion.1.refs_6_), channel_id=1, source_target_pairs={{0,128},{1,129},{2,130},{3,131},{4,132},{5,133},{6,134},{7,135},{8... | collective-permute-start | bytes 196616 | tf_op jit(solution)/shard_map/ppermute | solution.py:31
  60.2 3.5 %rows_third.1 = (bf16[256,512]{1,0:T(8,128)(2,1)S(1)}, bf16[256,512]{1,0:T(8,128)(2,1)S(1)}, bf16[256,512]{1,0:T(8,128)(2,1)S(1)}, bf16[256,512]{1,0:T(8,128)(2,...) custom-call(s32[33,16]{1,0:T(8,128)S(1)} %get-tuple-element.35.table, ...), custom_call_target="tpu_custom_call" | custom-call | flops 3200000000 | bytes 1000000 | tf_op jit(solution)/shard_map/rows_third/pallas_call | solution.py:161
  63.7 1.2 %collective-permute-done.19.refs_7_ = bf16[64,512]{1,0:T(8,128)(2,1)S(1)} collective-permute-done((bf16[64,512]{1,0:T(8,128)(2,1)S(1)}, bf16[64,512]{1,0:T(8,128)(2,1)S(1)}, u32[]{:S(2)}, u32[]{:S(2)}) %collective-permute-start.19) | collective-permute-done | bytes 65568 | tf_op jit(solution)/shard_map/ppermute | solution.py:31
  65.0 1.4 %collective-permute-done.15.refs_1_ = bf16[512,512]{1,0:T(8,128)(2,1)S(1)} collective-permute-done((bf16[512,512]{1,0:T(8,128)(2,1)S(1)}, bf16[512,512]{1,0:T(8,128)(2,1)S(1)}, u32[]{:S(2)}, u32[]{:S(2)}) %collective-permute-start.15) | collective-permute-done | bytes 524320 | tf_op jit(solution)/shard_map/ppermute | solution.py:31
  66.6 2.3 %collective-permute-start.20 = (bf16[256,512]{1,0:T(8,128)(2,1)S(1)}, bf16[256,512]{1,0:T(8,128)(2,1)S(1)}, u32[]{:S(2)}, u32[]{:S(2)}) collective-permute-start(bf16[256,512]{1,0:T(8,128)(2,1)S(1)} %get-tuple-element.56), channel_id=1, source_target_pairs={{0,32},{1,33},{2,34},{3,35},{4,36},{5,37},{6,38},{7,39},{8,40},{9,... | collective-permute-start | bytes 786440 | tf_op jit(solution)/shard_map/ppermute | solution.py:31
  68.9 1.0 %collective-permute-start.21 = (bf16[256,512]{1,0:T(8,128)(2,1)S(1)}, bf16[256,512]{1,0:T(8,128)(2,1)S(1)}, u32[]{:S(2)}, u32[]{:S(2)}) collective-permute-start(bf16[256,512]{1,0:T(8,128)(2,1)S(1)} %get-tuple-element.58), channel_id=1, source_target_pairs={{0,224},{1,225},{2,226},{3,227},{4,228},{5,229},{6,230},{7,231},{8... | collective-permute-start | bytes 786440 | tf_op jit(solution)/shard_map/ppermute | solution.py:31
  70.4 2.5 %collective-permute-start.23 = (bf16[64,512]{1,0:T(8,128)(2,1)S(1)}, bf16[64,512]{1,0:T(8,128)(2,1)S(1)}, u32[]{:S(2)}, u32[]{:S(2)}) collective-permute-start(bf16[64,512]{1,0:T(8,128)(2,1)S(1)} %get-tuple-element.59.refs_4_), channel_id=1, source_target_pairs={{0,16},{1,17},{2,18},{3,19},{4,20},{5,21},{6,22},{7,23},{8,24},{9,... | collective-permute-start | bytes 196616 | tf_op jit(solution)/shard_map/ppermute | solution.py:31
  72.9 1.1 %collective-permute-start.22 = (bf16[64,512]{1,0:T(8,128)(2,1)S(1)}, bf16[64,512]{1,0:T(8,128)(2,1)S(1)}, u32[]{:S(2)}, u32[]{:S(2)}) collective-permute-start(bf16[64,512]{1,0:T(8,128)(2,1)S(1)} %get-tuple-element.59.refs_4_), channel_id=1, source_target_pairs={{0,8},{1,9},{2,10},{3,11},{4,12},{5,13},{6,14},{7,15},{8,0},{9,1},... | collective-permute-start | bytes 196616 | tf_op jit(solution)/shard_map/ppermute | solution.py:31
  74.2 2.0 %collective-permute-done.23.refs_6_ = bf16[64,512]{1,0:T(8,128)(2,1)S(1)} collective-permute-done((bf16[64,512]{1,0:T(8,128)(2,1)S(1)}, bf16[64,512]{1,0:T(8,128)(2,1)S(1)}, u32[]{:S(2)}, u32[]{:S(2)}) %collective-permute-start.23) | collective-permute-done | bytes 65568 | tf_op jit(solution)/shard_map/ppermute | solution.py:31
  76.2 1.0 collective-permute-done.22.refs_5_
  77.4 0.9 collective-permute-start.25
  78.3 2.4 %collective-permute-start.26 = (bf16[256,512]{1,0:T(8,128)(2,1)S(1)}, bf16[256,512]{1,0:T(8,128)(2,1)S(1)}, u32[]{:S(2)}, u32[]{:S(2)}) collective-permute-start(bf16[256,512]{1,0:T(8,128)(2,1)S(1)} %get-tuple-element.62), channel_id=1, source_target_pairs={{0,224},{1,225},{2,226},{3,227},{4,228},{5,229},{6,230},{7,231},{8... | collective-permute-start | bytes 786440 | tf_op jit(solution)/shard_map/ppermute | solution.py:31
  80.7 3.8 %collective-permute-start.29 = (bf16[64,512]{1,0:T(8,128)(2,1)S(1)}, bf16[64,512]{1,0:T(8,128)(2,1)S(1)}, u32[]{:S(2)}, u32[]{:S(2)}) collective-permute-start(bf16[64,512]{1,0:T(8,128)(2,1)S(1)} %get-tuple-element.63.refs_4_), channel_id=1, source_target_pairs={{0,6},{1,7},{2,4},{3,5},{4,2},{5,3},{6,0},{7,1},{8,14},{9,15},{10,... | collective-permute-start | bytes 196616 | tf_op jit(solution)/shard_map/ppermute | solution.py:31
  84.4 0.9 collective-permute-start.27
  85.3 1.7 %collective-permute-done.29.refs_7_ = bf16[64,512]{1,0:T(8,128)(2,1)S(1)} collective-permute-done((bf16[64,512]{1,0:T(8,128)(2,1)S(1)}, bf16[64,512]{1,0:T(8,128)(2,1)S(1)}, u32[]{:S(2)}, u32[]{:S(2)}) %collective-permute-start.29) | collective-permute-done | bytes 65568 | tf_op jit(solution)/shard_map/ppermute | solution.py:31
  87.0 3.3 %collective-permute-done.28.refs_6_ = bf16[64,512]{1,0:T(8,128)(2,1)S(1)} collective-permute-done((bf16[64,512]{1,0:T(8,128)(2,1)S(1)}, bf16[64,512]{1,0:T(8,128)(2,1)S(1)}, u32[]{:S(2)}, u32[]{:S(2)}) %collective-permute-start.28) | collective-permute-done | bytes 65568 | tf_op jit(solution)/shard_map/ppermute | solution.py:31
  90.5 2.1 %collective-permute-start.32 = (bf16[256,512]{1,0:T(8,128)(2,1)S(1)}, bf16[256,512]{1,0:T(8,128)(2,1)S(1)}, u32[]{:S(2)}, u32[]{:S(2)}) collective-permute-start(bf16[256,512]{1,0:T(8,128)(2,1)S(1)} %get-tuple-element.66), channel_id=1, source_target_pairs={{0,16},{1,17},{2,18},{3,19},{4,20},{5,21},{6,22},{7,23},{8,24},{9,... | collective-permute-start | bytes 786440 | tf_op jit(solution)/shard_map/ppermute | solution.py:31
  92.6 3.2 %collective-permute-start.31 = (bf16[256,512]{1,0:T(8,128)(2,1)S(1)}, bf16[256,512]{1,0:T(8,128)(2,1)S(1)}, u32[]{:S(2)}, u32[]{:S(2)}) collective-permute-start(bf16[256,512]{1,0:T(8,128)(2,1)S(1)} %get-tuple-element.65), channel_id=1, source_target_pairs={{0,224},{1,225},{2,226},{3,227},{4,228},{5,229},{6,230},{7,231},{8... | collective-permute-start | bytes 786440 | tf_op jit(solution)/shard_map/ppermute | solution.py:31
  95.9 1.1 %maximum_convert_fusion = f32[512,512]{1,0:T(8,128)} fusion(bf16[256,512]{1,0:T(8,128)(2,1)S(1)} %get-tuple-element.72, bf16[256,512]{1,0:T(8,128)(2,1)S(1)} %get-tuple-element.71), kind=kLoop, calls=%fused_computation.1 | loop fusion | flops 1048576 | bytes 1572864 | tf_op jit(solution)/shard_map/convert_element_type | solution.py:327
  97.0 3.7 %collective-permute-done.32.refs_3_ = bf16[256,512]{1,0:T(8,128)(2,1)S(1)} collective-permute-done((bf16[256,512]{1,0:T(8,128)(2,1)S(1)}, bf16[256,512]{1,0:T(8,128)(2,1)S(1)}, u32[]{:S(2)}, u32[]{:S(2)}) %collective-permute-start.32) | collective-permute-done | bytes 262176 | tf_op jit(solution)/shard_map/ppermute | solution.py:31
  100.7 1.4 %collective-permute-done.30.refs_1_ = bf16[256,512]{1,0:T(8,128)(2,1)S(1)} collective-permute-done((bf16[256,512]{1,0:T(8,128)(2,1)S(1)}, bf16[256,512]{1,0:T(8,128)(2,1)S(1)}, u32[]{:S(2)}, u32[]{:S(2)}) %collective-permute-start.30) | collective-permute-done | bytes 262176 | tf_op jit(solution)/shard_map/ppermute | solution.py:31
  102.1 0.8 s5.1
  (56 shorter events, 5.4 us)
Async XLA Ops:
  0.6 1.0 %copy-start = (bf16[512,512]{1,0:T(8,128)(2,1)S(1)}, bf16[512,512]{1,0:T(8,128)(2,1)}, u32[]{:S(2)}) copy-start(bf16[512,512]{1,0:T(8,128)(2,1)} %param.12) | copy-start | bytes 1572868
  0.6 6.8 %copy-start.4 = (s32[16]{0:T(128)S(1)}, s32[16]{0:T(128)}, u32[]{:S(2)}) copy-start(s32[16]{0:T(128)} %constant.74.clone.order_ref) | copy-start | bytes 196
  0.7 6.8 %copy-start.3 = (s32[1,1,4]{2,1,0:T(1,128)S(1)}, s32[1,1,4]{2,1,0:T(1,128)}, u32[]{:S(2)}) copy-start(s32[1,1,4]{2,1,0:T(1,128)} %param.16) | copy-start | bytes 52
  0.7 6.8 %copy-start.2 = (s32[1,1,4,24]{3,2,1,0:T(4,128)S(1)}, s32[1,1,4,24]{3,2,1,0:T(4,128)}, u32[]{:S(2)}) copy-start(s32[1,1,4,24]{3,2,1,0:T(4,128)} %param.15) | copy-start | bytes 1156
  0.7 6.8 %copy-start.1 = (s32[1,1,4,24]{3,2,1,0:T(4,128)S(1)}, s32[1,1,4,24]{3,2,1,0:T(4,128)}, u32[]{:S(2)}) copy-start(s32[1,1,4,24]{3,2,1,0:T(4,128)} %param.14) | copy-start | bytes 1156
  3.2 10.0 %collective-permute-start.4 = (bf16[256,512]{1,0:T(8,128)(2,1)S(1)}, bf16[256,512]{1,0:T(8,128)(2,1)}, u32[]{:S(2)}, u32[]{:S(2)}) collective-permute-start(bf16[256,512]{1,0:T(8,128)(2,1)S(1)} %convolution_convert_fusion), channel_id=1, source_target_pairs={{0,8},{1,9},{2,10},{3,11},{16,24},{17,25},{18,26},{19,27},{32,40},... | collective-permute-start | bytes 786440 | tf_op jit(solution)/shard_map/ppermute | solution.py:31
  4.5 5.6 %collective-permute-start.1 = (bf16[256,512]{1,0:T(8,128)(2,1)S(1)}, bf16[256,512]{1,0:T(8,128)(2,1)S(1)}, u32[]{:S(2)}, u32[]{:S(2)}) collective-permute-start(bf16[256,512]{1,0:T(8,128)(2,1)S(1)} %convolution_convert_fusion), channel_id=1, source_target_pairs={{0,6},{1,7},{2,4},{3,5},{16,22},{17,23},{18,20},{19,21},{32,38},{3... | collective-permute-start | bytes 786440 | tf_op jit(solution)/shard_map/ppermute | solution.py:31
  5.1 4.9 %collective-permute-start = (bf16[256,512]{1,0:T(8,128)(2,1)S(1)}, bf16[256,512]{1,0:T(8,128)(2,1)S(1)}, u32[]{:S(2)}, u32[]{:S(2)}) collective-permute-start(bf16[256,512]{1,0:T(8,128)(2,1)S(1)} %convolution_convert_fusion), channel_id=1, source_target_pairs={{0,2},{1,3},{2,0},{3,1},{16,18},{17,19},{18,16},{19,17},{32,34},{3... | collective-permute-start | bytes 786440 | tf_op jit(solution)/shard_map/ppermute | solution.py:31
  9.9 7.4 %collective-permute-start.8 = (bf16[256,512]{1,0:T(8,128)(2,1)S(1)}, bf16[256,512]{1,0:T(8,128)(2,1)}, u32[]{:S(2)}, u32[]{:S(2)}) collective-permute-start(bf16[256,512]{1,0:T(8,128)(2,1)S(1)} %get-tuple-element.36), channel_id=1, source_target_pairs={{0,1},{1,0},{2,3},{3,2},{4,5},{5,4},{6,7},{7,6},{8,9},{9,8},{10,11... | collective-permute-start | bytes 786440 | tf_op jit(solution)/shard_map/ppermute | solution.py:31
  10.1 15.9 %collective-permute-start.3 = (bf16[256,512]{1,0:T(8,128)(2,1)S(1)}, bf16[256,512]{1,0:T(8,128)(2,1)S(1)}, u32[]{:S(2)}, u32[]{:S(2)}) collective-permute-start(bf16[256,512]{1,0:T(8,128)(2,1)S(1)} %broadcast_select_fusion.2), channel_id=1, source_target_pairs={{0,8},{1,9},{2,10},{3,11},{4,12},{5,13},{6,14},{7,15},{16,24},{17,... | collective-permute-start | bytes 786440 | tf_op jit(solution)/shard_map/ppermute | solution.py:31
  11.4 12.8 %collective-permute-start.2 = (bf16[256,512]{1,0:T(8,128)(2,1)S(1)}, bf16[256,512]{1,0:T(8,128)(2,1)S(1)}, u32[]{:S(2)}, u32[]{:S(2)}) collective-permute-start(bf16[256,512]{1,0:T(8,128)(2,1)S(1)} %collective-permute-done.1), channel_id=1, source_target_pairs={{4,6},{5,7},{6,4},{7,5},{20,22},{21,23},{22,20},{23,21},{36,38},{3... | collective-permute-start | bytes 786440 | tf_op jit(solution)/shard_map/ppermute | solution.py:31
  13.2 11.0 %collective-permute-start.5 = (bf16[256,512]{1,0:T(8,128)(2,1)}, bf16[256,512]{1,0:T(8,128)(2,1)S(1)}, u32[]{:S(2)}, u32[]{:S(2)}) collective-permute-start(bf16[256,512]{1,0:T(8,128)(2,1)} %collective-permute-done.4), channel_id=1, source_target_pairs={{8,12},{9,13},{10,14},{11,15},{24,28},{25,29},{26,30},{27,31},{40,... | collective-permute-start | bytes 786440 | tf_op jit(solution)/shard_map/ppermute | solution.py:31
  18.4 9.4 %collective-permute-start.9 = (bf16[128,512]{1,0:T(8,128)(2,1)S(1)}, bf16[128,512]{1,0:T(8,128)(2,1)S(1)}, u32[]{:S(2)}, u32[]{:S(2)}) collective-permute-start(bf16[128,512]{1,0:T(8,128)(2,1)S(1)} %dynamic-slice_convert_fusion.1), channel_id=1, source_target_pairs={{0,2},{1,3},{2,0},{3,1},{4,6},{5,7},{6,4},{7,5},{8,10},{9,11},{10,... | collective-permute-start | bytes 393224 | tf_op jit(solution)/shard_map/ppermute | solution.py:31
  27.2 1.6 %collective-permute-start.6 = (bf16[256,512]{1,0:T(8,128)(2,1)S(1)}, bf16[256,512]{1,0:T(8,128)(2,1)S(1)}, u32[]{:S(2)}, u32[]{:S(2)}) collective-permute-start(bf16[256,512]{1,0:T(8,128)(2,1)S(1)} %broadcast_select_fusion.4.refs_0_), channel_id=1, source_target_pairs={{0,1},{1,0},{2,3},{3,2},{4,5},{5,4},{6,7},{7,6},{8,9},{9,8},{10,11... | collective-permute-start | bytes 786440 | tf_op jit(solution)/shard_map/ppermute | solution.py:31
  27.3 1.9 %collective-permute-start.7 = (bf16[256,512]{1,0:T(8,128)(2,1)S(1)}, bf16[256,512]{1,0:T(8,128)(2,1)S(1)}, u32[]{:S(2)}, u32[]{:S(2)}) collective-permute-start(bf16[256,512]{1,0:T(8,128)(2,1)S(1)} %get-tuple-element.68.refs_1_), channel_id=1, source_target_pairs={{0,1},{1,0},{2,3},{3,2},{4,5},{5,4},{6,7},{7,6},{8,9},{9,8},{10,11... | collective-permute-start | bytes 786440 | tf_op jit(solution)/shard_map/ppermute | solution.py:31
  29.3 13.4 %collective-permute-start.13 = (bf16[128,512]{1,0:T(8,128)(2,1)S(1)}, bf16[128,512]{1,0:T(8,128)(2,1)S(1)}, u32[]{:S(2)}, u32[]{:S(2)}) collective-permute-start(bf16[128,512]{1,0:T(8,128)(2,1)S(1)} %get-tuple-element.49.refs_0_), channel_id=1, source_target_pairs={{0,32},{1,33},{2,34},{3,35},{4,36},{5,37},{6,38},{7,39},{8,40},{9,... | collective-permute-start | bytes 393224 | tf_op jit(solution)/shard_map/ppermute | solution.py:31
  31.3 1.9 %copy-start.5 = (bf16[1,1,4,24,128,128]{5,4,3,2,1,0:T(8,128)(2,1)S(1)}, bf16[1,1,4,24,128,128]{5,4,3,2,1,0:T(8,128)(2,1)}, u32[]{:S(2)}) copy-start(bf16[1,1,4,24,128,128]{5,4,3,2,1,0:T(8,128)(2,1)} %param.13) | copy-start | bytes 9437188
  35.6 12.9 %collective-permute-start.10 = (bf16[256,512]{1,0:T(8,128)(2,1)S(1)}, bf16[256,512]{1,0:T(8,128)(2,1)S(1)}, u32[]{:S(2)}, u32[]{:S(2)}) collective-permute-start(bf16[256,512]{1,0:T(8,128)(2,1)S(1)} %get-tuple-element.43), channel_id=1, source_target_pairs={{0,32},{1,33},{2,34},{3,35},{4,36},{5,37},{6,38},{7,39},{8,40},{9,... | collective-permute-start | bytes 786440 | tf_op jit(solution)/shard_map/ppermute | solution.py:31
  35.7 12.8 %collective-permute-start.12 = (bf16[256,512]{1,0:T(8,128)(2,1)S(1)}, bf16[256,512]{1,0:T(8,128)(2,1)S(1)}, u32[]{:S(2)}, u32[]{:S(2)}) collective-permute-start(bf16[256,512]{1,0:T(8,128)(2,1)S(1)} %get-tuple-element.47), channel_id=1, source_target_pairs={{0,224},{1,225},{2,226},{3,227},{4,228},{5,229},{6,230},{7,231},{8... | collective-permute-start | bytes 786440 | tf_op jit(solution)/shard_map/ppermute | solution.py:31
  40.0 9.3 %collective-permute-start.11 = (bf16[256,512]{1,0:T(8,128)(2,1)S(1)}, bf16[256,512]{1,0:T(8,128)(2,1)S(1)}, u32[]{:S(2)}, u32[]{:S(2)}) collective-permute-start(bf16[256,512]{1,0:T(8,128)(2,1)S(1)} %get-tuple-element.45.refs_2_), channel_id=1, source_target_pairs={{0,16},{1,17},{2,18},{3,19},{4,20},{5,21},{6,22},{7,23},{8,24},{9,... | collective-permute-start | bytes 786440 | tf_op jit(solution)/shard_map/ppermute | solution.py:31
  42.7 5.9 %collective-permute-start.14 = (bf16[64,512]{1,0:T(8,128)(2,1)S(1)}, bf16[64,512]{1,0:T(8,128)(2,1)S(1)}, u32[]{:S(2)}, u32[]{:S(2)}) collective-permute-start(bf16[64,512]{1,0:T(8,128)(2,1)S(1)} %get-tuple-element.73), channel_id=1, source_target_pairs={{0,4},{1,5},{2,6},{3,7},{4,0},{5,1},{6,2},{7,3},{8,12},{9,13},{10,... | collective-permute-start | bytes 196616 | tf_op jit(solution)/shard_map/ppermute | solution.py:31
  49.5 6.1 %collective-permute-start.18 = (bf16[64,512]{1,0:T(8,128)(2,1)S(1)}, bf16[64,512]{1,0:T(8,128)(2,1)S(1)}, u32[]{:S(2)}, u32[]{:S(2)}) collective-permute-start(bf16[64,512]{1,0:T(8,128)(2,1)S(1)} %get-tuple-element.55), channel_id=1, source_target_pairs={{0,64},{1,65},{2,66},{3,67},{4,68},{5,69},{6,70},{7,71},{8,72},{9,... | collective-permute-start | bytes 196616 | tf_op jit(solution)/shard_map/ppermute | solution.py:31
  49.8 15.2 %collective-permute-start.16 = (bf16[384,512]{1,0:T(8,128)(2,1)S(1)}, bf16[384,512]{1,0:T(8,128)(2,1)S(1)}, u32[]{:S(2)}, u32[]{:S(2)}) collective-permute-start(bf16[384,512]{1,0:T(8,128)(2,1)S(1)} %get-tuple-element.51), channel_id=1, source_target_pairs={{0,32},{1,33},{2,34},{3,35},{4,36},{5,37},{6,38},{7,39},{8,40},{9,... | collective-permute-start | bytes 1179656 | tf_op jit(solution)/shard_map/ppermute | solution.py:31
  51.9 13.0 %collective-permute-start.17 = (bf16[384,512]{1,0:T(8,128)(2,1)S(1)}, bf16[384,512]{1,0:T(8,128)(2,1)S(1)}, u32[]{:S(2)}, u32[]{:S(2)}) collective-permute-start(bf16[384,512]{1,0:T(8,128)(2,1)S(1)} %get-tuple-element.53), channel_id=1, source_target_pairs={{0,224},{1,225},{2,226},{3,227},{4,228},{5,229},{6,230},{7,231},{8... | collective-permute-start | bytes 1179656 | tf_op jit(solution)/shard_map/ppermute | solution.py:31
  53.0 13.3 %collective-permute-start.15 = (bf16[512,512]{1,0:T(8,128)(2,1)S(1)}, bf16[512,512]{1,0:T(8,128)(2,1)S(1)}, u32[]{:S(2)}, u32[]{:S(2)}) collective-permute-start(bf16[512,512]{1,0:T(8,128)(2,1)S(1)} %get-tuple-element.50), channel_id=1, source_target_pairs={{0,16},{1,17},{2,18},{3,19},{4,20},{5,21},{6,22},{7,23},{8,24},{9,... | collective-permute-start | bytes 1572872 | tf_op jit(solution)/shard_map/ppermute | solution.py:31
  55.6 9.4 %collective-permute-start.19 = (bf16[64,512]{1,0:T(8,128)(2,1)S(1)}, bf16[64,512]{1,0:T(8,128)(2,1)S(1)}, u32[]{:S(2)}, u32[]{:S(2)}) collective-permute-start(bf16[64,512]{1,0:T(8,128)(2,1)S(1)} %add_convert_fusion.1.refs_6_), channel_id=1, source_target_pairs={{0,128},{1,129},{2,130},{3,131},{4,132},{5,133},{6,134},{7,135},{8... | collective-permute-start | bytes 196616 | tf_op jit(solution)/shard_map/ppermute | solution.py:31
  66.6 10.6 %collective-permute-start.20 = (bf16[256,512]{1,0:T(8,128)(2,1)S(1)}, bf16[256,512]{1,0:T(8,128)(2,1)S(1)}, u32[]{:S(2)}, u32[]{:S(2)}) collective-permute-start(bf16[256,512]{1,0:T(8,128)(2,1)S(1)} %get-tuple-element.56), channel_id=1, source_target_pairs={{0,32},{1,33},{2,34},{3,35},{4,36},{5,37},{6,38},{7,39},{8,40},{9,... | collective-permute-start | bytes 786440 | tf_op jit(solution)/shard_map/ppermute | solution.py:31
  68.9 8.3 %collective-permute-start.21 = (bf16[256,512]{1,0:T(8,128)(2,1)S(1)}, bf16[256,512]{1,0:T(8,128)(2,1)S(1)}, u32[]{:S(2)}, u32[]{:S(2)}) collective-permute-start(bf16[256,512]{1,0:T(8,128)(2,1)S(1)} %get-tuple-element.58), channel_id=1, source_target_pairs={{0,224},{1,225},{2,226},{3,227},{4,228},{5,229},{6,230},{7,231},{8... | collective-permute-start | bytes 786440 | tf_op jit(solution)/shard_map/ppermute | solution.py:31
  69.9 4.3 %collective-permute-start.24 = (bf16[64,512]{1,0:T(8,128)(2,1)S(1)}, bf16[64,512]{1,0:T(8,128)(2,1)S(1)}, u32[]{:S(2)}, u32[]{:S(2)}) collective-permute-start(bf16[64,512]{1,0:T(8,128)(2,1)S(1)} %get-tuple-element.59.refs_4_), channel_id=1, source_target_pairs={{0,24},{1,25},{2,26},{3,27},{4,28},{5,29},{6,30},{7,31},{8,16},{9,... | collective-permute-start | bytes 196616 | tf_op jit(solution)/shard_map/ppermute | solution.py:31
  70.4 5.8 %collective-permute-start.23 = (bf16[64,512]{1,0:T(8,128)(2,1)S(1)}, bf16[64,512]{1,0:T(8,128)(2,1)S(1)}, u32[]{:S(2)}, u32[]{:S(2)}) collective-permute-start(bf16[64,512]{1,0:T(8,128)(2,1)S(1)} %get-tuple-element.59.refs_4_), channel_id=1, source_target_pairs={{0,16},{1,17},{2,18},{3,19},{4,20},{5,21},{6,22},{7,23},{8,24},{9,... | collective-permute-start | bytes 196616 | tf_op jit(solution)/shard_map/ppermute | solution.py:31
  72.9 4.3 %collective-permute-start.22 = (bf16[64,512]{1,0:T(8,128)(2,1)S(1)}, bf16[64,512]{1,0:T(8,128)(2,1)S(1)}, u32[]{:S(2)}, u32[]{:S(2)}) collective-permute-start(bf16[64,512]{1,0:T(8,128)(2,1)S(1)} %get-tuple-element.59.refs_4_), channel_id=1, source_target_pairs={{0,8},{1,9},{2,10},{3,11},{4,12},{5,13},{6,14},{7,15},{8,0},{9,1},... | collective-permute-start | bytes 196616 | tf_op jit(solution)/shard_map/ppermute | solution.py:31
  77.4 12.9 %collective-permute-start.25 = (bf16[256,512]{1,0:T(8,128)(2,1)S(1)}, bf16[256,512]{1,0:T(8,128)(2,1)S(1)}, u32[]{:S(2)}, u32[]{:S(2)}) collective-permute-start(bf16[256,512]{1,0:T(8,128)(2,1)S(1)} %get-tuple-element.60), channel_id=1, source_target_pairs={{0,32},{1,33},{2,34},{3,35},{4,36},{5,37},{6,38},{7,39},{8,40},{9,... | collective-permute-start | bytes 786440 | tf_op jit(solution)/shard_map/ppermute | solution.py:31
  78.3 12.0 %collective-permute-start.26 = (bf16[256,512]{1,0:T(8,128)(2,1)S(1)}, bf16[256,512]{1,0:T(8,128)(2,1)S(1)}, u32[]{:S(2)}, u32[]{:S(2)}) collective-permute-start(bf16[256,512]{1,0:T(8,128)(2,1)S(1)} %get-tuple-element.62), channel_id=1, source_target_pairs={{0,224},{1,225},{2,226},{3,227},{4,228},{5,229},{6,230},{7,231},{8... | collective-permute-start | bytes 786440 | tf_op jit(solution)/shard_map/ppermute | solution.py:31
  80.7 6.3 %collective-permute-start.29 = (bf16[64,512]{1,0:T(8,128)(2,1)S(1)}, bf16[64,512]{1,0:T(8,128)(2,1)S(1)}, u32[]{:S(2)}, u32[]{:S(2)}) collective-permute-start(bf16[64,512]{1,0:T(8,128)(2,1)S(1)} %get-tuple-element.63.refs_4_), channel_id=1, source_target_pairs={{0,6},{1,7},{2,4},{3,5},{4,2},{5,3},{6,0},{7,1},{8,14},{9,15},{10,... | collective-permute-start | bytes 196616 | tf_op jit(solution)/shard_map/ppermute | solution.py:31
  84.4 5.8 %collective-permute-start.28 = (bf16[64,512]{1,0:T(8,128)(2,1)S(1)}, bf16[64,512]{1,0:T(8,128)(2,1)S(1)}, u32[]{:S(2)}, u32[]{:S(2)}) collective-permute-start(bf16[64,512]{1,0:T(8,128)(2,1)S(1)} %get-tuple-element.63.refs_4_), channel_id=1, source_target_pairs={{0,4},{1,5},{2,6},{3,7},{4,0},{5,1},{6,2},{7,3},{8,12},{9,13},{10,... | collective-permute-start | bytes 196616 | tf_op jit(solution)/shard_map/ppermute | solution.py:31
  84.4 5.8 %collective-permute-start.27 = (bf16[64,512]{1,0:T(8,128)(2,1)S(1)}, bf16[64,512]{1,0:T(8,128)(2,1)S(1)}, u32[]{:S(2)}, u32[]{:S(2)}) collective-permute-start(bf16[64,512]{1,0:T(8,128)(2,1)S(1)} %get-tuple-element.63.refs_4_), channel_id=1, source_target_pairs={{0,2},{1,3},{2,0},{3,1},{4,6},{5,7},{6,4},{7,5},{8,10},{9,11},{10,... | collective-permute-start | bytes 196616 | tf_op jit(solution)/shard_map/ppermute | solution.py:31
  90.4 5.4 %collective-permute-start.33 = (bf16[256,512]{1,0:T(8,128)(2,1)S(1)}, bf16[256,512]{1,0:T(8,128)(2,1)S(1)}, u32[]{:S(2)}, u32[]{:S(2)}) collective-permute-start(bf16[256,512]{1,0:T(8,128)(2,1)S(1)} %get-tuple-element.67), channel_id=1, source_target_pairs={{0,1},{1,0},{2,3},{3,2},{4,5},{5,4},{6,7},{7,6},{8,9},{9,8},{10,11... | collective-permute-start | bytes 786440 | tf_op jit(solution)/shard_map/ppermute | solution.py:31
  90.5 10.2 %collective-permute-start.32 = (bf16[256,512]{1,0:T(8,128)(2,1)S(1)}, bf16[256,512]{1,0:T(8,128)(2,1)S(1)}, u32[]{:S(2)}, u32[]{:S(2)}) collective-permute-start(bf16[256,512]{1,0:T(8,128)(2,1)S(1)} %get-tuple-element.66), channel_id=1, source_target_pairs={{0,16},{1,17},{2,18},{3,19},{4,20},{5,21},{6,22},{7,23},{8,24},{9,... | collective-permute-start | bytes 786440 | tf_op jit(solution)/shard_map/ppermute | solution.py:31
  92.6 9.6 %collective-permute-start.30 = (bf16[256,512]{1,0:T(8,128)(2,1)S(1)}, bf16[256,512]{1,0:T(8,128)(2,1)S(1)}, u32[]{:S(2)}, u32[]{:S(2)}) collective-permute-start(bf16[256,512]{1,0:T(8,128)(2,1)S(1)} %get-tuple-element.64), channel_id=1, source_target_pairs={{0,32},{1,33},{2,34},{3,35},{4,36},{5,37},{6,38},{7,39},{8,40},{9,... | collective-permute-start | bytes 786440 | tf_op jit(solution)/shard_map/ppermute | solution.py:31
  92.6 9.6 %collective-permute-start.31 = (bf16[256,512]{1,0:T(8,128)(2,1)S(1)}, bf16[256,512]{1,0:T(8,128)(2,1)S(1)}, u32[]{:S(2)}, u32[]{:S(2)}) collective-permute-start(bf16[256,512]{1,0:T(8,128)(2,1)S(1)} %get-tuple-element.65), channel_id=1, source_target_pairs={{0,224},{1,225},{2,226},{3,227},{4,228},{5,229},{6,230},{7,231},{8... | collective-permute-start | bytes 786440 | tf_op jit(solution)/shard_map/ppermute | solution.py:31
